TPU v7x, 128 devices: a whole 4x4x4 slice. The times are simulated.
128 devices in a mesh: slab: 8 (over z, core), tile: 16 (over y, x).
Axes of the slice: x: 4, y: 4, z: 4, core: 2. Of those that a mesh axis runs over, the one named last changes fastest.
Arguments:
- density: bfloat16 [4096, 128, 128], P(('slab', 'tile')), may hold values from 0.099609375 to 10
- send_list: int32 [128, 16, 4], P(('slab', 'tile')), may hold values from 0 to 31, as said below
- entry_tile: int32 [128, 768], P(('slab', 'tile')), may hold values from 0 to 95
- entry_block: int32 [128, 768], P(('slab', 'tile')), may hold values from 0 to 63
- entry_rows: int32 [128, 768], P(('slab', 'tile')), may hold values from 0 to 63
- entry_cols: int32 [128, 768], P(('slab', 'tile')), may hold values from 0 to 63
- rows_table: bfloat16 [64, 128, 128], replicated, may hold values from 0 to 0.0024871826
- cols_table: bfloat16 [64, 128, 128], replicated, may hold values from 0 to 0.0024871826
- target: float32 [1536, 128, 128], P('tile'), may hold values from 0.5 to 8
Outputs:
- image: float32 [1536, 128, 128], P('tile', 'slab')
- density_grad: float32 [4096, 128, 128], P(('slab', 'tile'))
Inputs may be any that keep to these rules, and one draw needn't show every extreme that they name: `send_list`: within one row of 4 numbers (one device, one index along tile) the numbers are all different.
All inputs are finite; a program needn't handle non-finite values.
Results may differ from a plain program's by a relative error of at most 0.0003.
Values may be sent and summed in bfloat16 or wider, within the bound.
No kernel may reach another device: no remote copies, remote signals or barrier semaphores. Data moves between devices by JAX's collectives and lax.ppermute only.
A program may use at most 128 MiB of HBM per device.

v0:
```python
import jax
import jax.numpy as jnp
from jax import lax
from jax.sharding import PartitionSpec as P

entry_group = 64


def loss_slope(image, target):
    return ((jnp.log1p(image) - jnp.log1p(target)) / (1.0 + image)).astype(jnp.bfloat16)


def pick_rows(indices, table):
    count = table.shape[0]
    chooser = (indices[:, None] == jnp.arange(count, dtype=jnp.int32)[None, :]).astype(table.dtype)
    picked = jnp.dot(chooser, table.reshape(count, -1), preferred_element_type=jnp.float32)
    return picked.astype(table.dtype).reshape((indices.shape[0],) + table.shape[1:])


def add_rows(indices, values, count):
    placer = (jnp.arange(count, dtype=jnp.int32)[:, None] == indices[None, :]).astype(jnp.float32)
    summed = jnp.dot(
        placer,
        values.reshape(values.shape[0], -1),
        precision=lax.Precision.HIGHEST,
        preferred_element_type=jnp.float32,
    )
    return summed.reshape((count,) + values.shape[1:])


def local(
    density,
    send_list,
    entry_tile,
    entry_block,
    entry_rows,
    entry_cols,
    rows_table,
    cols_table,
    target,
):
    cell = density.shape[1]
    pix = rows_table.shape[1]
    tiles_here = target.shape[0]
    send_index = send_list[0]
    peers, slots = send_index.shape
    outgoing = density[send_index]
    received = lax.all_to_all(outgoing, "tile", split_axis=0, concat_axis=0, tiled=True).reshape(
        peers * slots, cell, cell
    )
    items = (
        entry_tile.reshape(-1, entry_group),
        entry_block.reshape(-1, entry_group),
        entry_rows.reshape(-1, entry_group),
        entry_cols.reshape(-1, entry_group),
    )

    def forward_step(total, item):
        tile_ids, block_ids, row_ids, col_ids = item
        left = pick_rows(row_ids, rows_table)
        blocks = pick_rows(block_ids, received)
        right = pick_rows(col_ids, cols_table)
        halfway = jnp.einsum(
            "epc,ecd->epd", left, blocks, preferred_element_type=jnp.float32
        ).astype(jnp.bfloat16)
        contrib = jnp.einsum("epd,edq->epq", halfway, right, preferred_element_type=jnp.float32)
        return (total + add_rows(tile_ids, contrib, tiles_here), None)

    partial_image, _ = lax.scan(forward_step, jnp.zeros((tiles_here, pix, pix), jnp.float32), items)
    band = pix // lax.axis_size("slab")
    first_row = lax.axis_index("slab") * band
    image = lax.psum(partial_image, "slab")
    pixel_grad = loss_slope(image, target)
    image_rows = lax.dynamic_slice_in_dim(image, first_row, band, 1)

    def backward_step(total, item):
        tile_ids, block_ids, row_ids, col_ids = item
        left = pick_rows(row_ids, rows_table)
        right = pick_rows(col_ids, cols_table)
        grads = pick_rows(tile_ids, pixel_grad)
        back = jnp.einsum("epq,edq->epd", grads, right, preferred_element_type=jnp.float32).astype(
            jnp.bfloat16
        )
        delta = jnp.einsum("epc,epd->ecd", left, back, preferred_element_type=jnp.float32)
        return (total + add_rows(block_ids, delta, peers * slots), None)

    slot_grads, _ = lax.scan(
        backward_step, jnp.zeros((peers * slots, cell, cell), jnp.float32), items
    )
    returned = lax.all_to_all(
        slot_grads.reshape(peers, slots, cell, cell),
        "tile",
        split_axis=0,
        concat_axis=0,
        tiled=True,
    )
    density_grad = add_rows(
        send_index.reshape(-1), returned.reshape(-1, cell, cell), density.shape[0]
    )
    return (image_rows, density_grad)


def solution(mesh):
    return jax.shard_map(
        local,
        mesh=mesh,
        in_specs=(
            P(("slab", "tile"), None, None),
            P(("slab", "tile"), None, None),
            P(("slab", "tile"), None),
            P(("slab", "tile"), None),
            P(("slab", "tile"), None),
            P(("slab", "tile"), None),
            P(),
            P(),
            P("tile", None, None),
        ),
        out_specs=(P("tile", "slab", None), P(("slab", "tile"), None, None)),
        check_vma=False,
    )
```

profile of v0, /device:TPU:1, one launch (start us, length us, event | category | flops | bytes accessed | tf_op | source)
XLA Modules:
  0.0 939.2 jit_solution(10990969379126689471)
XLA Ops:
  10.6 7.8 all-to-all-start
  18.8 30.1 %all-to-all-done = bf16[16,4,128,128]{3,2,1,0:T(8,128)(2,1)} async-done(((bf16[16,4,128,128]{3,2,1,0:T(8,128)(2,1)}), bf16[16,4,128,128]{3,2,1,0:T(8,128)(2,1)}, u32[]{:S(2)}, u32[]{:S(2)}) %all-to-all-start) | async-done | bytes 2097184 | tf_op jit(solution)/shard_map/all_to_all | solution.py:48
  48.9 358.5 %while.22 = (s32[]{:T(128)}, f32[96,128,128]{2,0,1:T(8,128)}, s32[12,64]{1,0:T(8,128)S(1)}, s32[12,64]{1,0:T(8,128)S(1)}, bf16[64,128,128]{2,1,0:T(8,128)(2,1)},...) while((s32[]{:T(128)}, f32[96,128,128]{2,0,1:T(8,128)}, ...), condition=%wide.region_1.2_spmd.clone, body=%wide.region_0.1_spmd.clone.sunk | while | flops 2154842112 | bytes 69209280 | solution.py:69
  66.5 10.6 %select_add_fusion.4 = f32[96,128,128]{2,0,1:T(8,128)} fusion(f32[96,128,128]{2,0,1:T(8,128)} %get-tuple-element.344, pred[]{:T(512)S(6)} %compare.6, s32[64]{0:T(128)S(1)} %get-tuple-element.315, f32[8,8,128,128]{3,2,1,0:T(8,128)} %bitcast.225), kind=kOutput, calls=%fused_computation.4.clone.1 | convolution fusion | flops 1211111424 | bytes 16777472 | tf_op jit(solution)/shard_map/while/body/eval_jaxpr/dot_general | solution.py:22
  94.6 12.4 %select_add_fusion.4 = f32[96,128,128]{2,0,1:T(8,128)} fusion(f32[96,128,128]{2,0,1:T(8,128)} %get-tuple-element.344, pred[]{:T(512)S(6)} %compare.6, s32[64]{0:T(128)S(1)} %get-tuple-element.315, f32[8,8,128,128]{3,2,1,0:T(8,128)} %bitcast.225), kind=kOutput, calls=%fused_computation.4.clone.1 | convolution fusion | flops 1211111424 | bytes 16777472 | tf_op jit(solution)/shard_map/while/body/eval_jaxpr/dot_general | solution.py:22
  124.7 12.4 %select_add_fusion.4 = f32[96,128,128]{2,0,1:T(8,128)} fusion(f32[96,128,128]{2,0,1:T(8,128)} %get-tuple-element.344, pred[]{:T(512)S(6)} %compare.6, s32[64]{0:T(128)S(1)} %get-tuple-element.315, f32[8,8,128,128]{3,2,1,0:T(8,128)} %bitcast.225), kind=kOutput, calls=%fused_computation.4.clone.1 | convolution fusion | flops 1211111424 | bytes 16777472 | tf_op jit(solution)/shard_map/while/body/eval_jaxpr/dot_general | solution.py:22
  149.2 5.5 fusion.124
  154.7 12.4 %select_add_fusion.4 = f32[96,128,128]{2,0,1:T(8,128)} fusion(f32[96,128,128]{2,0,1:T(8,128)} %get-tuple-element.344, pred[]{:T(512)S(6)} %compare.6, s32[64]{0:T(128)S(1)} %get-tuple-element.315, f32[8,8,128,128]{3,2,1,0:T(8,128)} %bitcast.225), kind=kOutput, calls=%fused_computation.4.clone.1 | convolution fusion | flops 1211111424 | bytes 16777472 | tf_op jit(solution)/shard_map/while/body/eval_jaxpr/dot_general | solution.py:22
  184.7 12.4 %select_add_fusion.4 = f32[96,128,128]{2,0,1:T(8,128)} fusion(f32[96,128,128]{2,0,1:T(8,128)} %get-tuple-element.344, pred[]{:T(512)S(6)} %compare.6, s32[64]{0:T(128)S(1)} %get-tuple-element.315, f32[8,8,128,128]{3,2,1,0:T(8,128)} %bitcast.225), kind=kOutput, calls=%fused_computation.4.clone.1 | convolution fusion | flops 1211111424 | bytes 16777472 | tf_op jit(solution)/shard_map/while/body/eval_jaxpr/dot_general | solution.py:22
  214.7 12.4 %select_add_fusion.4 = f32[96,128,128]{2,0,1:T(8,128)} fusion(f32[96,128,128]{2,0,1:T(8,128)} %get-tuple-element.344, pred[]{:T(512)S(6)} %compare.6, s32[64]{0:T(128)S(1)} %get-tuple-element.315, f32[8,8,128,128]{3,2,1,0:T(8,128)} %bitcast.225), kind=kOutput, calls=%fused_computation.4.clone.1 | convolution fusion | flops 1211111424 | bytes 16777472 | tf_op jit(solution)/shard_map/while/body/eval_jaxpr/dot_general | solution.py:22
  244.8 12.4 %select_add_fusion.4 = f32[96,128,128]{2,0,1:T(8,128)} fusion(f32[96,128,128]{2,0,1:T(8,128)} %get-tuple-element.344, pred[]{:T(512)S(6)} %compare.6, s32[64]{0:T(128)S(1)} %get-tuple-element.315, f32[8,8,128,128]{3,2,1,0:T(8,128)} %bitcast.225), kind=kOutput, calls=%fused_computation.4.clone.1 | convolution fusion | flops 1211111424 | bytes 16777472 | tf_op jit(solution)/shard_map/while/body/eval_jaxpr/dot_general | solution.py:22
  274.8 12.4 %select_add_fusion.4 = f32[96,128,128]{2,0,1:T(8,128)} fusion(f32[96,128,128]{2,0,1:T(8,128)} %get-tuple-element.344, pred[]{:T(512)S(6)} %compare.6, s32[64]{0:T(128)S(1)} %get-tuple-element.315, f32[8,8,128,128]{3,2,1,0:T(8,128)} %bitcast.225), kind=kOutput, calls=%fused_computation.4.clone.1 | convolution fusion | flops 1211111424 | bytes 16777472 | tf_op jit(solution)/shard_map/while/body/eval_jaxpr/dot_general | solution.py:22
  304.8 12.4 %select_add_fusion.4 = f32[96,128,128]{2,0,1:T(8,128)} fusion(f32[96,128,128]{2,0,1:T(8,128)} %get-tuple-element.344, pred[]{:T(512)S(6)} %compare.6, s32[64]{0:T(128)S(1)} %get-tuple-element.315, f32[8,8,128,128]{3,2,1,0:T(8,128)} %bitcast.225), kind=kOutput, calls=%fused_computation.4.clone.1 | convolution fusion | flops 1211111424 | bytes 16777472 | tf_op jit(solution)/shard_map/while/body/eval_jaxpr/dot_general | solution.py:22
  334.8 12.4 %select_add_fusion.4 = f32[96,128,128]{2,0,1:T(8,128)} fusion(f32[96,128,128]{2,0,1:T(8,128)} %get-tuple-element.344, pred[]{:T(512)S(6)} %compare.6, s32[64]{0:T(128)S(1)} %get-tuple-element.315, f32[8,8,128,128]{3,2,1,0:T(8,128)} %bitcast.225), kind=kOutput, calls=%fused_computation.4.clone.1 | convolution fusion | flops 1211111424 | bytes 16777472 | tf_op jit(solution)/shard_map/while/body/eval_jaxpr/dot_general | solution.py:22
  364.8 12.4 %select_add_fusion.4 = f32[96,128,128]{2,0,1:T(8,128)} fusion(f32[96,128,128]{2,0,1:T(8,128)} %get-tuple-element.344, pred[]{:T(512)S(6)} %compare.6, s32[64]{0:T(128)S(1)} %get-tuple-element.315, f32[8,8,128,128]{3,2,1,0:T(8,128)} %bitcast.225), kind=kOutput, calls=%fused_computation.4.clone.1 | convolution fusion | flops 1211111424 | bytes 16777472 | tf_op jit(solution)/shard_map/while/body/eval_jaxpr/dot_general | solution.py:22
  394.9 12.4 %select_add_fusion.4 = f32[96,128,128]{2,0,1:T(8,128)} fusion(f32[96,128,128]{2,0,1:T(8,128)} %get-tuple-element.344, pred[]{:T(512)S(6)} %compare.6, s32[64]{0:T(128)S(1)} %get-tuple-element.315, f32[8,8,128,128]{3,2,1,0:T(8,128)} %bitcast.225), kind=kOutput, calls=%fused_computation.4.clone.1 | convolution fusion | flops 1211111424 | bytes 16777472 | tf_op jit(solution)/shard_map/while/body/eval_jaxpr/dot_general | solution.py:22
  407.4 9.1 copy.20
  416.6 84.4 %all-reduce.2.cloned.1.call-done = f32[96,128,128]{2,1,0:T(8,128)} async-done(((f32[96,128,128]{2,1,0:T(8,128)}), f32[96,128,128]{2,1,0:T(8,128)}) %all-reduce.2.cloned.1.call-update) | async-done | bytes 6291472 | tf_op jit(solution)/shard_map/psum | solution.py:72
  501.0 10.7 %divide_convert_fusion = bf16[96,128,128]{2,1,0:T(8,128)(2,1)} fusion(f32[96,128,128]{2,1,0:T(8,128)} %all-reduce.2.cloned.1.call-done, f32[96,128,128]{2,1,0:T(8,128)} %param.21), kind=kLoop, calls=%fused_computation.75 | loop fusion | flops 6291456 | bytes 15728640 | tf_op jit(solution)/shard_map/convert_element_type | solution.py:10
  511.7 337.5 %while.23 = (s32[]{:T(128)}, f32[64,128,128]{2,0,1:T(8,128)}, s32[12,64]{1,0:T(8,128)S(1)}, s32[12,64]{1,0:T(8,128)S(1)}, bf16[64,128,128]{2,1,0:T(8,128)(2,1)S(...) while((s32[]{:T(128)}, f32[64,128,128]{2,0,1:T(8,128)}, ...), condition=%wide.region_4.5_spmd.clone, body=%wide.region_3.4_spmd.clone.sunk | while | flops 1818249216 | bytes 78646496 | solution.py:87
  523.3 6.5 fusion.139
  529.7 9.1 select_add_fusion.5
  550.2 6.5 fusion.139
  556.7 10.3 %select_add_fusion.5 = f32[64,128,128]{2,0,1:T(8,128)} fusion(f32[64,128,128]{2,0,1:T(8,128)} %get-tuple-element.377, pred[]{:T(512)S(6)} %compare.7, s32[64]{0:T(128)S(1)} %get-tuple-element.328, f32[8,8,128,128]{3,2,1,0:T(8,128)} %bitcast.224), kind=kOutput, calls=%fused_computation.45.clone.1 | convolution fusion | flops 807407616 | bytes 12583169 | tf_op jit(solution)/shard_map/while/body/eval_jaxpr/dot_general | solution.py:22
  578.4 6.5 fusion.139
  584.9 10.3 %select_add_fusion.5 = f32[64,128,128]{2,0,1:T(8,128)} fusion(f32[64,128,128]{2,0,1:T(8,128)} %get-tuple-element.377, pred[]{:T(512)S(6)} %compare.7, s32[64]{0:T(128)S(1)} %get-tuple-element.328, f32[8,8,128,128]{3,2,1,0:T(8,128)} %bitcast.224), kind=kOutput, calls=%fused_computation.45.clone.1 | convolution fusion | flops 807407616 | bytes 12583169 | tf_op jit(solution)/shard_map/while/body/eval_jaxpr/dot_general | solution.py:22
  606.6 6.5 fusion.139
  613.1 10.3 %select_add_fusion.5 = f32[64,128,128]{2,0,1:T(8,128)} fusion(f32[64,128,128]{2,0,1:T(8,128)} %get-tuple-element.377, pred[]{:T(512)S(6)} %compare.7, s32[64]{0:T(128)S(1)} %get-tuple-element.328, f32[8,8,128,128]{3,2,1,0:T(8,128)} %bitcast.224), kind=kOutput, calls=%fused_computation.45.clone.1 | convolution fusion | flops 807407616 | bytes 12583169 | tf_op jit(solution)/shard_map/while/body/eval_jaxpr/dot_general | solution.py:22
  634.8 6.5 fusion.139
  641.3 10.3 %select_add_fusion.5 = f32[64,128,128]{2,0,1:T(8,128)} fusion(f32[64,128,128]{2,0,1:T(8,128)} %get-tuple-element.377, pred[]{:T(512)S(6)} %compare.7, s32[64]{0:T(128)S(1)} %get-tuple-element.328, f32[8,8,128,128]{3,2,1,0:T(8,128)} %bitcast.224), kind=kOutput, calls=%fused_computation.45.clone.1 | convolution fusion | flops 807407616 | bytes 12583169 | tf_op jit(solution)/shard_map/while/body/eval_jaxpr/dot_general | solution.py:22
  663.0 6.5 fusion.139
  669.5 10.3 %select_add_fusion.5 = f32[64,128,128]{2,0,1:T(8,128)} fusion(f32[64,128,128]{2,0,1:T(8,128)} %get-tuple-element.377, pred[]{:T(512)S(6)} %compare.7, s32[64]{0:T(128)S(1)} %get-tuple-element.328, f32[8,8,128,128]{3,2,1,0:T(8,128)} %bitcast.224), kind=kOutput, calls=%fused_computation.45.clone.1 | convolution fusion | flops 807407616 | bytes 12583169 | tf_op jit(solution)/shard_map/while/body/eval_jaxpr/dot_general | solution.py:22
  691.2 6.5 fusion.139
  697.7 10.3 %select_add_fusion.5 = f32[64,128,128]{2,0,1:T(8,128)} fusion(f32[64,128,128]{2,0,1:T(8,128)} %get-tuple-element.377, pred[]{:T(512)S(6)} %compare.7, s32[64]{0:T(128)S(1)} %get-tuple-element.328, f32[8,8,128,128]{3,2,1,0:T(8,128)} %bitcast.224), kind=kOutput, calls=%fused_computation.45.clone.1 | convolution fusion | flops 807407616 | bytes 12583169 | tf_op jit(solution)/shard_map/while/body/eval_jaxpr/dot_general | solution.py:22
  719.4 6.5 fusion.139
  725.8 10.3 %select_add_fusion.5 = f32[64,128,128]{2,0,1:T(8,128)} fusion(f32[64,128,128]{2,0,1:T(8,128)} %get-tuple-element.377, pred[]{:T(512)S(6)} %compare.7, s32[64]{0:T(128)S(1)} %get-tuple-element.328, f32[8,8,128,128]{3,2,1,0:T(8,128)} %bitcast.224), kind=kOutput, calls=%fused_computation.45.clone.1 | convolution fusion | flops 807407616 | bytes 12583169 | tf_op jit(solution)/shard_map/while/body/eval_jaxpr/dot_general | solution.py:22
  747.6 6.5 fusion.139
  754.0 10.3 %select_add_fusion.5 = f32[64,128,128]{2,0,1:T(8,128)} fusion(f32[64,128,128]{2,0,1:T(8,128)} %get-tuple-element.377, pred[]{:T(512)S(6)} %compare.7, s32[64]{0:T(128)S(1)} %get-tuple-element.328, f32[8,8,128,128]{3,2,1,0:T(8,128)} %bitcast.224), kind=kOutput, calls=%fused_computation.45.clone.1 | convolution fusion | flops 807407616 | bytes 12583169 | tf_op jit(solution)/shard_map/while/body/eval_jaxpr/dot_general | solution.py:22
  775.7 6.5 fusion.139
  782.2 10.3 %select_add_fusion.5 = f32[64,128,128]{2,0,1:T(8,128)} fusion(f32[64,128,128]{2,0,1:T(8,128)} %get-tuple-element.377, pred[]{:T(512)S(6)} %compare.7, s32[64]{0:T(128)S(1)} %get-tuple-element.328, f32[8,8,128,128]{3,2,1,0:T(8,128)} %bitcast.224), kind=kOutput, calls=%fused_computation.45.clone.1 | convolution fusion | flops 807407616 | bytes 12583169 | tf_op jit(solution)/shard_map/while/body/eval_jaxpr/dot_general | solution.py:22
  803.9 6.5 fusion.139
  810.4 10.3 %select_add_fusion.5 = f32[64,128,128]{2,0,1:T(8,128)} fusion(f32[64,128,128]{2,0,1:T(8,128)} %get-tuple-element.377, pred[]{:T(512)S(6)} %compare.7, s32[64]{0:T(128)S(1)} %get-tuple-element.328, f32[8,8,128,128]{3,2,1,0:T(8,128)} %bitcast.224), kind=kOutput, calls=%fused_computation.45.clone.1 | convolution fusion | flops 807407616 | bytes 12583169 | tf_op jit(solution)/shard_map/while/body/eval_jaxpr/dot_general | solution.py:22
  832.1 6.5 fusion.139
  838.6 10.3 %select_add_fusion.5 = f32[64,128,128]{2,0,1:T(8,128)} fusion(f32[64,128,128]{2,0,1:T(8,128)} %get-tuple-element.377, pred[]{:T(512)S(6)} %compare.7, s32[64]{0:T(128)S(1)} %get-tuple-element.328, f32[8,8,128,128]{3,2,1,0:T(8,128)} %bitcast.224), kind=kOutput, calls=%fused_computation.45.clone.1 | convolution fusion | flops 807407616 | bytes 12583169 | tf_op jit(solution)/shard_map/while/body/eval_jaxpr/dot_general | solution.py:22
  849.2 6.6 copy.22
  855.8 6.7 all-to-all-start.1
  864.8 58.3 %all-to-all-done.1 = f32[16,4,128,128]{3,2,1,0:T(8,128)} async-done(((f32[16,4,128,128]{3,2,1,0:T(8,128)}), f32[16,4,128,128]{3,2,1,0:T(8,128)}, u32[]{:S(2)}, u32[]{:S(2)}) %all-to-all-start.1) | async-done | bytes 4194336 | tf_op jit(solution)/shard_map/all_to_all | solution.py:90
  923.2 6.2 fusion.68
  (362 shorter events, 349.9 us)
Async XLA Ops:
  10.5 7.9 copy-start.10
  10.5 8.0 copy-start.11
  10.5 8.1 copy-start.12
  10.6 8.1 copy-start.13
  10.6 38.3 %copy-start.5 = (bf16[64,128,128]{2,1,0:T(8,128)(2,1)S(1)}, bf16[64,128,128]{2,1,0:T(8,128)(2,1)}, u32[]{:S(2)}) copy-start(bf16[64,128,128]{2,1,0:T(8,128)(2,1)} %param.20) | copy-start | bytes 6291460
  10.6 38.3 %all-to-all-start = ((bf16[16,4,128,128]{3,2,1,0:T(8,128)(2,1)}), bf16[16,4,128,128]{3,2,1,0:T(8,128)(2,1)}, u32[]{:S(2)}, u32[]{:S(2)}) async-start(bf16[16,4,128,128]{3,2,1,0:T(8,128)(2,1)} %bitcast.238), calls=%async_computation | async-start | bytes 4194304 | tf_op jit(solution)/shard_map/all_to_all | solution.py:48
  18.4 482.6 %all-reduce.2.cloned.1.call-start = ((), (), s32[]{:S(2)}) async-start(), calls=%async_computation.2 | async-start | bytes 12582912 | tf_op jit(solution)/shard_map/psum | solution.py:72
  66.5 10.6 %copy-start.6 = (bf16[64,128,128]{2,1,0:T(8,128)(2,1)S(1)}, bf16[64,128,128]{2,1,0:T(8,128)(2,1)}, u32[]{:S(2)}) copy-start(bf16[64,128,128]{2,1,0:T(8,128)(2,1)} %get-tuple-element.423) | copy-start | bytes 6291460 | tf_op jit(solution)/shard_map/while
  94.6 12.4 %copy-start.6 = (bf16[64,128,128]{2,1,0:T(8,128)(2,1)S(1)}, bf16[64,128,128]{2,1,0:T(8,128)(2,1)}, u32[]{:S(2)}) copy-start(bf16[64,128,128]{2,1,0:T(8,128)(2,1)} %get-tuple-element.423) | copy-start | bytes 6291460 | tf_op jit(solution)/shard_map/while
  124.7 12.4 %copy-start.6 = (bf16[64,128,128]{2,1,0:T(8,128)(2,1)S(1)}, bf16[64,128,128]{2,1,0:T(8,128)(2,1)}, u32[]{:S(2)}) copy-start(bf16[64,128,128]{2,1,0:T(8,128)(2,1)} %get-tuple-element.423) | copy-start | bytes 6291460 | tf_op jit(solution)/shard_map/while
  154.7 12.4 %copy-start.6 = (bf16[64,128,128]{2,1,0:T(8,128)(2,1)S(1)}, bf16[64,128,128]{2,1,0:T(8,128)(2,1)}, u32[]{:S(2)}) copy-start(bf16[64,128,128]{2,1,0:T(8,128)(2,1)} %get-tuple-element.423) | copy-start | bytes 6291460 | tf_op jit(solution)/shard_map/while
  184.7 12.4 %copy-start.6 = (bf16[64,128,128]{2,1,0:T(8,128)(2,1)S(1)}, bf16[64,128,128]{2,1,0:T(8,128)(2,1)}, u32[]{:S(2)}) copy-start(bf16[64,128,128]{2,1,0:T(8,128)(2,1)} %get-tuple-element.423) | copy-start | bytes 6291460 | tf_op jit(solution)/shard_map/while
  214.7 12.4 %copy-start.6 = (bf16[64,128,128]{2,1,0:T(8,128)(2,1)S(1)}, bf16[64,128,128]{2,1,0:T(8,128)(2,1)}, u32[]{:S(2)}) copy-start(bf16[64,128,128]{2,1,0:T(8,128)(2,1)} %get-tuple-element.423) | copy-start | bytes 6291460 | tf_op jit(solution)/shard_map/while
  244.8 12.4 %copy-start.6 = (bf16[64,128,128]{2,1,0:T(8,128)(2,1)S(1)}, bf16[64,128,128]{2,1,0:T(8,128)(2,1)}, u32[]{:S(2)}) copy-start(bf16[64,128,128]{2,1,0:T(8,128)(2,1)} %get-tuple-element.423) | copy-start | bytes 6291460 | tf_op jit(solution)/shard_map/while
  274.8 12.4 %copy-start.6 = (bf16[64,128,128]{2,1,0:T(8,128)(2,1)S(1)}, bf16[64,128,128]{2,1,0:T(8,128)(2,1)}, u32[]{:S(2)}) copy-start(bf16[64,128,128]{2,1,0:T(8,128)(2,1)} %get-tuple-element.423) | copy-start | bytes 6291460 | tf_op jit(solution)/shard_map/while
  304.8 12.4 %copy-start.6 = (bf16[64,128,128]{2,1,0:T(8,128)(2,1)S(1)}, bf16[64,128,128]{2,1,0:T(8,128)(2,1)}, u32[]{:S(2)}) copy-start(bf16[64,128,128]{2,1,0:T(8,128)(2,1)} %get-tuple-element.423) | copy-start | bytes 6291460 | tf_op jit(solution)/shard_map/while
  334.8 12.4 %copy-start.6 = (bf16[64,128,128]{2,1,0:T(8,128)(2,1)S(1)}, bf16[64,128,128]{2,1,0:T(8,128)(2,1)}, u32[]{:S(2)}) copy-start(bf16[64,128,128]{2,1,0:T(8,128)(2,1)} %get-tuple-element.423) | copy-start | bytes 6291460 | tf_op jit(solution)/shard_map/while
  364.8 12.4 %copy-start.6 = (bf16[64,128,128]{2,1,0:T(8,128)(2,1)S(1)}, bf16[64,128,128]{2,1,0:T(8,128)(2,1)}, u32[]{:S(2)}) copy-start(bf16[64,128,128]{2,1,0:T(8,128)(2,1)} %get-tuple-element.423) | copy-start | bytes 6291460 | tf_op jit(solution)/shard_map/while
  394.9 12.4 %copy-start.6 = (bf16[64,128,128]{2,1,0:T(8,128)(2,1)S(1)}, bf16[64,128,128]{2,1,0:T(8,128)(2,1)}, u32[]{:S(2)}) copy-start(bf16[64,128,128]{2,1,0:T(8,128)(2,1)} %get-tuple-element.423) | copy-start | bytes 6291460 | tf_op jit(solution)/shard_map/while
  416.5 95.1 %copy-start.3 = (bf16[64,128,128]{2,1,0:T(8,128)(2,1)S(1)}, bf16[64,128,128]{2,1,0:T(8,128)(2,1)}, u32[]{:S(2)}) copy-start(bf16[64,128,128]{2,1,0:T(8,128)(2,1)} %get-tuple-element.416) | copy-start | bytes 6291460
  517.8 1.9 copy-start.7
  529.7 9.1 copy-start.4
  544.7 1.9 copy-start.7
  556.7 10.3 %copy-start.4 = (bf16[64,128,128]{2,1,0:T(8,128)(2,1)S(1)}, bf16[64,128,128]{2,1,0:T(8,128)(2,1)}, u32[]{:S(2)}) copy-start(bf16[64,128,128]{2,1,0:T(8,128)(2,1)} %get-tuple-element.411) | copy-start | bytes 6291460 | tf_op jit(solution)/shard_map/while
  568.7 1.9 copy-start.8
  572.9 1.9 copy-start.7
  584.9 10.3 %copy-start.4 = (bf16[64,128,128]{2,1,0:T(8,128)(2,1)S(1)}, bf16[64,128,128]{2,1,0:T(8,128)(2,1)}, u32[]{:S(2)}) copy-start(bf16[64,128,128]{2,1,0:T(8,128)(2,1)} %get-tuple-element.411) | copy-start | bytes 6291460 | tf_op jit(solution)/shard_map/while
  601.1 1.9 copy-start.7
  613.1 10.3 %copy-start.4 = (bf16[64,128,128]{2,1,0:T(8,128)(2,1)S(1)}, bf16[64,128,128]{2,1,0:T(8,128)(2,1)}, u32[]{:S(2)}) copy-start(bf16[64,128,128]{2,1,0:T(8,128)(2,1)} %get-tuple-element.411) | copy-start | bytes 6291460 | tf_op jit(solution)/shard_map/while
  629.3 1.9 copy-start.7
  641.3 10.3 %copy-start.4 = (bf16[64,128,128]{2,1,0:T(8,128)(2,1)S(1)}, bf16[64,128,128]{2,1,0:T(8,128)(2,1)}, u32[]{:S(2)}) copy-start(bf16[64,128,128]{2,1,0:T(8,128)(2,1)} %get-tuple-element.411) | copy-start | bytes 6291460 | tf_op jit(solution)/shard_map/while
  657.5 1.9 copy-start.7
  669.5 10.3 %copy-start.4 = (bf16[64,128,128]{2,1,0:T(8,128)(2,1)S(1)}, bf16[64,128,128]{2,1,0:T(8,128)(2,1)}, u32[]{:S(2)}) copy-start(bf16[64,128,128]{2,1,0:T(8,128)(2,1)} %get-tuple-element.411) | copy-start | bytes 6291460 | tf_op jit(solution)/shard_map/while
  685.7 1.9 copy-start.7
  697.7 10.3 %copy-start.4 = (bf16[64,128,128]{2,1,0:T(8,128)(2,1)S(1)}, bf16[64,128,128]{2,1,0:T(8,128)(2,1)}, u32[]{:S(2)}) copy-start(bf16[64,128,128]{2,1,0:T(8,128)(2,1)} %get-tuple-element.411) | copy-start | bytes 6291460 | tf_op jit(solution)/shard_map/while
  713.9 1.9 copy-start.7
  725.8 10.3 %copy-start.4 = (bf16[64,128,128]{2,1,0:T(8,128)(2,1)S(1)}, bf16[64,128,128]{2,1,0:T(8,128)(2,1)}, u32[]{:S(2)}) copy-start(bf16[64,128,128]{2,1,0:T(8,128)(2,1)} %get-tuple-element.411) | copy-start | bytes 6291460 | tf_op jit(solution)/shard_map/while
  742.0 1.9 copy-start.7
  754.0 10.3 %copy-start.4 = (bf16[64,128,128]{2,1,0:T(8,128)(2,1)S(1)}, bf16[64,128,128]{2,1,0:T(8,128)(2,1)}, u32[]{:S(2)}) copy-start(bf16[64,128,128]{2,1,0:T(8,128)(2,1)} %get-tuple-element.411) | copy-start | bytes 6291460 | tf_op jit(solution)/shard_map/while
  770.2 1.9 copy-start.7
  782.2 10.3 %copy-start.4 = (bf16[64,128,128]{2,1,0:T(8,128)(2,1)S(1)}, bf16[64,128,128]{2,1,0:T(8,128)(2,1)}, u32[]{:S(2)}) copy-start(bf16[64,128,128]{2,1,0:T(8,128)(2,1)} %get-tuple-element.411) | copy-start | bytes 6291460 | tf_op jit(solution)/shard_map/while
  798.4 1.9 copy-start.7
  810.4 10.3 %copy-start.4 = (bf16[64,128,128]{2,1,0:T(8,128)(2,1)S(1)}, bf16[64,128,128]{2,1,0:T(8,128)(2,1)}, u32[]{:S(2)}) copy-start(bf16[64,128,128]{2,1,0:T(8,128)(2,1)} %get-tuple-element.411) | copy-start | bytes 6291460 | tf_op jit(solution)/shard_map/while
  826.6 1.9 copy-start.7
  838.6 10.3 %copy-start.4 = (bf16[64,128,128]{2,1,0:T(8,128)(2,1)S(1)}, bf16[64,128,128]{2,1,0:T(8,128)(2,1)}, u32[]{:S(2)}) copy-start(bf16[64,128,128]{2,1,0:T(8,128)(2,1)} %get-tuple-element.411) | copy-start | bytes 6291460 | tf_op jit(solution)/shard_map/while
  855.8 6.7 copy-start.9
  855.8 67.3 %all-to-all-start.1 = ((f32[16,4,128,128]{3,2,1,0:T(8,128)}), f32[16,4,128,128]{3,2,1,0:T(8,128)}, u32[]{:S(2)}, u32[]{:S(2)}) async-start(f32[16,4,128,128]{3,2,1,0:T(8,128)} %copy.22), calls=%async_computation.1 | async-start | bytes 8388608 | tf_op jit(solution)/shard_map/all_to_all | solution.py:90
  923.2 8.7 copy-start.1
  (24 other events, 41.3 us)
Sparse Core Ops, SparseCore 0:
  416.7 84.2 all-reduce.1
where the time goes:
time: 953 us; the launch traced here: 939 us
  matrix products  567 us (59%)
  waiting for transfers between devices  173 us (18%)
  local copies, waits for them, and re-layouts  157 us (16%)
  between operations  14.6 us (2%)
  starting transfers between devices  14.5 us (2%)
  other arithmetic  11.5 us (1%)
    dot_general x25, matrix products, add_rows(): jnp.dot(placer, values.reshape(values.shape[0], -1), precision=lax.Precis...  276 us
    dot_general x72, matrix products, pick_rows(): jnp.dot(chooser, table.reshape(count, -1), preferred_element_type=jnp.flo...  147 us
    while x192, local copies, waits for them, and re-layouts  133 us
    psum x1, waiting for transfers between devices, local(): image = lax.psum(partial_image, 'slab')  84.4 us
    dot_general x12, matrix products, backward_step(): jnp.einsum('epc,epd->ecd', left, back, preferred_element_type=jnp.float32)  77.8 us
    dot_general x12, matrix products, forward_step(): jnp.einsum('epd,edq->epq', halfway, right, preferred_element_type=jnp.flo...  66.2 us
    all_to_all x1, waiting for transfers between devices, local(): lax.all_to_all(slot_grads.reshape(peers, slots, cell, cell), 'tile', spli...  58.3 us
    all_to_all x1, waiting for transfers between devices, local(): lax.all_to_all(outgoing, 'tile', split_axis=0, concat_axis=0, tiled=True)  30.1 us
  transfers between devices with their start and end apart: 3, of which 3 were waited for; matrix products, arithmetic and copies ran while one was open for 0% of the time, Pallas kernels for 0%

commit v1 on v0

v1 whole, which is shorter than its diff:
```python
import functools
import jax
import jax.numpy as jnp
from jax import lax
from jax.experimental import pallas as pl
from jax.experimental.pallas import tpu as pltpu
from jax.sharding import PartitionSpec as P

bf16, f32, i16, i32 = jnp.bfloat16, jnp.float32, jnp.int16, jnp.int32
vmem_bytes = 56 * 2**20
unroll = 32
top = 32000.0
tiny = 1e-30

SMEM = pl.BlockSpec(memory_space=pltpu.SMEM)
VMEM = pl.BlockSpec(memory_space=pltpu.VMEM)


def params():
    return pltpu.CompilerParams(vmem_limit_bytes=vmem_bytes)


def mm(a, b):
    return jnp.dot(a, b, preferred_element_type=f32)


def code_level(peak):
    return jnp.ceil(8.0 * jnp.log2(jnp.maximum(peak, tiny)))


def forward_kernel(tile_ids, block_ids, row_ids, col_ids, rows, cols, blocks, mine, theirs):
    mine[...] = jnp.zeros_like(mine)
    theirs[...] = jnp.zeros_like(theirs)

    def step(i, carry):
        half = []
        for u in range(unroll):
            e = i * unroll + u
            half.append(mm(rows[row_ids[0, e]], blocks[block_ids[0, e]]).astype(bf16))
        parts = []
        for u in range(unroll):
            e = i * unroll + u
            parts.append(mm(half[u], cols[col_ids[0, e]]))
        for u in range(unroll):
            t = tile_ids[0, i * unroll + u]
            for k in range(4):
                mine[k, t] += parts[u][k * 16:(k + 1) * 16]
                theirs[k, t] += parts[u][64 + k * 16:64 + (k + 1) * 16]
        return carry

    lax.fori_loop(0, tile_ids.shape[1] // unroll, step, 0)


def combine_kernel(mine, got, own, q1, q2, q3):
    own[...] = mine[0] + got[0]
    n = own.shape[0]
    for k, q in ((1, q1), (2, q2), (3, q3)):
        def group(g, carry):
            levels = []
            for s in range(16):
                t = g * 16 + s
                v = mine[k, t] + got[k, t]
                level = code_level(jnp.max(v, axis=0, keepdims=True))
                scale = jnp.exp2(level * -0.125) * (2.0 * top)
                q[t] = jnp.round(v * scale - top).astype(i32).astype(i16)
                levels.append(level)
            q[n + g] = jnp.concatenate(levels, 0).astype(i32).astype(i16)
            return carry
        lax.fori_loop(0, n // 16, group, 0)


def slope_kernel(place, own, q1, q2, q3, target, image, grad):
    n = own.shape[0]

    def group(g, carry):
        steps = [jnp.exp2(q[n + g].astype(i32).astype(f32) * 0.125) * (0.5 / top) for q in (q1, q2, q3)]
        for s in range(16):
            t = g * 16 + s
            v = own[t]
            for q, step in zip((q1, q2, q3), steps):
                v = v + (q[t].astype(i32).astype(f32) + top) * step[s:s + 1]
            image[t] = v
            grad[t] = ((jnp.log1p(v) - jnp.log1p(target[t])) / (1.0 + v)).astype(bf16)
        return carry

    lax.fori_loop(0, n // 16, group, 0)


def backward_kernel(tile_ids, block_ids, row_ids, col_ids, rows_t, cols_t, *rest):
    grads, out, acc = rest[:8], rest[8], rest[9]
    acc[...] = jnp.zeros_like(acc)

    def step(i, carry):
        back = []
        for u in range(unroll):
            e = i * unroll + u
            t = tile_ids[0, e]
            g = jnp.concatenate([band[t] for band in grads], 0)
            back.append(mm(g, cols_t[col_ids[0, e]]).astype(bf16))
        parts = []
        for u in range(unroll):
            parts.append(mm(rows_t[row_ids[0, i * unroll + u]], back[u]))
        for u in range(unroll):
            acc[block_ids[0, i * unroll + u]] += parts[u]
        return carry

    lax.fori_loop(0, tile_ids.shape[1] // unroll, step, 0)
    slots = (out.shape[1] - 16) // 128

    def pack(k, carry):
        levels = []
        for s in range(slots):
            v = acc[k * slots + s]
            level = code_level(jnp.max(jnp.abs(v), axis=0, keepdims=True))
            scale = jnp.exp2(level * -0.125) * top
            out[k, s * 128:(s + 1) * 128] = jnp.round(v * scale).astype(i32).astype(i16)
            levels.append(level)
        levels.append(jnp.zeros((16 - slots, 128), f32))
        out[k, slots * 128:slots * 128 + 16] = jnp.concatenate(levels, 0).astype(i32).astype(i16)
        return carry

    lax.fori_loop(0, out.shape[0], pack, 0)


def scatter_kernel(send, coded, out):
    out[...] = jnp.zeros_like(out)
    slots = (coded.shape[1] - 16) // 128

    def step(k, carry):
        steps = jnp.exp2(coded[k, slots * 128:slots * 128 + 16].astype(i32).astype(f32) * 0.125) * (1.0 / top)
        for s in range(slots):
            v = coded[k, s * 128:(s + 1) * 128].astype(i32).astype(f32) * steps[s:s + 1]
            out[send[k, s]] += v
        return carry

    lax.fori_loop(0, coded.shape[0], step, 0)


def local(density, send_list, entry_tile, entry_block, entry_rows, entry_cols, rows_table, cols_table, target):
    tiles = target.shape[0]
    send = send_list[0]
    peers, slots = send.shape
    me = lax.axis_index("slab")
    depth, core = me // 2, me % 2
    order = ((depth + jnp.arange(4)) % 4)[None, :] * 2 + (core + jnp.arange(2))[:, None] % 2
    order = order.reshape(-1).astype(i32)
    rows = jnp.take(rows_table.reshape(-1, 8, 16, 128), order, axis=1).reshape(rows_table.shape)
    rows_t = jnp.swapaxes(rows, 1, 2)
    cols_t = jnp.swapaxes(cols_table, 1, 2)

    pair = [(i, i ^ 1) for i in range(8)]

    def swap(x):
        return lax.ppermute(x, "slab", pair)

    def along(x, s):
        return lax.ppermute(x, "slab", [(i, (i + 2 * s) % 8) for i in range(8)])

    outgoing = density[send]
    blocks = lax.all_to_all(outgoing, "tile", split_axis=0, concat_axis=0, tiled=True)
    blocks = blocks.reshape(peers * slots, 128, 128)

    bands = jax.ShapeDtypeStruct((4, tiles, 16, 128), f32)
    mine, theirs = pl.pallas_call(
        forward_kernel,
        out_shape=(bands, bands),
        in_specs=[SMEM] * 4 + [VMEM] * 3,
        out_specs=(VMEM, VMEM),
        compiler_params=params(),
    )(entry_tile, entry_block, entry_rows, entry_cols, rows, cols_table, blocks)
    got = swap(theirs)
    coded = jax.ShapeDtypeStruct((tiles + tiles // 16, 16, 128), i16)
    own, q1, q2, q3 = pl.pallas_call(
        combine_kernel,
        out_shape=(jax.ShapeDtypeStruct((tiles, 16, 128), f32), coded, coded, coded),
        in_specs=[VMEM] * 2,
        out_specs=(VMEM,) * 4,
        compiler_params=params(),
    )(mine, got)
    q1, q2, q3 = along(q1, 1), along(q2, 2), along(q3, 3)
    band = pl.BlockSpec((tiles, 16, 128), lambda g, place: (0, 0, 0))
    code = pl.BlockSpec(coded.shape, lambda g, place: (0, 0, 0))
    image, grad = pl.pallas_call(
        slope_kernel,
        out_shape=(jax.ShapeDtypeStruct((tiles, 16, 128), f32), jax.ShapeDtypeStruct((tiles, 16, 128), bf16)),
        grid_spec=pltpu.PrefetchScalarGridSpec(
            num_scalar_prefetch=1,
            grid=(1,),
            in_specs=[band, code, code, code, pl.BlockSpec((tiles, 16, 128), lambda g, place: (0, place[0], 0))],
            out_specs=(band, band),
        ),
        compiler_params=params(),
    )(me.reshape(1).astype(i32), own, q1, q2, q3, target)
    grads = [grad, along(grad, 3), along(grad, 2), along(grad, 1)]
    grads += [swap(g) for g in grads]
    packed = pl.pallas_call(
        backward_kernel,
        out_shape=jax.ShapeDtypeStruct((peers, slots * 128 + 16, 128), i16),
        in_specs=[SMEM] * 4 + [VMEM] * 10,
        out_specs=VMEM,
        scratch_shapes=[pltpu.VMEM((peers * slots, 128, 128), f32)],
        compiler_params=params(),
    )(entry_tile, entry_block, entry_rows, entry_cols, rows_t, cols_t, *grads)
    returned = lax.all_to_all(packed, "tile", split_axis=0, concat_axis=0, tiled=True)
    density_grad = pl.pallas_call(
        scatter_kernel,
        out_shape=jax.ShapeDtypeStruct(density.shape, f32),
        in_specs=[SMEM, VMEM],
        out_specs=VMEM,
        compiler_params=params(),
    )(send, returned)
    return image, density_grad


def solution(mesh):
    return jax.shard_map(
        local,
        mesh=mesh,
        in_specs=(
            P(("slab", "tile"), None, None),
            P(("slab", "tile"), None, None),
            P(("slab", "tile"), None),
            P(("slab", "tile"), None),
            P(("slab", "tile"), None),
            P(("slab", "tile"), None),
            P(),
            P(),
            P("tile", None, None),
        ),
        out_specs=(P("tile", "slab", None), P(("slab", "tile"), None, None)),
        check_vma=False,
    )
```

time: 953 us -> 206 us (0.22); the launches traced: 939 us -> 206 us
  matrix products: 567 us -> 0 us
  local copies, waits for them, and re-layouts: 157 us -> 25.1 us
  waiting for transfers between devices: 173 us -> 75.8 us
  Pallas kernels: 0 us -> 60.3 us
  starting transfers between devices: 14.5 us -> 36.6 us
  between operations: 14.6 us -> 0.76 us
    dot_general x121 -> x0, matrix products: 567 us -> none  [the longest x25 276 us: add_rows(): jnp.dot(placer, values.reshape(values.shape[0], -1), precision=lax.Precis...]
    while x193 -> x0, local copies, waits for them, and re-layouts: 142 us -> none
    psum x1 -> x0, waiting for transfers between devices: 84.4 us -> none  [local(): image = lax.psum(partial_image, 'slab')]
    pallas_call x0 -> x5, Pallas kernels: none -> 60.3 us  [the longest x1 23.6 us: local(): pl.pallas_call(backward_kernel, out_shape=jax.ShapeDtypeStruct((peers, sl...]
    ppermute x0 -> x11, waiting for transfers between devices: none -> 28.9 us  [the longest x6 23.4 us: along(): return lax.ppermute(x, 'slab', [(i, (i + 2 * s) % 8) for i in range(8)])]
    all_to_all x1, waiting for transfers between devices: 58.3 us -> 33.8 us  [local(): lax.all_to_all(packed, 'tile', split_axis=0, concat_axis=0, tiled=True)]
    ppermute x0 -> x11, starting transfers between devices: none -> 24.4 us  [the longest x5 15.2 us: swap(): return lax.ppermute(x, 'slab', pair)]
    all_to_all x1, waiting for transfers between devices: 30.1 us -> 13 us  [local(): lax.all_to_all(outgoing, 'tile', split_axis=0, concat_axis=0, tiled=True)]
  transfers between devices with their start and end apart: 3 -> 13, of which waited for: 3 -> 7; matrix products, arithmetic and copies ran while one was open for 0% -> 12% of each run, Pallas kernels for 0% -> 0%
where the time goes in v1:
time: 206 us
  waiting for transfers between devices  75.8 us (37%)
  Pallas kernels  60.3 us (29%)
  starting transfers between devices  36.6 us (18%)
  local copies, waits for them, and re-layouts  25.1 us (12%)
  other arithmetic  7.17 us (3%)
    all_to_all x1, waiting for transfers between devices, local(): lax.all_to_all(packed, 'tile', split_axis=0, concat_axis=0, tiled=True)  33.8 us
    pallas_call x1, Pallas kernels, local(): pl.pallas_call(backward_kernel, out_shape=jax.ShapeDtypeStruct((peers, sl...  23.6 us
    pallas_call x1, Pallas kernels, local(): pl.pallas_call(forward_kernel, out_shape=(bands, bands), in_specs=[SMEM]...  23.6 us
    ppermute x6, waiting for transfers between devices, along(): return lax.ppermute(x, 'slab', [(i, (i + 2 * s) % 8) for i in range(8)])  23.4 us
    ppermute x5, starting transfers between devices, swap(): return lax.ppermute(x, 'slab', pair)  15.2 us
    all_to_all x1, waiting for transfers between devices, local(): lax.all_to_all(outgoing, 'tile', split_axis=0, concat_axis=0, tiled=True)  13 us
    gather x3, local copies, waits for them, and re-layouts, local(): jnp.take(rows_table.reshape(-1, 8, 16, 128), order, axis=1)  9.84 us
    ppermute x6, starting transfers between devices, along(): return lax.ppermute(x, 'slab', [(i, (i + 2 * s) % 8) for i in range(8)])  9.25 us
  transfers between devices with their start and end apart: 13, of which 7 were waited for; matrix products, arithmetic and copies ran while one was open for 12% of the time, Pallas kernels for 0%

profile of v1, /device:TPU:1, one launch (start us, length us, event | category | flops | bytes accessed | tf_op | source)
XLA Modules:
  0.0 205.7 jit_solution(18207801328702380384)
XLA Ops:
  0.6 0.0 copy-start
  0.6 0.8 compare_select_fusion
  1.5 0.1 copy.17
  1.6 0.1 reshape.134
  1.7 3.4 %gather_fusion.1 = bf16[64,128,128]{2,1,0:T(8,128)(2,1)} fusion(bf16[32,128,128]{2,1,0:T(8,128)(2,1)} %param.9, s32[1024]{0:T(1024)S(1)} %pad_clamp_fusion), kind=kCustom, calls=%fused_computation.1 | custom fusion | bytes 4194560 | tf_op jit(solution)/shard_map/gather | solution.py:159
  5.0 7.6 %all-to-all-start = ((bf16[16,4,128,128]{3,2,1,0:T(8,128)(2,1)}), bf16[16,4,128,128]{3,2,1,0:T(8,128)(2,1)}, u32[]{:S(2)}, u32[]{:S(2)}) async-start(bf16[16,4,128,128]{3,2,1,0:T(8,128)(2,1)} %bitcast.18), calls=%async_computation | async-start | bytes 4194304 | tf_op jit(solution)/shard_map/all_to_all | solution.py:160
  12.7 0.1 broadcast_add_fusion
  12.8 0.1 add.115
  12.9 0.1 add.113
  13.0 2.3 %gather_fusion = bf16[8,64,16,128]{3,2,1,0:T(8,128)(2,1)} fusion(bf16[64,8,16,128]{3,2,1,0:T(8,128)(2,1)S(1)} %bitcast.16, s32[1024]{0:T(1024)S(1)} %pad_clamp_fusion.1), kind=kCustom, calls=%fused_computation | custom fusion | bytes 4194336 | tf_op jit(solution)/shard_map/jit(_take)/gather | solution.py:147
  15.3 3.5 %copy.15 = bf16[64,8,16,128]{3,2,1,0:T(8,128)(2,1)} copy(bf16[64,8,16,128]{3,2,0,1:T(8,128)(2,1)} %bitcast.19) | data formatting | bytes 4194304 | tf_op jit(solution)/shard_map/jit(_take)/gather | solution.py:147
  18.8 4.1 %copy.16 = bf16[64,128,128]{1,2,0:T(8,128)(2,1)} copy(bf16[64,128,128]{2,1,0:T(8,128)(2,1)} %bitcast.20) | data formatting | bytes 4194304 | tf_op jit(solution)/shard_map/jit(_take)/gather | solution.py:147
  22.8 0.1 broadcast_in_dim.17
  22.9 0.1 broadcast_in_dim.18
  23.0 3.1 %broadcast_select_fusion = bf16[64,128,128]{1,2,0:T(8,128)(2,1)} fusion(bf16[64,128,128]{1,2,0:T(8,128)(2,1)} %copy.16, pred[128]{0:T(512)(128)(4,1)S(1)} %broadcast_in_dim.18), kind=kLoop, calls=%fused_computation.2 | loop fusion | flops 1048576 | bytes 4194432 | tf_op jit(solution)/shard_map/jit(_take)/select_n | solution.py:147
  26.1 4.1 %copy.18.rows = bf16[64,128,128]{2,1,0:T(8,128)(2,1)} copy(bf16[64,128,128]{1,2,0:T(8,128)(2,1)} %broadcast_select_fusion) | data formatting | bytes 4194304 | tf_op jit(solution)/shard_map/jit(_take)/select_n | solution.py:147
  30.2 13.0 %all-to-all-done = bf16[16,4,128,128]{3,2,1,0:T(8,128)(2,1)} async-done(((bf16[16,4,128,128]{3,2,1,0:T(8,128)(2,1)}), bf16[16,4,128,128]{3,2,1,0:T(8,128)(2,1)}, u32[]{:S(2)}, u32[]{:S(2)}) %all-to-all-start) | async-done | bytes 2097184 | tf_op jit(solution)/shard_map/all_to_all | solution.py:160
  43.2 23.6 %shard_map.104 = (f32[4,96,16,128]{3,2,1,0:T(8,128)}, f32[4,96,16,128]{3,2,1,0:T(8,128)}) custom-call(s32[1,768]{1,0:T(1,128)} %tile_ids.3, s32[1,768]{1,0:T(1,128)} %block_ids.3, s32[1,768]{1,0:T(1,128)} %row_ids.3, s32[1,768]{1,0:T(1,128)} %col_ids.3, bf16[64,128,128]{2,1,0:T(8,128)(2,1)} %copy.18.rows, bf16[64,128,128]{2,1,0:T(8,128)(2,1)} %cols.1, ...), custom_call_target="tpu_custom_call" | custom-call | tf_op jit(solution)/shard_map/pallas_call | solution.py:164
  66.8 2.1 %collective-permute-start = (f32[4,96,16,128]{3,2,1,0:T(8,128)}, f32[4,96,16,128]{3,2,1,0:T(8,128)S(1)}, u32[]{:S(2)}, u32[]{:S(2)}) collective-permute-start(f32[4,96,16,128]{3,2,1,0:T(8,128)} %get-tuple-element.11), channel_id=1, source_target_pairs={{0,16},{16,0},{32,48},{48,32},{64,80},{80,64},{96,112},{112,96},{1... | collective-permute-start | bytes 9437192 | tf_op jit(solution)/shard_map/ppermute | solution.py:154
  68.9 5.5 %collective-permute-done.got = f32[4,96,16,128]{3,2,1,0:T(8,128)S(1)} collective-permute-done((f32[4,96,16,128]{3,2,1,0:T(8,128)}, f32[4,96,16,128]{3,2,1,0:T(8,128)S(1)}, u32[]{:S(2)}, u32[]{:S(2)}) %collective-permute-start) | collective-permute-done | bytes 3145760 | tf_op jit(solution)/shard_map/ppermute | solution.py:154
  74.4 1.7 copy-done.1
  76.1 5.4 %shard_map.105 = (f32[96,16,128]{2,1,0:T(8,128)}, s16[102,16,128]{2,1,0:T(8,128)(2,1)}, s16[102,16,128]{2,1,0:T(8,128)(2,1)}, s16[102,16,128]{2,1,0:T(8,128)(2,1)}) custom-call(f32[4,96,16,128]{3,2,1,0:T(8,128)} %get-tuple-element.10.mine, f32[4,96,16,128]{3,2,1,0:T(8,128)} %copy-done.1), custom_call_target="tpu_custom_call" | custom-call | tf_op jit(solution)/shard_map/pallas_call | solution.py:173
  81.5 1.7 collective-permute-start.1
  83.2 3.3 %collective-permute-start.2 = (s16[102,16,128]{2,1,0:T(8,128)(2,1)}, s16[102,16,128]{2,1,0:T(8,128)(2,1)S(1)}, u32[]{:S(2)}, u32[]{:S(2)}) collective-permute-start(s16[102,16,128]{2,1,0:T(8,128)(2,1)} %get-tuple-element.14), channel_id=1, source_target_pairs={{0,64},{16,80},{32,96},{48,112},{64,0},{80,16},{96,32},{112,48},{1... | collective-permute-start | bytes 1253384 | tf_op jit(solution)/shard_map/ppermute | solution.py:157
  86.5 0.7 collective-permute-start.3
  87.2 8.0 %collective-permute-done.1.q1 = s16[102,16,128]{2,1,0:T(8,128)(2,1)S(1)} collective-permute-done((s16[102,16,128]{2,1,0:T(8,128)(2,1)}, s16[102,16,128]{2,1,0:T(8,128)(2,1)S(1)}, u32[]{:S(2)}, u32[]{:S(2)}) %collective-permute-start.1) | collective-permute-done | bytes 417824 | tf_op jit(solution)/shard_map/ppermute | solution.py:157
  95.2 9.8 %collective-permute-done.2.q2 = s16[102,16,128]{2,1,0:T(8,128)(2,1)S(1)} collective-permute-done((s16[102,16,128]{2,1,0:T(8,128)(2,1)}, s16[102,16,128]{2,1,0:T(8,128)(2,1)S(1)}, u32[]{:S(2)}, u32[]{:S(2)}) %collective-permute-start.2) | collective-permute-done | bytes 417824 | tf_op jit(solution)/shard_map/ppermute | solution.py:157
  105.1 0.0 collective-permute-done.3.q3
  105.1 0.8 copy-done.3
  105.8 0.1 copy-done.4
  106.0 3.8 %shard_map.106 = (f32[96,16,128]{2,1,0:T(8,128)}, bf16[96,16,128]{2,1,0:T(8,128)(2,1)}) custom-call(s32[1]{0:T(128)} %bitcast.place, f32[96,16,128]{2,1,0:T(8,128)} %get-tuple-element.12.own, s16[102,16,128]{2,1,0:T(8,128)(2,1)} %copy-done.2, s16[102,16,128]{2,1,0:T(8,128)(2,1)} %copy-done.3, s16[102,16,128]{2,1,0:T(8,128)(2,1)} %copy-done.4, ...), custom_call_target="tpu_custom_call" | custom-call | tf_op jit(solution)/shard_map/pallas_call | solution.py:183
  109.8 1.0 collective-permute-start.6
  110.8 1.7 collective-permute-start.4
  112.5 0.9 collective-permute-start.5
  113.3 1.8 collective-permute-start.7
  115.1 5.5 %collective-permute-done.6.rest_3_ = bf16[96,16,128]{2,1,0:T(8,128)(2,1)S(1)} collective-permute-done((bf16[96,16,128]{2,1,0:T(8,128)(2,1)}, bf16[96,16,128]{2,1,0:T(8,128)(2,1)S(1)}, u32[]{:S(2)}, u32[]{:S(2)}) %collective-permute-start.6) | collective-permute-done | bytes 393248 | tf_op jit(solution)/shard_map/ppermute | solution.py:157
  120.6 2.2 %collective-permute-start.10 = (bf16[96,16,128]{2,1,0:T(8,128)(2,1)S(1)}, bf16[96,16,128]{2,1,0:T(8,128)(2,1)}, u32[]{:S(2)}, u32[]{:S(2)}) collective-permute-start(bf16[96,16,128]{2,1,0:T(8,128)(2,1)S(1)} %collective-permute-done.6.rest_3_), channel_id=1, source_target_pairs={{0,16},{16,0},{32,48},{48,32},{64,80},{80,64},{96,112},{112,96},{1... | collective-permute-start | bytes 1179656 | tf_op jit(solution)/shard_map/ppermute | solution.py:154
  122.8 7.8 %collective-permute-start.8 = (bf16[96,16,128]{2,1,0:T(8,128)(2,1)S(1)}, bf16[96,16,128]{2,1,0:T(8,128)(2,1)}, u32[]{:S(2)}, u32[]{:S(2)}) collective-permute-start(bf16[96,16,128]{2,1,0:T(8,128)(2,1)S(1)} %collective-permute-done.4.rest_1_), channel_id=1, source_target_pairs={{0,16},{16,0},{32,48},{48,32},{64,80},{80,64},{96,112},{112,96},{1... | collective-permute-start | bytes 1179656 | tf_op jit(solution)/shard_map/ppermute | solution.py:154
  130.6 0.1 collective-permute-done.5.rest_2_
  130.7 1.3 collective-permute-start.9
  132.0 4.1 %copy.19 = bf16[64,128,128]{1,2,0:T(8,128)(2,1)} copy(bf16[64,128,128]{2,1,0:T(8,128)(2,1)} %cols.1) | data formatting | bytes 4194304 | tf_op args[7]
  136.1 3.1 %fusion.4.rows_t = bf16[64,128,128]{2,1,0:T(8,128)(2,1)} fusion(bf16[64,128,128]{1,2,0:T(8,128)(2,1)} %copy.16, pred[128]{0:T(512)(128)(4,1)S(1)} %broadcast_in_dim.18), kind=kLoop, calls=%fused_computation.20 | loop fusion | flops 1048576 | bytes 4194432 | tf_op jit(solution)/shard_map/transpose | solution.py:148
  139.2 0.0 collective-permute-done.8.rest_5_
  139.3 23.6 %shard_map.107 = s16[16,528,128]{2,1,0:T(8,128)(2,1)} custom-call(s32[1,768]{1,0:T(1,128)} %tile_ids.3, s32[1,768]{1,0:T(1,128)} %block_ids.3, s32[1,768]{1,0:T(1,128)} %row_ids.3, s32[1,768]{1,0:T(1,128)} %col_ids.3, bf16[64,128,128]{2,1,0:T(8,128)(2,1)} %fusion.4.rows_t, bf16[64,128,128]{2,1,0:T(8,128)(2,1)} %bitcast.17, ...), custom_call_target="tpu_custom_call" | custom-call | tf_op jit(solution)/shard_map/pallas_call | solution.py:196
  162.9 4.6 %all-to-all-start.1 = ((s16[16,528,128]{2,1,0:T(8,128)(2,1)}), s16[16,528,128]{2,1,0:T(8,128)(2,1)}, u32[]{:S(2)}, u32[]{:S(2)}) async-start(s16[16,528,128]{2,1,0:T(8,128)(2,1)} %shard_map.107), calls=%async_computation.1 | async-start | bytes 4325376 | tf_op jit(solution)/shard_map/all_to_all | solution.py:204
  167.5 0.7 copy.20.send
  168.1 33.8 %all-to-all-done.1.coded = s16[16,528,128]{2,1,0:T(8,128)(2,1)} async-done(((s16[16,528,128]{2,1,0:T(8,128)(2,1)}), s16[16,528,128]{2,1,0:T(8,128)(2,1)}, u32[]{:S(2)}, u32[]{:S(2)}) %all-to-all-start.1) | async-done | bytes 2162720 | tf_op jit(solution)/shard_map/all_to_all | solution.py:204
  201.9 3.8 %shard_map.108 = f32[32,128,128]{2,1,0:T(8,128)} custom-call(s32[16,4]{1,0:T(8,128)} %copy.20.send, s16[16,528,128]{2,1,0:T(8,128)(2,1)} %all-to-all-done.1.coded), custom_call_target="tpu_custom_call" | custom-call | tf_op jit(solution)/shard_map/pallas_call | solution.py:205
  (24 shorter events, 0.1 us)
Async XLA Ops:
  0.6 12.4 %copy-start = (bf16[64,128,128]{2,1,0:T(8,128)(2,1)S(1)}, bf16[64,128,128]{2,1,0:T(8,128)(2,1)}, u32[]{:S(2)}) copy-start(bf16[64,128,128]{2,1,0:T(8,128)(2,1)} %param.15) | copy-start | bytes 6291460
  5.0 38.2 %all-to-all-start = ((bf16[16,4,128,128]{3,2,1,0:T(8,128)(2,1)}), bf16[16,4,128,128]{3,2,1,0:T(8,128)(2,1)}, u32[]{:S(2)}, u32[]{:S(2)}) async-start(bf16[16,4,128,128]{3,2,1,0:T(8,128)(2,1)} %bitcast.18), calls=%async_computation | async-start | bytes 4194304 | tf_op jit(solution)/shard_map/all_to_all | solution.py:160
  66.8 7.6 %collective-permute-start = (f32[4,96,16,128]{3,2,1,0:T(8,128)}, f32[4,96,16,128]{3,2,1,0:T(8,128)S(1)}, u32[]{:S(2)}, u32[]{:S(2)}) collective-permute-start(f32[4,96,16,128]{3,2,1,0:T(8,128)} %get-tuple-element.11), channel_id=1, source_target_pairs={{0,16},{16,0},{32,48},{48,32},{64,80},{80,64},{96,112},{112,96},{1... | collective-permute-start | bytes 9437192 | tf_op jit(solution)/shard_map/ppermute | solution.py:154
  74.4 1.7 copy-start.1
  81.5 13.7 %collective-permute-start.1 = (s16[102,16,128]{2,1,0:T(8,128)(2,1)}, s16[102,16,128]{2,1,0:T(8,128)(2,1)S(1)}, u32[]{:S(2)}, u32[]{:S(2)}) collective-permute-start(s16[102,16,128]{2,1,0:T(8,128)(2,1)} %get-tuple-element.13), channel_id=1, source_target_pairs={{0,32},{16,48},{32,64},{48,80},{64,96},{80,112},{96,0},{112,16},{1... | collective-permute-start | bytes 1253384 | tf_op jit(solution)/shard_map/ppermute | solution.py:157
  83.2 21.8 %collective-permute-start.2 = (s16[102,16,128]{2,1,0:T(8,128)(2,1)}, s16[102,16,128]{2,1,0:T(8,128)(2,1)S(1)}, u32[]{:S(2)}, u32[]{:S(2)}) collective-permute-start(s16[102,16,128]{2,1,0:T(8,128)(2,1)} %get-tuple-element.14), channel_id=1, source_target_pairs={{0,64},{16,80},{32,96},{48,112},{64,0},{80,16},{96,32},{112,48},{1... | collective-permute-start | bytes 1253384 | tf_op jit(solution)/shard_map/ppermute | solution.py:157
  86.5 18.6 %collective-permute-start.3 = (s16[102,16,128]{2,1,0:T(8,128)(2,1)}, s16[102,16,128]{2,1,0:T(8,128)(2,1)S(1)}, u32[]{:S(2)}, u32[]{:S(2)}) collective-permute-start(s16[102,16,128]{2,1,0:T(8,128)(2,1)} %get-tuple-element.15), channel_id=1, source_target_pairs={{0,96},{16,112},{32,0},{48,16},{64,32},{80,48},{96,64},{112,80},{1... | collective-permute-start | bytes 1253384 | tf_op jit(solution)/shard_map/ppermute | solution.py:157
  95.2 9.8 %copy-start.2 = (s16[102,16,128]{2,1,0:T(8,128)(2,1)}, s16[102,16,128]{2,1,0:T(8,128)(2,1)S(1)}, u32[]{:S(2)}) copy-start(s16[102,16,128]{2,1,0:T(8,128)(2,1)S(1)} %collective-permute-done.1.q1) | copy-start | bytes 1253380
  105.1 0.8 copy-start.3
  105.1 0.9 copy-start.4
  109.8 10.8 %collective-permute-start.6 = (bf16[96,16,128]{2,1,0:T(8,128)(2,1)}, bf16[96,16,128]{2,1,0:T(8,128)(2,1)S(1)}, u32[]{:S(2)}, u32[]{:S(2)}) collective-permute-start(bf16[96,16,128]{2,1,0:T(8,128)(2,1)} %get-tuple-element.17.rest_0_), channel_id=1, source_target_pairs={{0,32},{16,48},{32,64},{48,80},{64,96},{80,112},{96,0},{112,16},{1... | collective-permute-start | bytes 1179656 | tf_op jit(solution)/shard_map/ppermute | solution.py:157
  110.8 12.1 %collective-permute-start.4 = (bf16[96,16,128]{2,1,0:T(8,128)(2,1)}, bf16[96,16,128]{2,1,0:T(8,128)(2,1)S(1)}, u32[]{:S(2)}, u32[]{:S(2)}) collective-permute-start(bf16[96,16,128]{2,1,0:T(8,128)(2,1)} %get-tuple-element.17.rest_0_), channel_id=1, source_target_pairs={{0,96},{16,112},{32,0},{48,16},{64,32},{80,48},{96,64},{112,80},{1... | collective-permute-start | bytes 1179656 | tf_op jit(solution)/shard_map/ppermute | solution.py:157
  112.5 18.2 %collective-permute-start.5 = (bf16[96,16,128]{2,1,0:T(8,128)(2,1)}, bf16[96,16,128]{2,1,0:T(8,128)(2,1)S(1)}, u32[]{:S(2)}, u32[]{:S(2)}) collective-permute-start(bf16[96,16,128]{2,1,0:T(8,128)(2,1)} %get-tuple-element.17.rest_0_), channel_id=1, source_target_pairs={{0,64},{16,80},{32,96},{48,112},{64,0},{80,16},{96,32},{112,48},{1... | collective-permute-start | bytes 1179656 | tf_op jit(solution)/shard_map/ppermute | solution.py:157
  113.3 25.9 %collective-permute-start.7 = (bf16[96,16,128]{2,1,0:T(8,128)(2,1)}, bf16[96,16,128]{2,1,0:T(8,128)(2,1)}, u32[]{:S(2)}, u32[]{:S(2)}) collective-permute-start(bf16[96,16,128]{2,1,0:T(8,128)(2,1)} %get-tuple-element.17.rest_0_), channel_id=1, source_target_pairs={{0,16},{16,0},{32,48},{48,32},{64,80},{80,64},{96,112},{112,96},{1... | collective-permute-start | bytes 1179656 | tf_op jit(solution)/shard_map/ppermute | solution.py:154
  120.6 15.5 %copy-start.5 = (bf16[96,16,128]{2,1,0:T(8,128)(2,1)}, bf16[96,16,128]{2,1,0:T(8,128)(2,1)S(1)}, u32[]{:S(2)}) copy-start(bf16[96,16,128]{2,1,0:T(8,128)(2,1)S(1)} %collective-permute-done.6.rest_3_) | copy-start | bytes 1179652
  120.6 18.6 %collective-permute-start.10 = (bf16[96,16,128]{2,1,0:T(8,128)(2,1)S(1)}, bf16[96,16,128]{2,1,0:T(8,128)(2,1)}, u32[]{:S(2)}, u32[]{:S(2)}) collective-permute-start(bf16[96,16,128]{2,1,0:T(8,128)(2,1)S(1)} %collective-permute-done.6.rest_3_), channel_id=1, source_target_pairs={{0,16},{16,0},{32,48},{48,32},{64,80},{80,64},{96,112},{112,96},{1... | collective-permute-start | bytes 1179656 | tf_op jit(solution)/shard_map/ppermute | solution.py:154
  122.8 13.3 %copy-start.6 = (bf16[96,16,128]{2,1,0:T(8,128)(2,1)}, bf16[96,16,128]{2,1,0:T(8,128)(2,1)S(1)}, u32[]{:S(2)}) copy-start(bf16[96,16,128]{2,1,0:T(8,128)(2,1)S(1)} %collective-permute-done.4.rest_1_) | copy-start | bytes 1179652
  122.8 16.4 %collective-permute-start.8 = (bf16[96,16,128]{2,1,0:T(8,128)(2,1)S(1)}, bf16[96,16,128]{2,1,0:T(8,128)(2,1)}, u32[]{:S(2)}, u32[]{:S(2)}) collective-permute-start(bf16[96,16,128]{2,1,0:T(8,128)(2,1)S(1)} %collective-permute-done.4.rest_1_), channel_id=1, source_target_pairs={{0,16},{16,0},{32,48},{48,32},{64,80},{80,64},{96,112},{112,96},{1... | collective-permute-start | bytes 1179656 | tf_op jit(solution)/shard_map/ppermute | solution.py:154
  130.7 5.4 %copy-start.7 = (bf16[96,16,128]{2,1,0:T(8,128)(2,1)}, bf16[96,16,128]{2,1,0:T(8,128)(2,1)S(1)}, u32[]{:S(2)}) copy-start(bf16[96,16,128]{2,1,0:T(8,128)(2,1)S(1)} %collective-permute-done.5.rest_2_) | copy-start | bytes 1179652
  130.7 8.6 %collective-permute-start.9 = (bf16[96,16,128]{2,1,0:T(8,128)(2,1)S(1)}, bf16[96,16,128]{2,1,0:T(8,128)(2,1)}, u32[]{:S(2)}, u32[]{:S(2)}) collective-permute-start(bf16[96,16,128]{2,1,0:T(8,128)(2,1)S(1)} %collective-permute-done.5.rest_2_), channel_id=1, source_target_pairs={{0,16},{16,0},{32,48},{48,32},{64,80},{80,64},{96,112},{112,96},{1... | collective-permute-start | bytes 1179656 | tf_op jit(solution)/shard_map/ppermute | solution.py:154
  162.9 4.6 %copy-start.8 = (s32[1,16,4]{1,2,0:T(4,128)S(1)}, s32[1,16,4]{1,2,0:T(4,128)}, u32[]{:S(2)}) copy-start(s32[1,16,4]{1,2,0:T(4,128)} %param.10) | copy-start | bytes 772
  162.9 39.0 %all-to-all-start.1 = ((s16[16,528,128]{2,1,0:T(8,128)(2,1)}), s16[16,528,128]{2,1,0:T(8,128)(2,1)}, u32[]{:S(2)}, u32[]{:S(2)}) async-start(s16[16,528,128]{2,1,0:T(8,128)(2,1)} %shard_map.107), calls=%async_computation.1 | async-start | bytes 4325376 | tf_op jit(solution)/shard_map/all_to_all | solution.py:204

commit v2 on v1

v2 whole, which is shorter than its diff:
```python
import functools
import jax
import jax.numpy as jnp
from jax import lax
from jax.experimental import pallas as pl
from jax.experimental.pallas import tpu as pltpu
from jax.sharding import PartitionSpec as P

bf16, f32, i16, i32 = jnp.bfloat16, jnp.float32, jnp.int16, jnp.int32
unroll = 32
groups = 2
top = 32000.0
tiny = 1e-30

SMEM = pl.BlockSpec(memory_space=pltpu.SMEM)
VMEM = pl.BlockSpec(memory_space=pltpu.VMEM)
ANY = pl.BlockSpec(memory_space=pl.ANY)


def params(mib):
    return pltpu.CompilerParams(vmem_limit_bytes=mib * 2**20)


def cost(us):
    return pl.CostEstimate(flops=int(us * 1e10), bytes_accessed=int(us * 3e7), transcendentals=0)


def mm(a, b):
    return jnp.dot(a, b, preferred_element_type=f32)


def code_level(peak):
    return jnp.ceil(8.0 * jnp.log2(jnp.maximum(peak, tiny)))


def gather_kernel(send, density, out):
    for k in range(out.shape[0]):
        for s in range(out.shape[1]):
            out[k, s] = density[send[0, k, s]]


def prepare_kernel(bands, tile_ids, block_ids, row_ids, col_ids, rows_table, cols_table,
                   lists, counts, rows, rows_t, cols_t, *, per):
    count = rows_table.shape[0]
    entries = tile_ids.shape[1]
    stride = lists.shape[1] // groups
    for g in range(groups):
        counts[g] = 0

    def bin_step(i, carry):
        for u in range(16):
            e = i * 16 + u
            tile = tile_ids[0, e]
            g = jnp.int32(0)
            for h in range(1, groups):
                g = g + (tile >= h * per).astype(i32)
            word = (tile - g * per) | (block_ids[0, e] << 7) | (row_ids[0, e] << 13) | (col_ids[0, e] << 20)
            at = counts[g]
            lists[0, g * stride + at] = word
            counts[g] = at + 1
        return carry

    lax.fori_loop(0, entries // 16, bin_step, 0)
    for g in range(groups):
        at = counts[g]

        def pad_step(i, carry):
            lists[0, g * stride + at + i] = jnp.int32(count << 13)
            return carry

        lax.fori_loop(0, unroll, pad_step, 0)

    def table_step(i, carry):
        for u in range(4):
            r = i * 4 + u
            for k in range(8):
                rows[r, k * 16:(k + 1) * 16] = rows_table[r, pl.ds(pl.multiple_of(bands[k] * 16, 16), 16)]
            cols_t[r] = cols_table[r].T
        for u in range(4):
            r = i * 4 + u
            rows_t[r] = rows[r].T
        return carry

    lax.fori_loop(0, count // 4, table_step, 0)
    rows[count] = jnp.zeros(rows.shape[1:], bf16)
    rows_t[count] = jnp.zeros(rows_t.shape[1:], bf16)


def unpack(word):
    return word & 127, (word >> 7) & 63, (word >> 13) & 127, word >> 20


def run_steps(count, step):
    short = (count + unroll - 1) // unroll
    double = short // 2
    lax.fori_loop(0, double, functools.partial(step, width=2 * unroll, first=0), 0)
    lax.fori_loop(0, short - 2 * double, functools.partial(step, width=unroll, first=double * 2 * unroll), 0)


def forward_kernel(lists, counts, rows, cols, blocks, *rest, g):
    mine, theirs = rest[-2:]
    mine[...] = jnp.zeros_like(mine)
    theirs[...] = jnp.zeros_like(theirs)
    base = g * (lists.shape[1] // groups)

    def step(i, carry, width, first):
        items = [unpack(lists[0, base + first + i * width + u]) for u in range(width)]
        half = [mm(rows[r], blocks[b]).astype(bf16) for _, b, r, _ in items]
        parts = [mm(h, cols[c]) for h, (_, _, _, c) in zip(half, items)]
        for part, (t, _, _, _) in zip(parts, items):
            for k in range(4):
                mine[k, t] += part[k * 16:(k + 1) * 16]
                theirs[k, t] += part[64 + k * 16:64 + (k + 1) * 16]
        return carry

    run_steps(counts[g], step)


def combine_kernel(mine, got, *rest):
    own, q1, q2, q3 = rest[-4:]
    own[...] = mine[0] + got[0]
    n = own.shape[0]
    for k, q in ((1, q1), (2, q2), (3, q3)):
        def group(g, carry):
            levels = []
            for s in range(16):
                t = g * 16 + s
                v = mine[k, t] + got[k, t]
                level = code_level(jnp.max(v, axis=0, keepdims=True))
                scale = jnp.exp2(level * -0.125) * (2.0 * top)
                q[t] = jnp.round(v * scale - top).astype(i32).astype(i16)
                levels.append(level)
            q[n + g] = jnp.concatenate(levels, 0).astype(i32).astype(i16)
            return carry
        lax.fori_loop(0, n // 16, group, 0)


def slope_kernel(place, own, q1, q2, q3, target, *rest):
    image, grad = rest[-2:]
    n = own.shape[0]

    def group(g, carry):
        steps = [jnp.exp2(q[n + g].astype(i32).astype(f32) * 0.125) * (0.5 / top) for q in (q1, q2, q3)]
        for s in range(16):
            t = g * 16 + s
            v = own[t]
            for q, step in zip((q1, q2, q3), steps):
                v = v + (q[t].astype(i32).astype(f32) + top) * step[s:s + 1]
            image[t] = v
            grad[t] = ((jnp.log1p(v) - jnp.log1p(target[t])) / (1.0 + v)).astype(bf16)
        return carry

    lax.fori_loop(0, n // 16, group, 0)


def backward_kernel(lists, counts, rows_t, cols_t, *rest, g):
    grads, rest = rest[:8], rest[8:]
    if g:
        rest[-1][...] = rest[0][...]
    else:
        rest[-1][...] = jnp.zeros_like(rest[-1])
    acc = rest[-1]
    base = g * (lists.shape[1] // groups)

    def step(i, carry, width, first):
        items = [unpack(lists[0, base + first + i * width + u]) for u in range(width)]
        back = [
            mm(jnp.concatenate([band[t] for band in grads], 0), cols_t[c]).astype(bf16)
            for t, _, _, c in items
        ]
        parts = [mm(rows_t[r], h) for h, (_, _, r, _) in zip(back, items)]
        for part, (_, b, _, _) in zip(parts, items):
            acc[b] += part
        return carry

    run_steps(counts[g], step)
    if g == groups - 1:
        pack_slots(acc, rest[-2])


def pack_slots(acc, out):
    slots = (out.shape[1] - 16) // 128

    def pack(k, carry):
        levels = []
        for s in range(slots):
            v = acc[k * slots + s]
            level = code_level(jnp.max(jnp.abs(v), axis=0, keepdims=True))
            scale = jnp.exp2(level * -0.125) * top
            out[k, s * 128:(s + 1) * 128] = jnp.round(v * scale).astype(i32).astype(i16)
            levels.append(level)
        levels.append(jnp.zeros((16 - slots, 128), f32))
        out[k, slots * 128:slots * 128 + 16] = jnp.concatenate(levels, 0).astype(i32).astype(i16)
        return carry

    lax.fori_loop(0, out.shape[0], pack, 0)


def scatter_kernel(send, coded, out):
    out[...] = jnp.zeros_like(out)
    slots = (coded.shape[1] - 16) // 128

    def step(k, carry):
        steps = jnp.exp2(coded[k, slots * 128:slots * 128 + 16].astype(i32).astype(f32) * 0.125) * (1.0 / top)
        for s in range(slots):
            v = coded[k, s * 128:(s + 1) * 128].astype(i32).astype(f32) * steps[s:s + 1]
            out[send[0, k, s]] += v
        return carry

    lax.fori_loop(0, coded.shape[0], step, 0)


def local(density, send_list, entry_tile, entry_block, entry_rows, entry_cols, rows_table, cols_table, target):
    tiles = target.shape[0]
    send = send_list
    peers, slots = send.shape[1:]
    me = lax.axis_index("slab")
    depth, core = me // 2, me % 2
    order = ((depth + jnp.arange(4)) % 4)[None, :] * 2 + (core + jnp.arange(2))[:, None] % 2
    order = order.reshape(-1).astype(i32)
    per = tiles // groups

    pair = [(i, i ^ 1) for i in range(8)]

    def swap(x):
        return lax.ppermute(x, "slab", pair)

    def along(x, s):
        return lax.ppermute(x, "slab", [(i, (i + 2 * s) % 8) for i in range(8)])

    outgoing = pl.pallas_call(
        gather_kernel,
        out_shape=jax.ShapeDtypeStruct((peers, slots, 128, 128), bf16),
        in_specs=[SMEM, VMEM],
        out_specs=VMEM,
        compiler_params=params(8),
        cost_estimate=cost(2),
    )(send, density)
    blocks = lax.all_to_all(outgoing, "tile", split_axis=0, concat_axis=0, tiled=True)
    blocks = blocks.reshape(peers * slots, 128, 128)

    table = jax.ShapeDtypeStruct((rows_table.shape[0] + 1, 128, 128), bf16)
    lists, counts, rows, rows_t, cols_t = pl.pallas_call(
        functools.partial(prepare_kernel, per=per),
        out_shape=(
            jax.ShapeDtypeStruct((1, groups * (entry_tile.shape[1] + 128)), i32),
            jax.ShapeDtypeStruct((groups,), i32),
            table,
            table,
            jax.ShapeDtypeStruct(cols_table.shape, bf16),
        ),
        in_specs=[SMEM] * 5 + [VMEM] * 2,
        out_specs=(SMEM, SMEM, VMEM, VMEM, VMEM),
        compiler_params=params(16),
        cost_estimate=cost(15),
    )(order, entry_tile, entry_block, entry_rows, entry_cols, rows_table, cols_table)

    bands = jax.ShapeDtypeStruct((4, per, 16, 128), f32)
    coded = jax.ShapeDtypeStruct((per + per // 16, 16, 128), i16)
    band = pl.BlockSpec((per, 16, 128), lambda i, place: (0, 0, 0))
    code = pl.BlockSpec(coded.shape, lambda i, place: (0, 0, 0))

    def forward(g, after):
        mine, theirs = pl.pallas_call(
            functools.partial(forward_kernel, g=g),
            out_shape=(bands, bands),
            in_specs=[SMEM] * 2 + [VMEM] * 3 + [ANY] * len(after),
            out_specs=(VMEM, VMEM),
            compiler_params=params(16),
            cost_estimate=cost(20 / groups),
        )(lists, counts, rows, cols_table, blocks, *after)
        return mine, swap(theirs)

    def combine(mine, got, after):
        return pl.pallas_call(
            combine_kernel,
            out_shape=(jax.ShapeDtypeStruct((per, 16, 128), f32), coded, coded, coded),
            in_specs=[VMEM] * 2 + [ANY] * len(after),
            out_specs=(VMEM,) * 4,
            compiler_params=params(16),
            cost_estimate=cost(2 / groups),
        )(mine, got, *after)

    def slope(g, part, held):
        return pl.pallas_call(
            slope_kernel,
            out_shape=(jax.ShapeDtypeStruct((tiles, 16, 128), f32), jax.ShapeDtypeStruct((per, 16, 128), bf16)),
            grid_spec=pltpu.PrefetchScalarGridSpec(
                num_scalar_prefetch=1,
                grid=(1,),
                in_specs=[band, code, code, code, pl.BlockSpec((per, 16, 128), lambda i, place, g=g: (g, place[0], 0))]
                + [ANY] * len(held),
                out_specs=(pl.BlockSpec((per, 16, 128), lambda i, place, g=g: (g, 0, 0)), band),
            ),
            input_output_aliases={6: 0} if held else {},
            compiler_params=params(16),
            cost_estimate=cost(3 / groups),
        )(me.reshape(1).astype(i32), *part, target, *held)

    image, token = [], []
    parts, grads = [], []

    def finish(part):
        nonlocal image, token
        picture, grad = slope(len(grads), part, image)
        image, token = [picture], [grad]
        grads.append((grad, along(grad, 3), along(grad, 1), along(grad, 2)))

    for g in range(groups):
        mine, got = forward(g, token)
        if g:
            finish(parts[g - 1])
        own, q1, q2, q3 = combine(mine, got, token if g else [])
        token = [own]
        parts.append((own, along(q1, 1), along(q3, 3), along(q2, 2)))
    finish(parts[-1])
    image = image[0]
    acc = None
    slot_sums = jax.ShapeDtypeStruct((peers * slots, 128, 128), f32)
    packed_shape = jax.ShapeDtypeStruct((peers, slots * 128 + 16, 128), i16)
    for g in range(groups):
        last = g == groups - 1
        near = grads[g]
        if g:
            near, acc = lax.optimization_barrier((near, acc))
        near = [near[0], near[1], near[3], near[2]]
        near = near + [swap(x) for x in near]
        acc = pl.pallas_call(
            functools.partial(backward_kernel, g=g),
            out_shape=packed_shape if last else slot_sums,
            in_specs=[SMEM] * 2 + [VMEM] * (11 if g else 10) + [ANY] * (0 if g else 1),
            out_specs=VMEM,
            scratch_shapes=[pltpu.VMEM(slot_sums.shape, f32)] if last else [],
            compiler_params=params(24),
            cost_estimate=cost(20 / groups),
        )(lists, counts, rows_t, cols_t, *near, *([acc] if g else token))
    returned = lax.all_to_all(acc, "tile", split_axis=0, concat_axis=0, tiled=True)
    density_grad = pl.pallas_call(
        scatter_kernel,
        out_shape=jax.ShapeDtypeStruct(density.shape, f32),
        in_specs=[SMEM, VMEM],
        out_specs=VMEM,
        compiler_params=params(8),
        cost_estimate=cost(4),
    )(send, returned)
    return image, density_grad


def solution(mesh):
    return jax.shard_map(
        local,
        mesh=mesh,
        in_specs=(
            P(("slab", "tile"), None, None),
            P(("slab", "tile"), None, None),
            P(("slab", "tile"), None),
            P(("slab", "tile"), None),
            P(("slab", "tile"), None),
            P(("slab", "tile"), None),
            P(),
            P(),
            P("tile", None, None),
        ),
        out_specs=(P("tile", "slab", None), P(("slab", "tile"), None, None)),
        check_vma=False,
    )
```

time: 206 us -> 171 us (0.83)
  waiting for transfers between devices: 75.8 us -> 33.5 us
  blocking collectives: 0 us -> 32.1 us
  local copies, waits for them, and re-layouts: 25.1 us -> 11 us
  other arithmetic: 7.17 us -> 0.09 us
  starting transfers between devices: 36.6 us -> 32.4 us
    all_to_all x1 -> x0, waiting for transfers between devices: 33.8 us -> none  [local(): lax.all_to_all(packed, 'tile', split_axis=0, concat_axis=0, tiled=True)]
    all_to_all x0 -> x1, blocking collectives: none -> 32.1 us  [local(): lax.all_to_all(acc, 'tile', split_axis=0, concat_axis=0, tiled=True)]
    gather x4 -> x0, local copies, waits for them, and re-layouts: 13.2 us -> none  [the longest x3 9.84 us: local(): jnp.take(rows_table.reshape(-1, 8, 16, 128), order, axis=1)]
    ppermute x6 -> x12, waiting for transfers between devices: 23.4 us -> 12.5 us  [along(): return lax.ppermute(x, 'slab', [(i, (i + 2 * s) % 8) for i in range(8)])]
    ppermute x6 -> x12, starting transfers between devices: 9.25 us -> 16.7 us  [along(): return lax.ppermute(x, 'slab', [(i, (i + 2 * s) % 8) for i in range(8)])]
    ppermute x5 -> x10, starting transfers between devices: 15.2 us -> 7.93 us  [swap(): return lax.ppermute(x, 'slab', pair)]
    all_to_all x1 -> x0, starting transfers between devices: 4.56 us -> none  [local(): lax.all_to_all(packed, 'tile', split_axis=0, concat_axis=0, tiled=True)]
    select_n x3 -> x0, local copies, waits for them, and re-layouts: 4.27 us -> none  [the longest x1 4.09 us: local(): jnp.take(rows_table.reshape(-1, 8, 16, 128), order, axis=1)]
  transfers between devices with their start and end apart: 13 -> 23, of which waited for: 7 -> 8; matrix products, arithmetic and copies ran while one was open for 12% -> 0% of each run, Pallas kernels for 0% -> 19%
where the time goes in v2:
time: 171 us; the launch traced here: 170 us
  Pallas kernels  60.3 us (35%)
  waiting for transfers between devices  33.5 us (20%)
  starting transfers between devices  32.4 us (19%)
  blocking collectives  32.1 us (19%)
  local copies, waits for them, and re-layouts  11 us (6%)
    all_to_all x1, blocking collectives, local(): lax.all_to_all(acc, 'tile', split_axis=0, concat_axis=0, tiled=True)  32.1 us
    pallas_call x2, Pallas kernels, forward(): pl.pallas_call(functools.partial(forward_kernel, g=g), out_shape=(bands,...  21.9 us
    pallas_call x2, Pallas kernels, local(): pl.pallas_call(functools.partial(backward_kernel, g=g), out_shape=packed_...  20.4 us
    ppermute x12, starting transfers between devices, along(): return lax.ppermute(x, 'slab', [(i, (i + 2 * s) % 8) for i in range(8)])  16.7 us
    all_to_all x1, waiting for transfers between devices, local(): lax.all_to_all(outgoing, 'tile', split_axis=0, concat_axis=0, tiled=True)  15.6 us
    ppermute x12, waiting for transfers between devices, along(): return lax.ppermute(x, 'slab', [(i, (i + 2 * s) % 8) for i in range(8)])  12.5 us
    unnamed x35, local copies, waits for them, and re-layouts  10.9 us
    pallas_call x1, Pallas kernels, local(): pl.pallas_call(functools.partial(prepare_kernel, per=per), out_shape=(jax...  9.02 us
  transfers between devices with their start and end apart: 23, of which 8 were waited for; matrix products, arithmetic and copies ran while one was open for 0% of the time, Pallas kernels for 19%

profile of v2, /device:TPU:1, one launch (start us, length us, event | category | flops | bytes accessed | tf_op | source)
XLA Modules:
  0.0 170.3 jit_solution(16607946417999657178)
XLA Ops:
  0.6 0.8 copy.12.send
  1.4 1.2 copy-done.4
  2.6 2.1 %shard_map.105 = bf16[16,4,128,128]{3,2,1,0:T(8,128)(2,1)} custom-call(s32[1,16,4]{2,1,0:T(8,128)S(1)} %copy.12.send, bf16[32,128,128]{2,1,0:T(8,128)(2,1)S(1)} %copy-done.4), custom_call_target="tpu_custom_call" | custom-call | flops 20000000000 | bytes 60000000 | tf_op jit(solution)/shard_map/pallas_call | solution.py:231
  4.8 7.8 %all-to-all-start = ((bf16[16,4,128,128]{3,2,1,0:T(8,128)(2,1)}), bf16[16,4,128,128]{3,2,1,0:T(8,128)(2,1)}, u32[]{:S(2)}, u32[]{:S(2)}) async-start(bf16[16,4,128,128]{3,2,1,0:T(8,128)(2,1)} %shard_map.105), calls=%async_computation | async-start | bytes 4194304 | tf_op jit(solution)/shard_map/all_to_all | solution.py:239
  12.8 1.6 copy-done.1
  14.4 9.0 %shard_map.104 = (s32[1,1792]{1,0:T(1,128)S(1)}, s32[2]{0:T(128)S(1)}, bf16[65,128,128]{2,1,0:T(8,128)(2,1)S(1)}, bf16[65,128,128]{2,1,0:T(8,128)(2,1)S(1)}, bf16[64,128,128]{2,1,0:T(8,128)(2,1)S(1)}) custom-call(s32[8]{0:T(128)S(1)} %add.73.bands, s32[1,768]{1,0:T(1,128)S(1)} %copy-done.5, s32[1,768]{1,0:T(1,128)S(1)} %copy-done.6, s32[1,768]{1,0:T(1,128)S(1)} %copy-done.7, ...), custom_call_target="tpu_custom_call" | custom-call | flops 149999992832 | bytes 450000000 | tf_op jit(solution)/shard_map/pallas_call | solution.py:243
  23.4 1.3 copy-done.9
  24.8 1.4 copy-done.11
  26.2 1.4 copy-done.13
  27.5 15.6 %all-to-all-done = bf16[16,4,128,128]{3,2,1,0:T(8,128)(2,1)} async-done(((bf16[16,4,128,128]{3,2,1,0:T(8,128)(2,1)}), bf16[16,4,128,128]{3,2,1,0:T(8,128)(2,1)}, u32[]{:S(2)}, u32[]{:S(2)}) %all-to-all-start) | async-done | bytes 2097184 | tf_op jit(solution)/shard_map/all_to_all | solution.py:239
  43.1 1.6 copy-done.2
  44.7 1.6 copy-done.14
  46.3 11.1 %shard_map.106 = (f32[4,48,16,128]{3,2,1,0:T(8,128)S(1)}, f32[4,48,16,128]{3,2,1,0:T(8,128)S(1)}) custom-call(s32[1,1792]{1,0:T(1,128)S(1)} %get-tuple-element.28.lists, s32[2]{0:T(128)S(1)} %get-tuple-element.29.counts, bf16[65,128,128]{2,1,0:T(8,128)(2,1)S(1)} %copy-done.14, bf16[64,128,128]{2,1,0:T(8,128)(2,1)S(1)} %copy-done.2, ...), custom_call_target="tpu_custom_call" | custom-call | flops 99999997952 | bytes 300000000 | tf_op jit(solution)/shard_map/pallas_call | solution.py:264
  57.4 2.2 %collective-permute-start = (f32[4,48,16,128]{3,2,1,0:T(8,128)S(1)}, f32[4,48,16,128]{3,2,1,0:T(8,128)S(1)}, u32[]{:S(2)}, u32[]{:S(2)}) collective-permute-start(f32[4,48,16,128]{3,2,1,0:T(8,128)S(1)} %get-tuple-element.32), channel_id=1, source_target_pairs={{0,16},{16,0},{32,48},{48,32},{64,80},{80,64},{96,112},{112,96},{1... | collective-permute-start | bytes 4718600 | tf_op jit(solution)/shard_map/ppermute | solution.py:226
  59.6 3.0 %collective-permute-done.got = f32[4,48,16,128]{3,2,1,0:T(8,128)S(1)} collective-permute-done((f32[4,48,16,128]{3,2,1,0:T(8,128)S(1)}, f32[4,48,16,128]{3,2,1,0:T(8,128)S(1)}, u32[]{:S(2)}, u32[]{:S(2)}) %collective-permute-start) | collective-permute-done | bytes 1572896 | tf_op jit(solution)/shard_map/ppermute | solution.py:226
  62.6 0.7 shard_map.107
  63.3 1.7 %collective-permute-start.2 = (s16[51,16,128]{2,1,0:T(8,128)(2,1)S(1)}, s16[51,16,128]{2,1,0:T(8,128)(2,1)S(1)}, u32[]{:S(2)}, u32[]{:S(2)}) collective-permute-start(s16[51,16,128]{2,1,0:T(8,128)(2,1)S(1)} %get-tuple-element.36), channel_id=1, source_target_pairs={{0,32},{16,48},{32,64},{48,80},{64,96},{80,112},{96,0},{112,16},{1... | collective-permute-start | bytes 626696 | tf_op jit(solution)/shard_map/ppermute | solution.py:229
  65.0 1.4 collective-permute-start.3
  66.5 1.2 collective-permute-start.4
  67.7 10.8 %shard_map.108 = (f32[4,48,16,128]{3,2,1,0:T(8,128)S(1)}, f32[4,48,16,128]{3,2,1,0:T(8,128)S(1)}) custom-call(s32[1,1792]{1,0:T(1,128)S(1)} %get-tuple-element.28.lists, s32[2]{0:T(128)S(1)} %get-tuple-element.29.counts, bf16[65,128,128]{2,1,0:T(8,128)(2,1)S(1)} %copy-done.14, bf16[64,128,128]{2,1,0:T(8,128)(2,1)S(1)} %copy-done.3, ...), custom_call_target="tpu_custom_call" | custom-call | flops 99999997952 | bytes 300000000 | tf_op jit(solution)/shard_map/pallas_call | solution.py:264
  78.5 1.3 collective-permute-start.1
  79.8 1.3 shard_map.109
  81.1 0.7 collective-permute-start.13
  81.9 1.0 collective-permute-done.1.got
  82.8 0.7 shard_map.110
  83.5 0.8 collective-permute-start.5
  84.3 1.9 %collective-permute-start.6 = (s16[51,16,128]{2,1,0:T(8,128)(2,1)S(1)}, s16[51,16,128]{2,1,0:T(8,128)(2,1)S(1)}, u32[]{:S(2)}, u32[]{:S(2)}) collective-permute-start(s16[51,16,128]{2,1,0:T(8,128)(2,1)S(1)} %get-tuple-element.42), channel_id=1, source_target_pairs={{0,96},{16,112},{32,0},{48,16},{64,32},{80,48},{96,64},{112,80},{1... | collective-permute-start | bytes 626696 | tf_op jit(solution)/shard_map/ppermute | solution.py:229
  86.3 1.1 collective-permute-start.7
  87.3 1.9 %collective-permute-start.12 = (bf16[48,16,128]{2,1,0:T(8,128)(2,1)S(1)}, bf16[48,16,128]{2,1,0:T(8,128)(2,1)S(1)}, u32[]{:S(2)}, u32[]{:S(2)}) collective-permute-start(bf16[48,16,128]{2,1,0:T(8,128)(2,1)S(1)} %get-tuple-element.39.rest_0_), channel_id=1, source_target_pairs={{0,64},{16,80},{32,96},{48,112},{64,0},{80,16},{96,32},{112,48},{1... | collective-permute-start | bytes 589832 | tf_op jit(solution)/shard_map/ppermute | solution.py:229
  89.2 0.8 collective-permute-start.11
  90.0 12.5 %collective-permute-done.12.rest_2_ = bf16[48,16,128]{2,1,0:T(8,128)(2,1)S(1)} collective-permute-done((bf16[48,16,128]{2,1,0:T(8,128)(2,1)S(1)}, bf16[48,16,128]{2,1,0:T(8,128)(2,1)S(1)}, u32[]{:S(2)}, u32[]{:S(2)}) %collective-permute-start.12) | collective-permute-done | bytes 196640 | tf_op jit(solution)/shard_map/ppermute | solution.py:229
  102.5 0.8 collective-permute-start.14
  103.3 1.5 collective-permute-start.17
  104.9 0.5 collective-permute-start.15
  105.4 1.3 shard_map.111
  106.7 2.5 %collective-permute-start.10 = (bf16[48,16,128]{2,1,0:T(8,128)(2,1)S(1)}, bf16[48,16,128]{2,1,0:T(8,128)(2,1)S(1)}, u32[]{:S(2)}, u32[]{:S(2)}) collective-permute-start(bf16[48,16,128]{2,1,0:T(8,128)(2,1)S(1)} %get-tuple-element.49.rest_8_.rest_0_), channel_id=1, source_target_pairs={{0,64},{16,80},{32,96},{48,112},{64,0},{80,16},{96,32},{112,48},{1... | collective-permute-start | bytes 589832 | tf_op jit(solution)/shard_map/ppermute | solution.py:229
  109.1 1.2 collective-permute-start.9
  110.4 1.4 collective-permute-start.8
  111.8 10.1 %shard_map.112.rest_8_ = f32[64,128,128]{2,1,0:T(8,128)S(1)} custom-call(s32[1,1792]{1,0:T(1,128)S(1)} %get-tuple-element.28.lists, s32[2]{0:T(128)S(1)} %get-tuple-element.29.counts, bf16[65,128,128]{2,1,0:T(8,128)(2,1)S(1)} %copy-done.10, bf16[64,128,128]{2,1,0:T(8,128)(2,1)S(1)} %copy-done.12, bf16[48,16,128]{2,1,0:T(8,128)(2,1)S(1)} %get-tuple-element.39.rest_0_, ...), custom_call_target="tpu_custom_call" | custom-call | flops 99999997952 | bytes 300000000 | tf_op jit(solution)/shard_map/pallas_call | solution.py:328
  121.9 1.0 collective-permute-start.18
  123.0 0.4 collective-permute-start.20
  123.5 0.5 collective-permute-done.18.rest_4_
  124.0 0.4 collective-permute-done.19.rest_5_
  124.4 0.3 collective-permute-done.20.rest_6_
  124.7 0.3 collective-permute-done.21.rest_7_
  124.9 10.3 %shard_map.113 = s16[16,528,128]{2,1,0:T(8,128)(2,1)S(1)} custom-call(s32[1,1792]{1,0:T(1,128)S(1)} %get-tuple-element.28.lists, s32[2]{0:T(128)S(1)} %get-tuple-element.29.counts, bf16[65,128,128]{2,1,0:T(8,128)(2,1)S(1)} %copy-done.10, bf16[64,128,128]{2,1,0:T(8,128)(2,1)S(1)} %copy-done.12, bf16[48,16,128]{2,1,0:T(8,128)(2,1)S(1)} %get-tuple-element.49.rest_8_.rest_0_, ...), custom_call_target="tpu_custom_call" | custom-call | flops 99999997952 | bytes 300000000 | tf_op jit(solution)/shard_map/pallas_call | solution.py:328
  135.3 32.1 %all_to_all.10.coded = s16[16,528,128]{2,1,0:T(8,128)(2,1)S(1)} all-to-all(s16[16,528,128]{2,1,0:T(8,128)(2,1)S(1)} %shard_map.113), channel_id=1, replica_groups=mesh['slab'=8,'tile'=16] {'tile'}, dimensions={0} | all-to-all | bytes 4325376 | tf_op jit(solution)/shard_map/all_to_all | solution.py:337
  167.4 2.8 %shard_map.114 = f32[32,128,128]{2,1,0:T(8,128)} custom-call(s32[1,16,4]{2,1,0:T(8,128)S(1)} %copy.12.send, s16[16,528,128]{2,1,0:T(8,128)(2,1)S(1)} %all_to_all.10.coded), custom_call_target="tpu_custom_call" | custom-call | flops 40000000000 | bytes 120000000 | tf_op jit(solution)/shard_map/pallas_call | solution.py:338
  (50 shorter events, 0.5 us)
Async XLA Ops:
  1.4 1.2 copy-start.4
  4.7 8.0 %copy-start = (bf16[64,128,128]{2,1,0:T(8,128)(2,1)S(1)}, bf16[64,128,128]{2,1,0:T(8,128)(2,1)}, u32[]{:S(2)}) copy-start(bf16[64,128,128]{2,1,0:T(8,128)(2,1)} %rows_table.1) | copy-start | bytes 6291460
  4.7 8.0 %copy-start.5 = (s32[1,768]{1,0:T(1,128)S(1)}, s32[1,768]{1,0:T(1,128)}, u32[]{:S(2)}) copy-start(s32[1,768]{1,0:T(1,128)} %tile_ids.1) | copy-start | bytes 9220
  4.7 8.0 %copy-start.6 = (s32[1,768]{1,0:T(1,128)S(1)}, s32[1,768]{1,0:T(1,128)}, u32[]{:S(2)}) copy-start(s32[1,768]{1,0:T(1,128)} %block_ids.1) | copy-start | bytes 9220
  4.7 8.0 %copy-start.7 = (s32[1,768]{1,0:T(1,128)S(1)}, s32[1,768]{1,0:T(1,128)}, u32[]{:S(2)}) copy-start(s32[1,768]{1,0:T(1,128)} %row_ids.1) | copy-start | bytes 9220
  4.7 8.0 %copy-start.8 = (s32[1,768]{1,0:T(1,128)S(1)}, s32[1,768]{1,0:T(1,128)}, u32[]{:S(2)}) copy-start(s32[1,768]{1,0:T(1,128)} %col_ids.1) | copy-start | bytes 9220
  4.8 38.3 %all-to-all-start = ((bf16[16,4,128,128]{3,2,1,0:T(8,128)(2,1)}), bf16[16,4,128,128]{3,2,1,0:T(8,128)(2,1)}, u32[]{:S(2)}, u32[]{:S(2)}) async-start(bf16[16,4,128,128]{3,2,1,0:T(8,128)(2,1)} %shard_map.105), calls=%async_computation | async-start | bytes 4194304 | tf_op jit(solution)/shard_map/all_to_all | solution.py:239
  12.8 1.6 copy-start.1
  23.4 1.4 copy-start.9
  24.8 1.4 copy-start.11
  26.2 1.4 copy-start.13
  43.1 1.6 copy-start.2
  44.7 1.6 copy-start.14
  57.4 5.2 %collective-permute-start = (f32[4,48,16,128]{3,2,1,0:T(8,128)S(1)}, f32[4,48,16,128]{3,2,1,0:T(8,128)S(1)}, u32[]{:S(2)}, u32[]{:S(2)}) collective-permute-start(f32[4,48,16,128]{3,2,1,0:T(8,128)S(1)} %get-tuple-element.32), channel_id=1, source_target_pairs={{0,16},{16,0},{32,48},{48,32},{64,80},{80,64},{96,112},{112,96},{1... | collective-permute-start | bytes 4718600 | tf_op jit(solution)/shard_map/ppermute | solution.py:226
  62.6 5.0 %copy-start.3 = (bf16[64,128,128]{2,1,0:T(8,128)(2,1)S(1)}, bf16[64,128,128]{2,1,0:T(8,128)(2,1)}, u32[]{:S(2)}) copy-start(bf16[64,128,128]{2,1,0:T(8,128)(2,1)} %cols.3) | copy-start | bytes 6291460
  62.6 17.2 %slice-start = ((s8[6291456]{0:T(1024)(128)(4,1)}), s8[4194304]{0:T(1024)(128)(4,1)S(1)}, s32[]{:S(2)}) async-start(s8[6291456]{0:T(1024)(128)(4,1)} %bitcast.2), calls=%async_computation.2 | async-start | bytes 8388608
  63.3 16.5 %collective-permute-start.2 = (s16[51,16,128]{2,1,0:T(8,128)(2,1)S(1)}, s16[51,16,128]{2,1,0:T(8,128)(2,1)S(1)}, u32[]{:S(2)}, u32[]{:S(2)}) collective-permute-start(s16[51,16,128]{2,1,0:T(8,128)(2,1)S(1)} %get-tuple-element.36), channel_id=1, source_target_pairs={{0,32},{16,48},{32,64},{48,80},{64,96},{80,112},{96,0},{112,16},{1... | collective-permute-start | bytes 626696 | tf_op jit(solution)/shard_map/ppermute | solution.py:229
  65.0 14.8 %collective-permute-start.3 = (s16[51,16,128]{2,1,0:T(8,128)(2,1)S(1)}, s16[51,16,128]{2,1,0:T(8,128)(2,1)S(1)}, u32[]{:S(2)}, u32[]{:S(2)}) collective-permute-start(s16[51,16,128]{2,1,0:T(8,128)(2,1)S(1)} %get-tuple-element.37), channel_id=1, source_target_pairs={{0,96},{16,112},{32,0},{48,16},{64,32},{80,48},{96,64},{112,80},{1... | collective-permute-start | bytes 626696 | tf_op jit(solution)/shard_map/ppermute | solution.py:229
  66.5 13.3 %collective-permute-start.4 = (s16[51,16,128]{2,1,0:T(8,128)(2,1)S(1)}, s16[51,16,128]{2,1,0:T(8,128)(2,1)S(1)}, u32[]{:S(2)}, u32[]{:S(2)}) collective-permute-start(s16[51,16,128]{2,1,0:T(8,128)(2,1)S(1)} %get-tuple-element.38), channel_id=1, source_target_pairs={{0,64},{16,80},{32,96},{48,112},{64,0},{80,16},{96,32},{112,48},{1... | collective-permute-start | bytes 626696 | tf_op jit(solution)/shard_map/ppermute | solution.py:229
  67.7 12.2 %slice-start.1 = ((s8[6291456]{0:T(1024)(128)(4,1)}), s8[2097152]{0:T(1024)(128)(4,1)S(1)}, s32[]{:S(2)}) async-start(s8[6291456]{0:T(1024)(128)(4,1)} %bitcast.2), calls=%async_computation.3 | async-start | bytes 4194304
  78.5 4.3 %collective-permute-start.1 = (f32[4,48,16,128]{3,2,1,0:T(8,128)S(1)}, f32[4,48,16,128]{3,2,1,0:T(8,128)S(1)}, u32[]{:S(2)}, u32[]{:S(2)}) collective-permute-start(f32[4,48,16,128]{3,2,1,0:T(8,128)S(1)} %get-tuple-element.35), channel_id=1, source_target_pairs={{0,16},{16,0},{32,48},{48,32},{64,80},{80,64},{96,112},{112,96},{1... | collective-permute-start | bytes 4718600 | tf_op jit(solution)/shard_map/ppermute | solution.py:226
  81.1 8.1 %collective-permute-start.13 = (bf16[48,16,128]{2,1,0:T(8,128)(2,1)S(1)}, bf16[48,16,128]{2,1,0:T(8,128)(2,1)S(1)}, u32[]{:S(2)}, u32[]{:S(2)}) collective-permute-start(bf16[48,16,128]{2,1,0:T(8,128)(2,1)S(1)} %get-tuple-element.39.rest_0_), channel_id=1, source_target_pairs={{0,32},{16,48},{32,64},{48,80},{64,96},{80,112},{96,0},{112,16},{1... | collective-permute-start | bytes 589832 | tf_op jit(solution)/shard_map/ppermute | solution.py:229
  83.5 21.3 %collective-permute-start.5 = (s16[51,16,128]{2,1,0:T(8,128)(2,1)S(1)}, s16[51,16,128]{2,1,0:T(8,128)(2,1)S(1)}, u32[]{:S(2)}, u32[]{:S(2)}) collective-permute-start(s16[51,16,128]{2,1,0:T(8,128)(2,1)S(1)} %get-tuple-element.41), channel_id=1, source_target_pairs={{0,32},{16,48},{32,64},{48,80},{64,96},{80,112},{96,0},{112,16},{1... | collective-permute-start | bytes 626696 | tf_op jit(solution)/shard_map/ppermute | solution.py:229
  84.3 20.5 %collective-permute-start.6 = (s16[51,16,128]{2,1,0:T(8,128)(2,1)S(1)}, s16[51,16,128]{2,1,0:T(8,128)(2,1)S(1)}, u32[]{:S(2)}, u32[]{:S(2)}) collective-permute-start(s16[51,16,128]{2,1,0:T(8,128)(2,1)S(1)} %get-tuple-element.42), channel_id=1, source_target_pairs={{0,96},{16,112},{32,0},{48,16},{64,32},{80,48},{96,64},{112,80},{1... | collective-permute-start | bytes 626696 | tf_op jit(solution)/shard_map/ppermute | solution.py:229
  86.3 19.1 %collective-permute-start.7 = (s16[51,16,128]{2,1,0:T(8,128)(2,1)S(1)}, s16[51,16,128]{2,1,0:T(8,128)(2,1)S(1)}, u32[]{:S(2)}, u32[]{:S(2)}) collective-permute-start(s16[51,16,128]{2,1,0:T(8,128)(2,1)S(1)} %get-tuple-element.43), channel_id=1, source_target_pairs={{0,64},{16,80},{32,96},{48,112},{64,0},{80,16},{96,32},{112,48},{1... | collective-permute-start | bytes 626696 | tf_op jit(solution)/shard_map/ppermute | solution.py:229
  87.3 15.2 %collective-permute-start.12 = (bf16[48,16,128]{2,1,0:T(8,128)(2,1)S(1)}, bf16[48,16,128]{2,1,0:T(8,128)(2,1)S(1)}, u32[]{:S(2)}, u32[]{:S(2)}) collective-permute-start(bf16[48,16,128]{2,1,0:T(8,128)(2,1)S(1)} %get-tuple-element.39.rest_0_), channel_id=1, source_target_pairs={{0,64},{16,80},{32,96},{48,112},{64,0},{80,16},{96,32},{112,48},{1... | collective-permute-start | bytes 589832 | tf_op jit(solution)/shard_map/ppermute | solution.py:229
  89.2 14.1 %collective-permute-start.11 = (bf16[48,16,128]{2,1,0:T(8,128)(2,1)S(1)}, bf16[48,16,128]{2,1,0:T(8,128)(2,1)S(1)}, u32[]{:S(2)}, u32[]{:S(2)}) collective-permute-start(bf16[48,16,128]{2,1,0:T(8,128)(2,1)S(1)} %get-tuple-element.39.rest_0_), channel_id=1, source_target_pairs={{0,96},{16,112},{32,0},{48,16},{64,32},{80,48},{96,64},{112,80},{1... | collective-permute-start | bytes 589832 | tf_op jit(solution)/shard_map/ppermute | solution.py:229
  102.5 6.6 %collective-permute-start.14 = (bf16[48,16,128]{2,1,0:T(8,128)(2,1)S(1)}, bf16[48,16,128]{2,1,0:T(8,128)(2,1)S(1)}, u32[]{:S(2)}, u32[]{:S(2)}) collective-permute-start(bf16[48,16,128]{2,1,0:T(8,128)(2,1)S(1)} %get-tuple-element.39.rest_0_), channel_id=1, source_target_pairs={{0,16},{16,0},{32,48},{48,32},{64,80},{80,64},{96,112},{112,96},{1... | collective-permute-start | bytes 589832 | tf_op jit(solution)/shard_map/ppermute | solution.py:226
  103.3 7.0 %collective-permute-start.17 = (bf16[48,16,128]{2,1,0:T(8,128)(2,1)S(1)}, bf16[48,16,128]{2,1,0:T(8,128)(2,1)S(1)}, u32[]{:S(2)}, u32[]{:S(2)}) collective-permute-start(bf16[48,16,128]{2,1,0:T(8,128)(2,1)S(1)} %collective-permute-done.13.rest_3_), channel_id=1, source_target_pairs={{0,16},{16,0},{32,48},{48,32},{64,80},{80,64},{96,112},{112,96},{1... | collective-permute-start | bytes 589832 | tf_op jit(solution)/shard_map/ppermute | solution.py:226
  104.9 7.0 %collective-permute-start.16 = (bf16[48,16,128]{2,1,0:T(8,128)(2,1)S(1)}, bf16[48,16,128]{2,1,0:T(8,128)(2,1)S(1)}, u32[]{:S(2)}, u32[]{:S(2)}) collective-permute-start(bf16[48,16,128]{2,1,0:T(8,128)(2,1)S(1)} %collective-permute-done.12.rest_2_), channel_id=1, source_target_pairs={{0,16},{16,0},{32,48},{48,32},{64,80},{80,64},{96,112},{112,96},{1... | collective-permute-start | bytes 589832 | tf_op jit(solution)/shard_map/ppermute | solution.py:226
  104.9 7.0 %collective-permute-start.15 = (bf16[48,16,128]{2,1,0:T(8,128)(2,1)S(1)}, bf16[48,16,128]{2,1,0:T(8,128)(2,1)S(1)}, u32[]{:S(2)}, u32[]{:S(2)}) collective-permute-start(bf16[48,16,128]{2,1,0:T(8,128)(2,1)S(1)} %collective-permute-done.11.rest_1_), channel_id=1, source_target_pairs={{0,16},{16,0},{32,48},{48,32},{64,80},{80,64},{96,112},{112,96},{1... | collective-permute-start | bytes 589832 | tf_op jit(solution)/shard_map/ppermute | solution.py:226
  105.4 6.5 %copy-start.10 = (bf16[65,128,128]{2,1,0:T(8,128)(2,1)S(1)}, bf16[65,128,128]{2,1,0:T(8,128)(2,1)}, u32[]{:S(2)}) copy-start(bf16[65,128,128]{2,1,0:T(8,128)(2,1)} %copy-done.9) | copy-start | bytes 6389764
  105.4 6.5 %copy-start.12 = (bf16[64,128,128]{2,1,0:T(8,128)(2,1)S(1)}, bf16[64,128,128]{2,1,0:T(8,128)(2,1)}, u32[]{:S(2)}) copy-start(bf16[64,128,128]{2,1,0:T(8,128)(2,1)} %copy-done.11) | copy-start | bytes 6291460
  106.7 15.2 %collective-permute-start.10 = (bf16[48,16,128]{2,1,0:T(8,128)(2,1)S(1)}, bf16[48,16,128]{2,1,0:T(8,128)(2,1)S(1)}, u32[]{:S(2)}, u32[]{:S(2)}) collective-permute-start(bf16[48,16,128]{2,1,0:T(8,128)(2,1)S(1)} %get-tuple-element.49.rest_8_.rest_0_), channel_id=1, source_target_pairs={{0,64},{16,80},{32,96},{48,112},{64,0},{80,16},{96,32},{112,48},{1... | collective-permute-start | bytes 589832 | tf_op jit(solution)/shard_map/ppermute | solution.py:229
  109.1 12.8 %collective-permute-start.9 = (bf16[48,16,128]{2,1,0:T(8,128)(2,1)S(1)}, bf16[48,16,128]{2,1,0:T(8,128)(2,1)S(1)}, u32[]{:S(2)}, u32[]{:S(2)}) collective-permute-start(bf16[48,16,128]{2,1,0:T(8,128)(2,1)S(1)} %get-tuple-element.49.rest_8_.rest_0_), channel_id=1, source_target_pairs={{0,32},{16,48},{32,64},{48,80},{64,96},{80,112},{96,0},{112,16},{1... | collective-permute-start | bytes 589832 | tf_op jit(solution)/shard_map/ppermute | solution.py:229
  110.4 11.6 %collective-permute-start.8 = (bf16[48,16,128]{2,1,0:T(8,128)(2,1)S(1)}, bf16[48,16,128]{2,1,0:T(8,128)(2,1)S(1)}, u32[]{:S(2)}, u32[]{:S(2)}) collective-permute-start(bf16[48,16,128]{2,1,0:T(8,128)(2,1)S(1)} %get-tuple-element.49.rest_8_.rest_0_), channel_id=1, source_target_pairs={{0,96},{16,112},{32,0},{48,16},{64,32},{80,48},{96,64},{112,80},{1... | collective-permute-start | bytes 589832 | tf_op jit(solution)/shard_map/ppermute | solution.py:229
  121.9 2.1 %collective-permute-start.18 = (bf16[48,16,128]{2,1,0:T(8,128)(2,1)S(1)}, bf16[48,16,128]{2,1,0:T(8,128)(2,1)S(1)}, u32[]{:S(2)}, u32[]{:S(2)}) collective-permute-start(bf16[48,16,128]{2,1,0:T(8,128)(2,1)S(1)} %get-tuple-element.49.rest_8_.rest_0_), channel_id=1, source_target_pairs={{0,16},{16,0},{32,48},{48,32},{64,80},{80,64},{96,112},{112,96},{1... | collective-permute-start | bytes 589832 | tf_op jit(solution)/shard_map/ppermute | solution.py:226
  122.9 1.4 collective-permute-start.19
  123.0 1.6 collective-permute-start.20
  123.4 1.5 collective-permute-start.21

commit v3 on v2

--- a/solution.py
+++ b/solution.py
@@ -39,8 +39,8 @@
             out[k, s] = density[send[0, k, s]]
 
 
-def prepare_kernel(bands, tile_ids, block_ids, row_ids, col_ids, rows_table, cols_table,
-                   lists, counts, rows, rows_t, cols_t, *, per):
+def prepare_kernel(bands, tile_ids, block_ids, row_ids, col_ids, rows_table, cols_table, after,
+                   lists, counts, rows_t, cols_t, *, per):
     count = rows_table.shape[0]
     entries = tile_ids.shape[1]
     stride = lists.shape[1] // groups
@@ -70,19 +70,16 @@
 
         lax.fori_loop(0, unroll, pad_step, 0)
 
+    starts = [pl.multiple_of(bands[k] * 16, 16) for k in range(8)]
+
     def table_step(i, carry):
         for u in range(4):
             r = i * 4 + u
-            for k in range(8):
-                rows[r, k * 16:(k + 1) * 16] = rows_table[r, pl.ds(pl.multiple_of(bands[k] * 16, 16), 16)]
             cols_t[r] = cols_table[r].T
-        for u in range(4):
-            r = i * 4 + u
-            rows_t[r] = rows[r].T
+            rows_t[r] = jnp.concatenate([rows_table[r, pl.ds(start, 16)] for start in starts], 0).T
         return carry
 
     lax.fori_loop(0, count // 4, table_step, 0)
-    rows[count] = jnp.zeros(rows.shape[1:], bf16)
     rows_t[count] = jnp.zeros(rows_t.shape[1:], bf16)
 
 
@@ -97,53 +94,56 @@
     lax.fori_loop(0, short - 2 * double, functools.partial(step, width=unroll, first=double * 2 * unroll), 0)
 
 
-def forward_kernel(lists, counts, rows, cols, blocks, *rest, g):
-    mine, theirs = rest[-2:]
-    mine[...] = jnp.zeros_like(mine)
-    theirs[...] = jnp.zeros_like(theirs)
-    base = g * (lists.shape[1] // groups)
-
-    def step(i, carry, width, first):
-        items = [unpack(lists[0, base + first + i * width + u]) for u in range(width)]
-        half = [mm(rows[r], blocks[b]).astype(bf16) for _, b, r, _ in items]
-        parts = [mm(h, cols[c]) for h, (_, _, _, c) in zip(half, items)]
-        for part, (t, _, _, _) in zip(parts, items):
-            for k in range(4):
-                mine[k, t] += part[k * 16:(k + 1) * 16]
-                theirs[k, t] += part[64 + k * 16:64 + (k + 1) * 16]
-        return carry
-
-    run_steps(counts[g], step)
-
-
-def combine_kernel(mine, got, *rest):
-    own, q1, q2, q3 = rest[-4:]
-    own[...] = mine[0] + got[0]
-    n = own.shape[0]
-    for k, q in ((1, q1), (2, q2), (3, q3)):
-        def group(g, carry):
+def forward_kernel(bands, tile_ids, block_ids, row_ids, col_ids, rows, cols, blocks, *sums):
+    for total in sums:
+        total[...] = jnp.zeros_like(total)
+    starts = [pl.multiple_of(bands[k] * 16, 16) for k in range(8)]
+
+    def step(i, carry):
+        entries = [i * 2 * unroll + u for u in range(2 * unroll)]
+        half = []
+        for e in entries:
+            r = row_ids[0, e]
+            left = jnp.concatenate([rows[r, pl.ds(start, 16)] for start in starts], 0)
+            half.append(mm(left, blocks[block_ids[0, e]]).astype(bf16))
+        parts = [mm(h, cols[col_ids[0, e]]) for h, e in zip(half, entries)]
+        for part, e in zip(parts, entries):
+            t = tile_ids[0, e]
+            for k, total in enumerate(sums):
+                total[t] += part[k * 16:(k + 1) * 16]
+        return carry
+
+    lax.fori_loop(0, tile_ids.shape[1] // (2 * unroll), step, 0)
+
+
+def combine_kernel(mine, got, q):
+    per = mine.shape[0] // groups
+    wide = q.shape[0] // groups
+    for g in range(groups):
+        def pack(h, carry):
             levels = []
             for s in range(16):
-                t = g * 16 + s
-                v = mine[k, t] + got[k, t]
+                t = h * 16 + s
+                v = mine[g * per + t] + got[g * per + t]
                 level = code_level(jnp.max(v, axis=0, keepdims=True))
                 scale = jnp.exp2(level * -0.125) * (2.0 * top)
-                q[t] = jnp.round(v * scale - top).astype(i32).astype(i16)
+                q[g * wide + t] = jnp.round(v * scale - top).astype(i32).astype(i16)
                 levels.append(level)
-            q[n + g] = jnp.concatenate(levels, 0).astype(i32).astype(i16)
+            q[g * wide + per + h] = jnp.concatenate(levels, 0).astype(i32).astype(i16)
             return carry
-        lax.fori_loop(0, n // 16, group, 0)
-
-
-def slope_kernel(place, own, q1, q2, q3, target, *rest):
+
+        lax.fori_loop(0, per // 16, pack, 0)
+
+
+def slope_kernel(place, mine, got, q1, q2, q3, target, *rest):
     image, grad = rest[-2:]
-    n = own.shape[0]
+    n = mine.shape[0]
 
     def group(g, carry):
         steps = [jnp.exp2(q[n + g].astype(i32).astype(f32) * 0.125) * (0.5 / top) for q in (q1, q2, q3)]
         for s in range(16):
             t = g * 16 + s
-            v = own[t]
+            v = mine[t] + got[t]
             for q, step in zip((q1, q2, q3), steps):
                 v = v + (q[t].astype(i32).astype(f32) + top) * step[s:s + 1]
             image[t] = v
@@ -210,14 +210,16 @@
     lax.fori_loop(0, coded.shape[0], step, 0)
 
 
+def band_order(me):
+    depth, core = me // 2, me % 2
+    order = ((depth + jnp.arange(4)) % 4)[None, :] * 2 + (core + jnp.arange(2))[:, None] % 2
+    return order.reshape(-1).astype(i32)
+
+
 def local(density, send_list, entry_tile, entry_block, entry_rows, entry_cols, rows_table, cols_table, target):
     tiles = target.shape[0]
     send = send_list
     peers, slots = send.shape[1:]
-    me = lax.axis_index("slab")
-    depth, core = me // 2, me % 2
-    order = ((depth + jnp.arange(4)) % 4)[None, :] * 2 + (core + jnp.arange(2))[:, None] % 2
-    order = order.reshape(-1).astype(i32)
     per = tiles // groups
 
     pair = [(i, i ^ 1) for i in range(8)]
@@ -228,6 +230,7 @@
     def along(x, s):
         return lax.ppermute(x, "slab", [(i, (i + 2 * s) % 8) for i in range(8)])
 
+    me, send = lax.optimization_barrier((lax.axis_index("slab"), send))
     outgoing = pl.pallas_call(
         gather_kernel,
         out_shape=jax.ShapeDtypeStruct((peers, slots, 128, 128), bf16),
@@ -238,82 +241,70 @@
     )(send, density)
     blocks = lax.all_to_all(outgoing, "tile", split_axis=0, concat_axis=0, tiled=True)
     blocks = blocks.reshape(peers * slots, 128, 128)
-
-    table = jax.ShapeDtypeStruct((rows_table.shape[0] + 1, 128, 128), bf16)
-    lists, counts, rows, rows_t, cols_t = pl.pallas_call(
+    me, blocks = lax.optimization_barrier((me, blocks))
+    order = band_order(me)
+
+    band_sum = jax.ShapeDtypeStruct((tiles, 16, 128), f32)
+    wide = per + per // 16
+    coded = jax.ShapeDtypeStruct((groups * wide, 16, 128), i16)
+    sums = pl.pallas_call(
+        forward_kernel,
+        out_shape=(band_sum,) * 8,
+        in_specs=[SMEM] * 5 + [VMEM] * 3,
+        out_specs=(VMEM,) * 8,
+        compiler_params=params(16),
+        cost_estimate=cost(20),
+    )(order, entry_tile, entry_block, entry_rows, entry_cols, rows_table, cols_table, blocks)
+    mine = sums[:4]
+    got = [None] * 4
+    coded_sums = [None] * 4
+    for k in (2, 1, 3):
+        got[k] = swap(sums[4 + k])
+        coded_sums[k] = pl.pallas_call(
+            combine_kernel,
+            out_shape=coded,
+            in_specs=[VMEM] * 2,
+            out_specs=VMEM,
+            compiler_params=params(12),
+            cost_estimate=cost(0.5),
+        )(mine[k], got[k])
+    got[0] = swap(sums[4])
+    arrived = [along(coded_sums[k], k) for k in (1, 3, 2)]
+    lists, counts, rows_t, cols_t = pl.pallas_call(
         functools.partial(prepare_kernel, per=per),
         out_shape=(
             jax.ShapeDtypeStruct((1, groups * (entry_tile.shape[1] + 128)), i32),
             jax.ShapeDtypeStruct((groups,), i32),
-            table,
-            table,
+            jax.ShapeDtypeStruct((rows_table.shape[0] + 1, 128, 128), bf16),
             jax.ShapeDtypeStruct(cols_table.shape, bf16),
         ),
-        in_specs=[SMEM] * 5 + [VMEM] * 2,
-        out_specs=(SMEM, SMEM, VMEM, VMEM, VMEM),
-        compiler_params=params(16),
-        cost_estimate=cost(15),
-    )(order, entry_tile, entry_block, entry_rows, entry_cols, rows_table, cols_table)
-
-    bands = jax.ShapeDtypeStruct((4, per, 16, 128), f32)
-    coded = jax.ShapeDtypeStruct((per + per // 16, 16, 128), i16)
-    band = pl.BlockSpec((per, 16, 128), lambda i, place: (0, 0, 0))
-    code = pl.BlockSpec(coded.shape, lambda i, place: (0, 0, 0))
-
-    def forward(g, after):
-        mine, theirs = pl.pallas_call(
-            functools.partial(forward_kernel, g=g),
-            out_shape=(bands, bands),
-            in_specs=[SMEM] * 2 + [VMEM] * 3 + [ANY] * len(after),
-            out_specs=(VMEM, VMEM),
-            compiler_params=params(16),
-            cost_estimate=cost(20 / groups),
-        )(lists, counts, rows, cols_table, blocks, *after)
-        return mine, swap(theirs)
-
-    def combine(mine, got, after):
-        return pl.pallas_call(
-            combine_kernel,
-            out_shape=(jax.ShapeDtypeStruct((per, 16, 128), f32), coded, coded, coded),
-            in_specs=[VMEM] * 2 + [ANY] * len(after),
-            out_specs=(VMEM,) * 4,
-            compiler_params=params(16),
-            cost_estimate=cost(2 / groups),
-        )(mine, got, *after)
-
-    def slope(g, part, held):
-        return pl.pallas_call(
+        in_specs=[SMEM] * 5 + [VMEM] * 2 + [ANY],
+        out_specs=(SMEM, SMEM, VMEM, VMEM),
+        compiler_params=params(12),
+        cost_estimate=cost(10),
+    )(order, entry_tile, entry_block, entry_rows, entry_cols, rows_table, cols_table, coded_sums[3])
+    part = (mine[0], got[0], *arrived)
+    image, grads, token = [], [], []
+    for g in range(groups):
+        band = pl.BlockSpec((per, 16, 128), lambda i, place: (0, 0, 0))
+        code = pl.BlockSpec((wide, 16, 128), lambda i, place, g=g: (g, 0, 0))
+        picked = pl.BlockSpec((per, 16, 128), lambda i, place, g=g: (g, 0, 0))
+        picture, grad = pl.pallas_call(
             slope_kernel,
             out_shape=(jax.ShapeDtypeStruct((tiles, 16, 128), f32), jax.ShapeDtypeStruct((per, 16, 128), bf16)),
             grid_spec=pltpu.PrefetchScalarGridSpec(
                 num_scalar_prefetch=1,
                 grid=(1,),
-                in_specs=[band, code, code, code, pl.BlockSpec((per, 16, 128), lambda i, place, g=g: (g, place[0], 0))]
-                + [ANY] * len(held),
-                out_specs=(pl.BlockSpec((per, 16, 128), lambda i, place, g=g: (g, 0, 0)), band),
+                in_specs=[picked, picked, code, code, code, pl.BlockSpec((per, 16, 128), lambda i, place, g=g: (g, place[0], 0))]
+                + [ANY] * (len(image) + 1),
+                out_specs=(picked, band),
             ),
-            input_output_aliases={6: 0} if held else {},
+            input_output_aliases={7: 0} if image else {},
             compiler_params=params(16),
             cost_estimate=cost(3 / groups),
-        )(me.reshape(1).astype(i32), *part, target, *held)
-
-    image, token = [], []
-    parts, grads = [], []
-
-    def finish(part):
-        nonlocal image, token
-        picture, grad = slope(len(grads), part, image)
+        )(me.reshape(1).astype(i32), *part, target, *image, rows_t)
         image, token = [picture], [grad]
         grads.append((grad, along(grad, 3), along(grad, 1), along(grad, 2)))
-
-    for g in range(groups):
-        mine, got = forward(g, token)
-        if g:
-            finish(parts[g - 1])
-        own, q1, q2, q3 = combine(mine, got, token if g else [])
-        token = [own]
-        parts.append((own, along(q1, 1), along(q3, 3), along(q2, 2)))
-    finish(parts[-1])
     image = image[0]
     acc = None
     slot_sums = jax.ShapeDtypeStruct((peers * slots, 128, 128), f32)
@@ -323,6 +314,8 @@
         near = grads[g]
         if g:
             near, acc = lax.optimization_barrier((near, acc))
+        else:
+            near, token = lax.optimization_barrier((near, token))
         near = [near[0], near[1], near[3], near[2]]
         near = near + [swap(x) for x in near]
         acc = pl.pallas_call(

time: 171 us -> 169 us (0.988)
  blocking collectives: 32.1 us -> 68.2 us
  waiting for transfers between devices: 33.5 us -> 17.8 us
  starting transfers between devices: 32.4 us -> 19.6 us
  local copies, waits for them, and re-layouts: 11 us -> 6.02 us
  Pallas kernels: 60.3 us -> 56.5 us
    all_to_all x0 -> x1, blocking collectives: none -> 34.9 us  [local(): lax.all_to_all(outgoing, 'tile', split_axis=0, concat_axis=0, tiled=True)]
    all_to_all x1 -> x0, waiting for transfers between devices: 15.6 us -> none  [local(): lax.all_to_all(outgoing, 'tile', split_axis=0, concat_axis=0, tiled=True)]
    all_to_all x1 -> x0, starting transfers between devices: 7.78 us -> none  [local(): lax.all_to_all(outgoing, 'tile', split_axis=0, concat_axis=0, tiled=True)]
    unnamed x35 -> x26, local copies, waits for them, and re-layouts: 10.9 us -> 5.18 us
    ppermute x12 -> x9, starting transfers between devices: 16.7 us -> 13.6 us  [along(): return lax.ppermute(x, 'slab', [(i, (i + 2 * s) % 8) for i in range(8)])]
    ppermute x10 -> x12, waiting for transfers between devices: 5.41 us -> 2.72 us  [swap(): return lax.ppermute(x, 'slab', pair)]
    ppermute x12 -> x9, waiting for transfers between devices: 12.5 us -> 15.1 us  [along(): return lax.ppermute(x, 'slab', [(i, (i + 2 * s) % 8) for i in range(8)])]
    pallas_call x6, Pallas kernels: 25.9 us -> 23.6 us  [the longest x1 19.7 us: local(): pl.pallas_call(forward_kernel, out_shape=(band_sum,) * 8, in_specs=[SMEM]...]
  transfers between devices with their start and end apart: 23 -> 21, of which waited for: 8 -> 9; matrix products, arithmetic and copies ran while one was open for 0% -> 0% of each run, Pallas kernels for 19% -> 12%
where the time goes in v3:
time: 169 us
  blocking collectives  68.2 us (40%)
  Pallas kernels  56.5 us (33%)
  starting transfers between devices  19.6 us (12%)
  waiting for transfers between devices  17.8 us (11%)
  local copies, waits for them, and re-layouts  6.02 us (4%)
    all_to_all x1, blocking collectives, local(): lax.all_to_all(outgoing, 'tile', split_axis=0, concat_axis=0, tiled=True)  34.9 us
    all_to_all x1, blocking collectives, local(): lax.all_to_all(acc, 'tile', split_axis=0, concat_axis=0, tiled=True)  33.3 us
    pallas_call x2, Pallas kernels, local(): pl.pallas_call(functools.partial(backward_kernel, g=g), out_shape=packed_...  20.4 us
    pallas_call x1, Pallas kernels, local(): pl.pallas_call(forward_kernel, out_shape=(band_sum,) * 8, in_specs=[SMEM]...  19.7 us
    ppermute x9, waiting for transfers between devices, along(): return lax.ppermute(x, 'slab', [(i, (i + 2 * s) % 8) for i in range(8)])  15.1 us
    ppermute x9, starting transfers between devices, along(): return lax.ppermute(x, 'slab', [(i, (i + 2 * s) % 8) for i in range(8)])  13.6 us
    pallas_call x1, Pallas kernels, local(): pl.pallas_call(functools.partial(prepare_kernel, per=per), out_shape=(jax...  8.83 us
    ppermute x12, starting transfers between devices, swap(): return lax.ppermute(x, 'slab', pair)  5.97 us
  transfers between devices with their start and end apart: 21, of which 9 were waited for; matrix products, arithmetic and copies ran while one was open for 0% of the time, Pallas kernels for 12%

profile of v3, /device:TPU:1, one launch (start us, length us, event | category | flops | bytes accessed | tf_op | source)
XLA Modules:
  0.0 169.0 jit_solution(11130012077549368823)
XLA Ops:
  0.6 0.8 copy.12.send
  1.4 1.2 copy-done.6
  2.6 0.8 shard_map.104
  3.4 0.6 copy-done
  4.0 34.9 %all_to_all.10 = bf16[16,4,128,128]{3,2,1,0:T(8,128)(2,1)S(1)} all-to-all(bf16[16,4,128,128]{3,2,1,0:T(8,128)(2,1)S(1)} %shard_map.104), channel_id=1, replica_groups=mesh['slab'=8,'tile'=16] {'tile'}, dimensions={0} | all-to-all | bytes 4194304 | tf_op jit(solution)/shard_map/all_to_all | solution.py:242
  39.0 0.1 broadcast_add_fusion
  39.0 0.1 add.73.bands
  39.1 1.6 copy-done.2
  40.7 1.6 copy-done.4
  42.3 19.7 %shard_map.105 = (f32[96,16,128]{2,1,0:T(8,128)S(1)}, f32[96,16,128]{2,1,0:T(8,128)S(1)}, f32[96,16,128]{2,1,0:T(8,128)S(1)}, f32[96,16,128]{2,1,0:T(8,128)S(1)}...) custom-call(s32[8]{0:T(128)S(1)} %add.73.bands, ...), custom_call_target="tpu_custom_call" | custom-call | flops 199999995904 | bytes 600000000 | tf_op jit(solution)/shard_map/pallas_call | solution.py:250
  62.0 2.1 %collective-permute-start.1 = (f32[96,16,128]{2,1,0:T(8,128)S(1)}, f32[96,16,128]{2,1,0:T(8,128)S(1)}, u32[]{:S(2)}, u32[]{:S(2)}) collective-permute-start(f32[96,16,128]{2,1,0:T(8,128)S(1)} %get-tuple-element.39), channel_id=1, source_target_pairs={{0,16},{16,0},{32,48},{48,32},{64,80},{80,64},{96,112},{112,96},{1... | collective-permute-start | bytes 2359304 | tf_op jit(solution)/shard_map/ppermute | solution.py:228
  64.0 0.1 collective-permute-start.3
  64.1 0.4 collective-permute-start
  64.6 0.1 collective-permute-start.5
  64.6 1.3 collective-permute-done.1.got
  66.0 0.4 shard_map.106
  66.4 1.8 %collective-permute-start.2 = (s16[102,16,128]{2,1,0:T(8,128)(2,1)S(1)}, s16[102,16,128]{2,1,0:T(8,128)(2,1)S(1)}, u32[]{:S(2)}, u32[]{:S(2)}) collective-permute-start(s16[102,16,128]{2,1,0:T(8,128)(2,1)S(1)} %shard_map.106), channel_id=1, source_target_pairs={{0,32},{16,48},{32,64},{48,80},{64,96},{80,112},{96,0},{112,16},{1... | collective-permute-start | bytes 1253384 | tf_op jit(solution)/shard_map/ppermute | solution.py:231
  68.2 0.4 shard_map.107.after
  68.6 2.8 %collective-permute-start.4 = (s16[102,16,128]{2,1,0:T(8,128)(2,1)S(1)}, s16[102,16,128]{2,1,0:T(8,128)(2,1)S(1)}, u32[]{:S(2)}, u32[]{:S(2)}) collective-permute-start(s16[102,16,128]{2,1,0:T(8,128)(2,1)S(1)} %shard_map.107.after), channel_id=1, source_target_pairs={{0,96},{16,112},{32,0},{48,16},{64,32},{80,48},{96,64},{112,80},{1... | collective-permute-start | bytes 1253384 | tf_op jit(solution)/shard_map/ppermute | solution.py:231
  71.4 0.5 shard_map.108
  71.9 1.6 collective-permute-start.6
  73.5 0.1 copy-done.5
  73.6 8.8 %shard_map.109 = (s32[1,1792]{1,0:T(1,128)S(1)}, s32[2]{0:T(128)S(1)}, bf16[65,128,128]{2,1,0:T(8,128)(2,1)S(1)}, bf16[64,128,128]{2,1,0:T(8,128)(2,1)S(1)}) custom-call(s32[8]{0:T(128)S(1)} %add.73.bands, s32[1,768]{1,0:T(1,128)S(1)} %copy-done.7, s32[1,768]{1,0:T(1,128)S(1)} %copy-done.8, s32[1,768]{1,0:T(1,128)S(1)} %copy-done.9, ...), custom_call_target="tpu_custom_call" | custom-call | flops 99999997952 | bytes 300000000 | tf_op jit(solution)/shard_map/pallas_call | solution.py:273
  82.5 6.4 %collective-permute-done.4.q2 = s16[102,16,128]{2,1,0:T(8,128)(2,1)S(1)} collective-permute-done((s16[102,16,128]{2,1,0:T(8,128)(2,1)S(1)}, s16[102,16,128]{2,1,0:T(8,128)(2,1)S(1)}, u32[]{:S(2)}, u32[]{:S(2)}) %collective-permute-start.4) | collective-permute-done | bytes 417824 | tf_op jit(solution)/shard_map/ppermute | solution.py:231
  88.9 0.9 collective-permute-done.6.q3
  89.8 1.3 shard_map.110
  91.1 3.2 %collective-permute-start.11 = (bf16[48,16,128]{2,1,0:T(8,128)(2,1)S(1)}, bf16[48,16,128]{2,1,0:T(8,128)(2,1)S(1)}, u32[]{:S(2)}, u32[]{:S(2)}) collective-permute-start(bf16[48,16,128]{2,1,0:T(8,128)(2,1)S(1)} %get-tuple-element.52.rest_0_), channel_id=1, source_target_pairs={{0,32},{16,48},{32,64},{48,80},{64,96},{80,112},{96,0},{112,16},{1... | collective-permute-start | bytes 589832 | tf_op jit(solution)/shard_map/ppermute | solution.py:231
  94.3 0.2 collective-permute-start.10
  94.6 1.3 shard_map.111
  95.9 2.0 %collective-permute-done.12.rest_2_ = bf16[48,16,128]{2,1,0:T(8,128)(2,1)S(1)} collective-permute-done((bf16[48,16,128]{2,1,0:T(8,128)(2,1)S(1)}, bf16[48,16,128]{2,1,0:T(8,128)(2,1)S(1)}, u32[]{:S(2)}, u32[]{:S(2)}) %collective-permute-start.12) | collective-permute-done | bytes 196640 | tf_op jit(solution)/shard_map/ppermute | solution.py:231
  97.9 5.8 %collective-permute-done.11.rest_3_ = bf16[48,16,128]{2,1,0:T(8,128)(2,1)S(1)} collective-permute-done((bf16[48,16,128]{2,1,0:T(8,128)(2,1)S(1)}, bf16[48,16,128]{2,1,0:T(8,128)(2,1)S(1)}, u32[]{:S(2)}, u32[]{:S(2)}) %collective-permute-start.11) | collective-permute-done | bytes 196640 | tf_op jit(solution)/shard_map/ppermute | solution.py:231
  103.7 0.8 collective-permute-start.13
  104.5 0.5 collective-permute-start.15
  105.0 1.4 collective-permute-start.9
  106.3 1.6 collective-permute-start.8
  107.9 1.1 collective-permute-start.7
  109.0 9.3 %shard_map.112.rest_8_ = f32[64,128,128]{2,1,0:T(8,128)S(1)} custom-call(s32[1,1792]{1,0:T(1,128)S(1)} %get-tuple-element.47.lists, s32[2]{0:T(128)S(1)} %get-tuple-element.48.counts, bf16[65,128,128]{2,1,0:T(8,128)(2,1)S(1)} %get-tuple-element.44.rest_0_.rest_1_.rows_t, bf16[64,128,128]{2,1,0:T(8,128)(2,1)S(1)} %get-tuple-element.49.cols_t, ...), custom_call_target="tpu_custom_call" | custom-call | flops 99999997952 | bytes 300000000 | tf_op jit(solution)/shard_map/pallas_call | solution.py:321
  118.4 1.4 collective-permute-start.17
  119.8 0.1 collective-permute-start.18
  119.9 0.4 collective-permute-start.19
  120.3 0.1 collective-permute-start.20
  120.4 0.5 collective-permute-done.17.rest_4_
  120.9 0.4 collective-permute-done.18.rest_5_
  121.2 0.3 collective-permute-done.19.rest_6_
  121.5 0.3 collective-permute-done.20.rest_7_
  121.8 11.1 %shard_map.113 = s16[16,528,128]{2,1,0:T(8,128)(2,1)S(1)} custom-call(s32[1,1792]{1,0:T(1,128)S(1)} %get-tuple-element.47.lists, s32[2]{0:T(128)S(1)} %get-tuple-element.48.counts, bf16[65,128,128]{2,1,0:T(8,128)(2,1)S(1)} %get-tuple-element.44.rest_0_.rest_1_.rows_t, bf16[64,128,128]{2,1,0:T(8,128)(2,1)S(1)} %get-tuple-element.49.cols_t, ...), custom_call_target="tpu_custom_call" | custom-call | flops 99999997952 | bytes 300000000 | tf_op jit(solution)/shard_map/pallas_call | solution.py:321
  132.9 33.3 %all_to_all.11.coded = s16[16,528,128]{2,1,0:T(8,128)(2,1)S(1)} all-to-all(s16[16,528,128]{2,1,0:T(8,128)(2,1)S(1)} %shard_map.113), channel_id=1, replica_groups=mesh['slab'=8,'tile'=16] {'tile'}, dimensions={0} | all-to-all | bytes 4325376 | tf_op jit(solution)/shard_map/all_to_all | solution.py:330
  166.2 2.8 %shard_map.114 = f32[32,128,128]{2,1,0:T(8,128)} custom-call(s32[1,16,4]{2,1,0:T(8,128)S(1)} %copy-done.1, s16[16,528,128]{2,1,0:T(8,128)(2,1)S(1)} %all_to_all.11.coded), custom_call_target="tpu_custom_call" | custom-call | flops 40000000000 | bytes 120000000 | tf_op jit(solution)/shard_map/pallas_call | solution.py:331
  (39 shorter events, 0.1 us)
Async XLA Ops:
  1.4 1.2 copy-start.6
  3.4 0.6 copy-start
  4.0 35.1 %copy-start.7 = (s32[1,768]{1,0:T(1,128)S(1)}, s32[1,768]{1,0:T(1,128)}, u32[]{:S(2)}) copy-start(s32[1,768]{1,0:T(1,128)} %tile_ids.3) | copy-start | bytes 9220
  4.0 35.1 %copy-start.8 = (s32[1,768]{1,0:T(1,128)S(1)}, s32[1,768]{1,0:T(1,128)}, u32[]{:S(2)}) copy-start(s32[1,768]{1,0:T(1,128)} %block_ids.3) | copy-start | bytes 9220
  4.0 35.1 %copy-start.9 = (s32[1,768]{1,0:T(1,128)S(1)}, s32[1,768]{1,0:T(1,128)}, u32[]{:S(2)}) copy-start(s32[1,768]{1,0:T(1,128)} %row_ids.3) | copy-start | bytes 9220
  4.0 35.1 %copy-start.10 = (s32[1,768]{1,0:T(1,128)S(1)}, s32[1,768]{1,0:T(1,128)}, u32[]{:S(2)}) copy-start(s32[1,768]{1,0:T(1,128)} %col_ids.3) | copy-start | bytes 9220
  39.1 1.6 copy-start.2
  40.7 1.6 copy-start.4
  62.0 4.0 %collective-permute-start.1 = (f32[96,16,128]{2,1,0:T(8,128)S(1)}, f32[96,16,128]{2,1,0:T(8,128)S(1)}, u32[]{:S(2)}, u32[]{:S(2)}) collective-permute-start(f32[96,16,128]{2,1,0:T(8,128)S(1)} %get-tuple-element.39), channel_id=1, source_target_pairs={{0,16},{16,0},{32,48},{48,32},{64,80},{80,64},{96,112},{112,96},{1... | collective-permute-start | bytes 2359304 | tf_op jit(solution)/shard_map/ppermute | solution.py:228
  64.0 4.1 %collective-permute-start.3 = (f32[96,16,128]{2,1,0:T(8,128)S(1)}, f32[96,16,128]{2,1,0:T(8,128)S(1)}, u32[]{:S(2)}, u32[]{:S(2)}) collective-permute-start(f32[96,16,128]{2,1,0:T(8,128)S(1)} %get-tuple-element.41), channel_id=1, source_target_pairs={{0,16},{16,0},{32,48},{48,32},{64,80},{80,64},{96,112},{112,96},{1... | collective-permute-start | bytes 2359304 | tf_op jit(solution)/shard_map/ppermute | solution.py:228
  64.1 18.3 %collective-permute-start = (f32[96,16,128]{2,1,0:T(8,128)S(1)}, f32[96,16,128]{2,1,0:T(8,128)S(1)}, u32[]{:S(2)}, u32[]{:S(2)}) collective-permute-start(f32[96,16,128]{2,1,0:T(8,128)S(1)} %get-tuple-element.37), channel_id=1, source_target_pairs={{0,16},{16,0},{32,48},{48,32},{64,80},{80,64},{96,112},{112,96},{1... | collective-permute-start | bytes 2359304 | tf_op jit(solution)/shard_map/ppermute | solution.py:228
  64.6 6.9 %collective-permute-start.5 = (f32[96,16,128]{2,1,0:T(8,128)S(1)}, f32[96,16,128]{2,1,0:T(8,128)S(1)}, u32[]{:S(2)}, u32[]{:S(2)}) collective-permute-start(f32[96,16,128]{2,1,0:T(8,128)S(1)} %get-tuple-element.43), channel_id=1, source_target_pairs={{0,16},{16,0},{32,48},{48,32},{64,80},{80,64},{96,112},{112,96},{1... | collective-permute-start | bytes 2359304 | tf_op jit(solution)/shard_map/ppermute | solution.py:228
  66.4 16.1 %collective-permute-start.2 = (s16[102,16,128]{2,1,0:T(8,128)(2,1)S(1)}, s16[102,16,128]{2,1,0:T(8,128)(2,1)S(1)}, u32[]{:S(2)}, u32[]{:S(2)}) collective-permute-start(s16[102,16,128]{2,1,0:T(8,128)(2,1)S(1)} %shard_map.106), channel_id=1, source_target_pairs={{0,32},{16,48},{32,64},{48,80},{64,96},{80,112},{96,0},{112,16},{1... | collective-permute-start | bytes 1253384 | tf_op jit(solution)/shard_map/ppermute | solution.py:231
  68.6 20.3 %collective-permute-start.4 = (s16[102,16,128]{2,1,0:T(8,128)(2,1)S(1)}, s16[102,16,128]{2,1,0:T(8,128)(2,1)S(1)}, u32[]{:S(2)}, u32[]{:S(2)}) collective-permute-start(s16[102,16,128]{2,1,0:T(8,128)(2,1)S(1)} %shard_map.107.after), channel_id=1, source_target_pairs={{0,96},{16,112},{32,0},{48,16},{64,32},{80,48},{96,64},{112,80},{1... | collective-permute-start | bytes 1253384 | tf_op jit(solution)/shard_map/ppermute | solution.py:231
  71.4 2.1 %copy-start.3 = (bf16[64,128,128]{2,1,0:T(8,128)(2,1)S(1)}, bf16[64,128,128]{2,1,0:T(8,128)(2,1)}, u32[]{:S(2)}) copy-start(bf16[64,128,128]{2,1,0:T(8,128)(2,1)} %rows_table.1) | copy-start | bytes 6291460
  71.4 2.2 %copy-start.5 = (bf16[64,128,128]{2,1,0:T(8,128)(2,1)S(1)}, bf16[64,128,128]{2,1,0:T(8,128)(2,1)}, u32[]{:S(2)}) copy-start(bf16[64,128,128]{2,1,0:T(8,128)(2,1)} %cols_table.1) | copy-start | bytes 6291460
  71.4 18.4 %slice-start = ((s8[6291456]{0:T(1024)(128)(4,1)}), s8[4194304]{0:T(1024)(128)(4,1)S(1)}, s32[]{:S(2)}) async-start(s8[6291456]{0:T(1024)(128)(4,1)} %bitcast.3), calls=%async_computation.2 | async-start | bytes 8388608
  71.9 17.9 %slice-start.1 = ((s8[6291456]{0:T(1024)(128)(4,1)}), s8[2097152]{0:T(1024)(128)(4,1)S(1)}, s32[]{:S(2)}) async-start(s8[6291456]{0:T(1024)(128)(4,1)} %bitcast.3), calls=%async_computation.3 | async-start | bytes 4194304
  71.9 17.9 %collective-permute-start.6 = (s16[102,16,128]{2,1,0:T(8,128)(2,1)S(1)}, s16[102,16,128]{2,1,0:T(8,128)(2,1)S(1)}, u32[]{:S(2)}, u32[]{:S(2)}) collective-permute-start(s16[102,16,128]{2,1,0:T(8,128)(2,1)S(1)} %shard_map.108), channel_id=1, source_target_pairs={{0,64},{16,80},{32,96},{48,112},{64,0},{80,16},{96,32},{112,48},{1... | collective-permute-start | bytes 1253384 | tf_op jit(solution)/shard_map/ppermute | solution.py:231
  91.1 6.7 %collective-permute-start.12 = (bf16[48,16,128]{2,1,0:T(8,128)(2,1)S(1)}, bf16[48,16,128]{2,1,0:T(8,128)(2,1)S(1)}, u32[]{:S(2)}, u32[]{:S(2)}) collective-permute-start(bf16[48,16,128]{2,1,0:T(8,128)(2,1)S(1)} %get-tuple-element.52.rest_0_), channel_id=1, source_target_pairs={{0,64},{16,80},{32,96},{48,112},{64,0},{80,16},{96,32},{112,48},{1... | collective-permute-start | bytes 589832 | tf_op jit(solution)/shard_map/ppermute | solution.py:231
  91.1 12.5 %collective-permute-start.11 = (bf16[48,16,128]{2,1,0:T(8,128)(2,1)S(1)}, bf16[48,16,128]{2,1,0:T(8,128)(2,1)S(1)}, u32[]{:S(2)}, u32[]{:S(2)}) collective-permute-start(bf16[48,16,128]{2,1,0:T(8,128)(2,1)S(1)} %get-tuple-element.52.rest_0_), channel_id=1, source_target_pairs={{0,32},{16,48},{32,64},{48,80},{64,96},{80,112},{96,0},{112,16},{1... | collective-permute-start | bytes 589832 | tf_op jit(solution)/shard_map/ppermute | solution.py:231
  94.3 9.3 %collective-permute-start.10 = (bf16[48,16,128]{2,1,0:T(8,128)(2,1)S(1)}, bf16[48,16,128]{2,1,0:T(8,128)(2,1)S(1)}, u32[]{:S(2)}, u32[]{:S(2)}) collective-permute-start(bf16[48,16,128]{2,1,0:T(8,128)(2,1)S(1)} %get-tuple-element.52.rest_0_), channel_id=1, source_target_pairs={{0,96},{16,112},{32,0},{48,16},{64,32},{80,48},{96,64},{112,80},{1... | collective-permute-start | bytes 589832 | tf_op jit(solution)/shard_map/ppermute | solution.py:231
  103.7 2.7 %collective-permute-start.13 = (bf16[48,16,128]{2,1,0:T(8,128)(2,1)S(1)}, bf16[48,16,128]{2,1,0:T(8,128)(2,1)S(1)}, u32[]{:S(2)}, u32[]{:S(2)}) collective-permute-start(bf16[48,16,128]{2,1,0:T(8,128)(2,1)S(1)} %get-tuple-element.52.rest_0_), channel_id=1, source_target_pairs={{0,16},{16,0},{32,48},{48,32},{64,80},{80,64},{96,112},{112,96},{1... | collective-permute-start | bytes 589832 | tf_op jit(solution)/shard_map/ppermute | solution.py:228
  104.4 3.4 %collective-permute-start.14 = (bf16[48,16,128]{2,1,0:T(8,128)(2,1)S(1)}, bf16[48,16,128]{2,1,0:T(8,128)(2,1)S(1)}, u32[]{:S(2)}, u32[]{:S(2)}) collective-permute-start(bf16[48,16,128]{2,1,0:T(8,128)(2,1)S(1)} %collective-permute-done.10.rest_1_), channel_id=1, source_target_pairs={{0,16},{16,0},{32,48},{48,32},{64,80},{80,64},{96,112},{112,96},{1... | collective-permute-start | bytes 589832 | tf_op jit(solution)/shard_map/ppermute | solution.py:228
  104.5 4.6 %collective-permute-start.15 = (bf16[48,16,128]{2,1,0:T(8,128)(2,1)S(1)}, bf16[48,16,128]{2,1,0:T(8,128)(2,1)S(1)}, u32[]{:S(2)}, u32[]{:S(2)}) collective-permute-start(bf16[48,16,128]{2,1,0:T(8,128)(2,1)S(1)} %collective-permute-done.12.rest_2_), channel_id=1, source_target_pairs={{0,16},{16,0},{32,48},{48,32},{64,80},{80,64},{96,112},{112,96},{1... | collective-permute-start | bytes 589832 | tf_op jit(solution)/shard_map/ppermute | solution.py:228
  105.0 4.1 %collective-permute-start.16 = (bf16[48,16,128]{2,1,0:T(8,128)(2,1)S(1)}, bf16[48,16,128]{2,1,0:T(8,128)(2,1)S(1)}, u32[]{:S(2)}, u32[]{:S(2)}) collective-permute-start(bf16[48,16,128]{2,1,0:T(8,128)(2,1)S(1)} %collective-permute-done.11.rest_3_), channel_id=1, source_target_pairs={{0,16},{16,0},{32,48},{48,32},{64,80},{80,64},{96,112},{112,96},{1... | collective-permute-start | bytes 589832 | tf_op jit(solution)/shard_map/ppermute | solution.py:228
  105.0 13.4 %collective-permute-start.9 = (bf16[48,16,128]{2,1,0:T(8,128)(2,1)S(1)}, bf16[48,16,128]{2,1,0:T(8,128)(2,1)S(1)}, u32[]{:S(2)}, u32[]{:S(2)}) collective-permute-start(bf16[48,16,128]{2,1,0:T(8,128)(2,1)S(1)} %get-tuple-element.57.rest_8_.rest_0_), channel_id=1, source_target_pairs={{0,64},{16,80},{32,96},{48,112},{64,0},{80,16},{96,32},{112,48},{1... | collective-permute-start | bytes 589832 | tf_op jit(solution)/shard_map/ppermute | solution.py:231
  106.3 12.0 %collective-permute-start.8 = (bf16[48,16,128]{2,1,0:T(8,128)(2,1)S(1)}, bf16[48,16,128]{2,1,0:T(8,128)(2,1)S(1)}, u32[]{:S(2)}, u32[]{:S(2)}) collective-permute-start(bf16[48,16,128]{2,1,0:T(8,128)(2,1)S(1)} %get-tuple-element.57.rest_8_.rest_0_), channel_id=1, source_target_pairs={{0,32},{16,48},{32,64},{48,80},{64,96},{80,112},{96,0},{112,16},{1... | collective-permute-start | bytes 589832 | tf_op jit(solution)/shard_map/ppermute | solution.py:231
  107.9 10.5 %collective-permute-start.7 = (bf16[48,16,128]{2,1,0:T(8,128)(2,1)S(1)}, bf16[48,16,128]{2,1,0:T(8,128)(2,1)S(1)}, u32[]{:S(2)}, u32[]{:S(2)}) collective-permute-start(bf16[48,16,128]{2,1,0:T(8,128)(2,1)S(1)} %get-tuple-element.57.rest_8_.rest_0_), channel_id=1, source_target_pairs={{0,96},{16,112},{32,0},{48,16},{64,32},{80,48},{96,64},{112,80},{1... | collective-permute-start | bytes 589832 | tf_op jit(solution)/shard_map/ppermute | solution.py:231
  118.4 2.5 %collective-permute-start.17 = (bf16[48,16,128]{2,1,0:T(8,128)(2,1)S(1)}, bf16[48,16,128]{2,1,0:T(8,128)(2,1)S(1)}, u32[]{:S(2)}, u32[]{:S(2)}) collective-permute-start(bf16[48,16,128]{2,1,0:T(8,128)(2,1)S(1)} %get-tuple-element.57.rest_8_.rest_0_), channel_id=1, source_target_pairs={{0,16},{16,0},{32,48},{48,32},{64,80},{80,64},{96,112},{112,96},{1... | collective-permute-start | bytes 589832 | tf_op jit(solution)/shard_map/ppermute | solution.py:228
  119.8 1.4 collective-permute-start.18
  119.9 1.6 collective-permute-start.19
  120.3 1.5 collective-permute-start.20
  132.9 33.3 %copy-start.1 = (s32[1,16,4]{2,1,0:T(8,128)S(1)}, s32[1,16,4]{2,1,0:T(8,128)}, u32[]{:S(2)}) copy-start(s32[1,16,4]{2,1,0:T(8,128)} %copy-done) | copy-start | bytes 772

commit v4 on v3

--- a/solution.py
+++ b/solution.py
@@ -304,7 +304,7 @@
             cost_estimate=cost(3 / groups),
         )(me.reshape(1).astype(i32), *part, target, *image, rows_t)
         image, token = [picture], [grad]
-        grads.append((grad, along(grad, 3), along(grad, 1), along(grad, 2)))
+        grads.append((grad, along(grad, 2), along(grad, 3), along(grad, 1)))
     image = image[0]
     acc = None
     slot_sums = jax.ShapeDtypeStruct((peers * slots, 128, 128), f32)
@@ -316,7 +316,7 @@
             near, acc = lax.optimization_barrier((near, acc))
         else:
             near, token = lax.optimization_barrier((near, token))
-        near = [near[0], near[1], near[3], near[2]]
+        near = [near[0], near[2], near[1], near[3]]
         near = near + [swap(x) for x in near]
         acc = pl.pallas_call(
             functools.partial(backward_kernel, g=g),

time: 169 us -> 168 us (level)
  no operation moved by 1% of the time
where the time goes in v4:
time: 168 us
  blocking collectives  67.3 us (40%)
  Pallas kernels  56.5 us (34%)
  starting transfers between devices  20.8 us (12%)
  waiting for transfers between devices  16.7 us (10%)
  local copies, waits for them, and re-layouts  6.04 us (4%)
    all_to_all x1, blocking collectives, local(): lax.all_to_all(outgoing, 'tile', split_axis=0, concat_axis=0, tiled=True)  34.9 us
    all_to_all x1, blocking collectives, local(): lax.all_to_all(acc, 'tile', split_axis=0, concat_axis=0, tiled=True)  32.4 us
    pallas_call x2, Pallas kernels, local(): pl.pallas_call(functools.partial(backward_kernel, g=g), out_shape=packed_...  20.4 us
    pallas_call x1, Pallas kernels, local(): pl.pallas_call(forward_kernel, out_shape=(band_sum,) * 8, in_specs=[SMEM]...  19.7 us
    ppermute x9, waiting for transfers between devices, along(): return lax.ppermute(x, 'slab', [(i, (i + 2 * s) % 8) for i in range(8)])  14 us
    ppermute x9, starting transfers between devices, along(): return lax.ppermute(x, 'slab', [(i, (i + 2 * s) % 8) for i in range(8)])  13.2 us
    pallas_call x1, Pallas kernels, local(): pl.pallas_call(functools.partial(prepare_kernel, per=per), out_shape=(jax...  8.83 us
    ppermute x12, starting transfers between devices, swap(): return lax.ppermute(x, 'slab', pair)  7.62 us
  transfers between devices with their start and end apart: 21, of which 9 were waited for; matrix products, arithmetic and copies ran while one was open for 0% of the time, Pallas kernels for 12%

profile of v4, /device:TPU:1, one launch (start us, length us, event | category | flops | bytes accessed | tf_op | source)
XLA Modules:
  0.0 168.2 jit_solution(5725156810675211827)
XLA Ops:
  0.6 0.8 copy.12.send
  1.4 1.2 copy-done.6
  2.6 0.8 shard_map.104
  3.4 0.6 copy-done
  4.0 34.9 %all_to_all.10 = bf16[16,4,128,128]{3,2,1,0:T(8,128)(2,1)S(1)} all-to-all(bf16[16,4,128,128]{3,2,1,0:T(8,128)(2,1)S(1)} %shard_map.104), channel_id=1, replica_groups=mesh['slab'=8,'tile'=16] {'tile'}, dimensions={0} | all-to-all | bytes 4194304 | tf_op jit(solution)/shard_map/all_to_all | solution.py:242
  39.0 0.1 add.73.bands
  39.1 1.6 copy-done.2
  40.7 1.6 copy-done.4
  42.3 19.7 %shard_map.105 = (f32[96,16,128]{2,1,0:T(8,128)S(1)}, f32[96,16,128]{2,1,0:T(8,128)S(1)}, f32[96,16,128]{2,1,0:T(8,128)S(1)}, f32[96,16,128]{2,1,0:T(8,128)S(1)}...) custom-call(s32[8]{0:T(128)S(1)} %add.73.bands, ...), custom_call_target="tpu_custom_call" | custom-call | flops 199999995904 | bytes 600000000 | tf_op jit(solution)/shard_map/pallas_call | solution.py:250
  62.0 2.0 %collective-permute-start.1 = (f32[96,16,128]{2,1,0:T(8,128)S(1)}, f32[96,16,128]{2,1,0:T(8,128)S(1)}, u32[]{:S(2)}, u32[]{:S(2)}) collective-permute-start(f32[96,16,128]{2,1,0:T(8,128)S(1)} %get-tuple-element.39), channel_id=1, source_target_pairs={{0,16},{16,0},{32,48},{48,32},{64,80},{80,64},{96,112},{112,96},{1... | collective-permute-start | bytes 2359304 | tf_op jit(solution)/shard_map/ppermute | solution.py:228
  64.0 0.1 collective-permute-start.3
  64.1 0.4 collective-permute-start
  64.5 0.1 collective-permute-start.5
  64.6 1.3 collective-permute-done.1.got
  65.9 0.4 shard_map.106
  66.3 1.8 %collective-permute-start.2 = (s16[102,16,128]{2,1,0:T(8,128)(2,1)S(1)}, s16[102,16,128]{2,1,0:T(8,128)(2,1)S(1)}, u32[]{:S(2)}, u32[]{:S(2)}) collective-permute-start(s16[102,16,128]{2,1,0:T(8,128)(2,1)S(1)} %shard_map.106), channel_id=1, source_target_pairs={{0,32},{16,48},{32,64},{48,80},{64,96},{80,112},{96,0},{112,16},{1... | collective-permute-start | bytes 1253384 | tf_op jit(solution)/shard_map/ppermute | solution.py:231
  68.2 0.4 shard_map.107.after
  68.6 2.8 %collective-permute-start.4 = (s16[102,16,128]{2,1,0:T(8,128)(2,1)S(1)}, s16[102,16,128]{2,1,0:T(8,128)(2,1)S(1)}, u32[]{:S(2)}, u32[]{:S(2)}) collective-permute-start(s16[102,16,128]{2,1,0:T(8,128)(2,1)S(1)} %shard_map.107.after), channel_id=1, source_target_pairs={{0,96},{16,112},{32,0},{48,16},{64,32},{80,48},{96,64},{112,80},{1... | collective-permute-start | bytes 1253384 | tf_op jit(solution)/shard_map/ppermute | solution.py:231
  71.4 0.5 shard_map.108
  71.9 1.6 collective-permute-start.6
  73.5 0.2 copy-done.5
  73.6 8.8 %shard_map.109 = (s32[1,1792]{1,0:T(1,128)S(1)}, s32[2]{0:T(128)S(1)}, bf16[65,128,128]{2,1,0:T(8,128)(2,1)S(1)}, bf16[64,128,128]{2,1,0:T(8,128)(2,1)S(1)}) custom-call(s32[8]{0:T(128)S(1)} %add.73.bands, s32[1,768]{1,0:T(1,128)S(1)} %copy-done.7, s32[1,768]{1,0:T(1,128)S(1)} %copy-done.8, s32[1,768]{1,0:T(1,128)S(1)} %copy-done.9, ...), custom_call_target="tpu_custom_call" | custom-call | flops 99999997952 | bytes 300000000 | tf_op jit(solution)/shard_map/pallas_call | solution.py:273
  82.5 6.4 %collective-permute-done.4.q2 = s16[102,16,128]{2,1,0:T(8,128)(2,1)S(1)} collective-permute-done((s16[102,16,128]{2,1,0:T(8,128)(2,1)S(1)}, s16[102,16,128]{2,1,0:T(8,128)(2,1)S(1)}, u32[]{:S(2)}, u32[]{:S(2)}) %collective-permute-start.4) | collective-permute-done | bytes 417824 | tf_op jit(solution)/shard_map/ppermute | solution.py:231
  88.9 0.9 collective-permute-done.6.q3
  89.8 1.3 shard_map.110
  91.1 1.0 collective-permute-start.12
  92.2 1.6 collective-permute-start.11
  93.8 1.1 collective-permute-start.10
  94.9 1.3 shard_map.111
  96.3 1.3 collective-permute-done.12.rest_3_
  97.5 5.4 %collective-permute-done.10.rest_2_ = bf16[48,16,128]{2,1,0:T(8,128)(2,1)S(1)} collective-permute-done((bf16[48,16,128]{2,1,0:T(8,128)(2,1)S(1)}, bf16[48,16,128]{2,1,0:T(8,128)(2,1)S(1)}, u32[]{:S(2)}, u32[]{:S(2)}) %collective-permute-start.10) | collective-permute-done | bytes 196640 | tf_op jit(solution)/shard_map/ppermute | solution.py:231
  102.9 2.1 %collective-permute-start.13 = (bf16[48,16,128]{2,1,0:T(8,128)(2,1)S(1)}, bf16[48,16,128]{2,1,0:T(8,128)(2,1)S(1)}, u32[]{:S(2)}, u32[]{:S(2)}) collective-permute-start(bf16[48,16,128]{2,1,0:T(8,128)(2,1)S(1)} %get-tuple-element.52.rest_0_), channel_id=1, source_target_pairs={{0,16},{16,0},{32,48},{48,32},{64,80},{80,64},{96,112},{112,96},{1... | collective-permute-start | bytes 589832 | tf_op jit(solution)/shard_map/ppermute | solution.py:228
  105.0 0.5 collective-permute-start.15
  105.5 0.9 collective-permute-start.9
  106.4 1.8 %collective-permute-start.8 = (bf16[48,16,128]{2,1,0:T(8,128)(2,1)S(1)}, bf16[48,16,128]{2,1,0:T(8,128)(2,1)S(1)}, u32[]{:S(2)}, u32[]{:S(2)}) collective-permute-start(bf16[48,16,128]{2,1,0:T(8,128)(2,1)S(1)} %get-tuple-element.57.rest_8_.rest_0_), channel_id=1, source_target_pairs={{0,96},{16,112},{32,0},{48,16},{64,32},{80,48},{96,64},{112,80},{1... | collective-permute-start | bytes 589832 | tf_op jit(solution)/shard_map/ppermute | solution.py:231
  108.2 0.5 collective-permute-start.7
  108.7 9.3 %shard_map.112.rest_8_ = f32[64,128,128]{2,1,0:T(8,128)S(1)} custom-call(s32[1,1792]{1,0:T(1,128)S(1)} %get-tuple-element.47.lists, s32[2]{0:T(128)S(1)} %get-tuple-element.48.counts, bf16[65,128,128]{2,1,0:T(8,128)(2,1)S(1)} %get-tuple-element.44.rest_0_.rest_1_.rows_t, bf16[64,128,128]{2,1,0:T(8,128)(2,1)S(1)} %get-tuple-element.49.cols_t, ...), custom_call_target="tpu_custom_call" | custom-call | flops 99999997952 | bytes 300000000 | tf_op jit(solution)/shard_map/pallas_call | solution.py:321
  118.1 1.8 %collective-permute-start.17 = (bf16[48,16,128]{2,1,0:T(8,128)(2,1)S(1)}, bf16[48,16,128]{2,1,0:T(8,128)(2,1)S(1)}, u32[]{:S(2)}, u32[]{:S(2)}) collective-permute-start(bf16[48,16,128]{2,1,0:T(8,128)(2,1)S(1)} %get-tuple-element.57.rest_8_.rest_0_), channel_id=1, source_target_pairs={{0,16},{16,0},{32,48},{48,32},{64,80},{80,64},{96,112},{112,96},{1... | collective-permute-start | bytes 589832 | tf_op jit(solution)/shard_map/ppermute | solution.py:228
  119.8 0.1 collective-permute-start.18
  119.9 0.4 collective-permute-start.19
  120.4 0.1 collective-permute-start.20
  120.4 0.5 collective-permute-done.17.rest_4_
  120.9 0.4 collective-permute-done.18.rest_5_
  121.3 0.3 collective-permute-done.19.rest_6_
  121.6 0.3 collective-permute-done.20.rest_7_
  121.8 11.1 %shard_map.113 = s16[16,528,128]{2,1,0:T(8,128)(2,1)S(1)} custom-call(s32[1,1792]{1,0:T(1,128)S(1)} %get-tuple-element.47.lists, s32[2]{0:T(128)S(1)} %get-tuple-element.48.counts, bf16[65,128,128]{2,1,0:T(8,128)(2,1)S(1)} %get-tuple-element.44.rest_0_.rest_1_.rows_t, bf16[64,128,128]{2,1,0:T(8,128)(2,1)S(1)} %get-tuple-element.49.cols_t, ...), custom_call_target="tpu_custom_call" | custom-call | flops 99999997952 | bytes 300000000 | tf_op jit(solution)/shard_map/pallas_call | solution.py:321
  133.0 32.4 %all_to_all.11.coded = s16[16,528,128]{2,1,0:T(8,128)(2,1)S(1)} all-to-all(s16[16,528,128]{2,1,0:T(8,128)(2,1)S(1)} %shard_map.113), channel_id=1, replica_groups=mesh['slab'=8,'tile'=16] {'tile'}, dimensions={0} | all-to-all | bytes 4325376 | tf_op jit(solution)/shard_map/all_to_all | solution.py:330
  165.4 2.8 %shard_map.114 = f32[32,128,128]{2,1,0:T(8,128)} custom-call(s32[1,16,4]{2,1,0:T(8,128)S(1)} %copy-done.1, s16[16,528,128]{2,1,0:T(8,128)(2,1)S(1)} %all_to_all.11.coded), custom_call_target="tpu_custom_call" | custom-call | flops 40000000000 | bytes 120000000 | tf_op jit(solution)/shard_map/pallas_call | solution.py:331
  (39 shorter events, 0.2 us)
Async XLA Ops:
  1.4 1.2 copy-start.6
  3.4 0.6 copy-start
  4.0 35.1 %copy-start.7 = (s32[1,768]{1,0:T(1,128)S(1)}, s32[1,768]{1,0:T(1,128)}, u32[]{:S(2)}) copy-start(s32[1,768]{1,0:T(1,128)} %tile_ids.3) | copy-start | bytes 9220
  4.0 35.1 %copy-start.8 = (s32[1,768]{1,0:T(1,128)S(1)}, s32[1,768]{1,0:T(1,128)}, u32[]{:S(2)}) copy-start(s32[1,768]{1,0:T(1,128)} %block_ids.3) | copy-start | bytes 9220
  4.0 35.1 %copy-start.9 = (s32[1,768]{1,0:T(1,128)S(1)}, s32[1,768]{1,0:T(1,128)}, u32[]{:S(2)}) copy-start(s32[1,768]{1,0:T(1,128)} %row_ids.3) | copy-start | bytes 9220
  4.0 35.1 %copy-start.10 = (s32[1,768]{1,0:T(1,128)S(1)}, s32[1,768]{1,0:T(1,128)}, u32[]{:S(2)}) copy-start(s32[1,768]{1,0:T(1,128)} %col_ids.3) | copy-start | bytes 9220
  39.1 1.6 copy-start.2
  40.7 1.6 copy-start.4
  62.0 3.9 %collective-permute-start.1 = (f32[96,16,128]{2,1,0:T(8,128)S(1)}, f32[96,16,128]{2,1,0:T(8,128)S(1)}, u32[]{:S(2)}, u32[]{:S(2)}) collective-permute-start(f32[96,16,128]{2,1,0:T(8,128)S(1)} %get-tuple-element.39), channel_id=1, source_target_pairs={{0,16},{16,0},{32,48},{48,32},{64,80},{80,64},{96,112},{112,96},{1... | collective-permute-start | bytes 2359304 | tf_op jit(solution)/shard_map/ppermute | solution.py:228
  64.0 4.2 %collective-permute-start.3 = (f32[96,16,128]{2,1,0:T(8,128)S(1)}, f32[96,16,128]{2,1,0:T(8,128)S(1)}, u32[]{:S(2)}, u32[]{:S(2)}) collective-permute-start(f32[96,16,128]{2,1,0:T(8,128)S(1)} %get-tuple-element.41), channel_id=1, source_target_pairs={{0,16},{16,0},{32,48},{48,32},{64,80},{80,64},{96,112},{112,96},{1... | collective-permute-start | bytes 2359304 | tf_op jit(solution)/shard_map/ppermute | solution.py:228
  64.1 18.4 %collective-permute-start = (f32[96,16,128]{2,1,0:T(8,128)S(1)}, f32[96,16,128]{2,1,0:T(8,128)S(1)}, u32[]{:S(2)}, u32[]{:S(2)}) collective-permute-start(f32[96,16,128]{2,1,0:T(8,128)S(1)} %get-tuple-element.37), channel_id=1, source_target_pairs={{0,16},{16,0},{32,48},{48,32},{64,80},{80,64},{96,112},{112,96},{1... | collective-permute-start | bytes 2359304 | tf_op jit(solution)/shard_map/ppermute | solution.py:228
  64.5 6.9 %collective-permute-start.5 = (f32[96,16,128]{2,1,0:T(8,128)S(1)}, f32[96,16,128]{2,1,0:T(8,128)S(1)}, u32[]{:S(2)}, u32[]{:S(2)}) collective-permute-start(f32[96,16,128]{2,1,0:T(8,128)S(1)} %get-tuple-element.43), channel_id=1, source_target_pairs={{0,16},{16,0},{32,48},{48,32},{64,80},{80,64},{96,112},{112,96},{1... | collective-permute-start | bytes 2359304 | tf_op jit(solution)/shard_map/ppermute | solution.py:228
  66.3 16.1 %collective-permute-start.2 = (s16[102,16,128]{2,1,0:T(8,128)(2,1)S(1)}, s16[102,16,128]{2,1,0:T(8,128)(2,1)S(1)}, u32[]{:S(2)}, u32[]{:S(2)}) collective-permute-start(s16[102,16,128]{2,1,0:T(8,128)(2,1)S(1)} %shard_map.106), channel_id=1, source_target_pairs={{0,32},{16,48},{32,64},{48,80},{64,96},{80,112},{96,0},{112,16},{1... | collective-permute-start | bytes 1253384 | tf_op jit(solution)/shard_map/ppermute | solution.py:231
  68.6 20.3 %collective-permute-start.4 = (s16[102,16,128]{2,1,0:T(8,128)(2,1)S(1)}, s16[102,16,128]{2,1,0:T(8,128)(2,1)S(1)}, u32[]{:S(2)}, u32[]{:S(2)}) collective-permute-start(s16[102,16,128]{2,1,0:T(8,128)(2,1)S(1)} %shard_map.107.after), channel_id=1, source_target_pairs={{0,96},{16,112},{32,0},{48,16},{64,32},{80,48},{96,64},{112,80},{1... | collective-permute-start | bytes 1253384 | tf_op jit(solution)/shard_map/ppermute | solution.py:231
  71.4 2.1 %copy-start.3 = (bf16[64,128,128]{2,1,0:T(8,128)(2,1)S(1)}, bf16[64,128,128]{2,1,0:T(8,128)(2,1)}, u32[]{:S(2)}) copy-start(bf16[64,128,128]{2,1,0:T(8,128)(2,1)} %rows_table.1) | copy-start | bytes 6291460
  71.4 2.2 %copy-start.5 = (bf16[64,128,128]{2,1,0:T(8,128)(2,1)S(1)}, bf16[64,128,128]{2,1,0:T(8,128)(2,1)}, u32[]{:S(2)}) copy-start(bf16[64,128,128]{2,1,0:T(8,128)(2,1)} %cols_table.1) | copy-start | bytes 6291460
  71.4 18.4 %slice-start = ((s8[6291456]{0:T(1024)(128)(4,1)}), s8[4194304]{0:T(1024)(128)(4,1)S(1)}, s32[]{:S(2)}) async-start(s8[6291456]{0:T(1024)(128)(4,1)} %bitcast.3), calls=%async_computation.2 | async-start | bytes 8388608
  71.9 17.9 %slice-start.1 = ((s8[6291456]{0:T(1024)(128)(4,1)}), s8[2097152]{0:T(1024)(128)(4,1)S(1)}, s32[]{:S(2)}) async-start(s8[6291456]{0:T(1024)(128)(4,1)} %bitcast.3), calls=%async_computation.3 | async-start | bytes 4194304
  71.9 17.9 %collective-permute-start.6 = (s16[102,16,128]{2,1,0:T(8,128)(2,1)S(1)}, s16[102,16,128]{2,1,0:T(8,128)(2,1)S(1)}, u32[]{:S(2)}, u32[]{:S(2)}) collective-permute-start(s16[102,16,128]{2,1,0:T(8,128)(2,1)S(1)} %shard_map.108), channel_id=1, source_target_pairs={{0,64},{16,80},{32,96},{48,112},{64,0},{80,16},{96,32},{112,48},{1... | collective-permute-start | bytes 1253384 | tf_op jit(solution)/shard_map/ppermute | solution.py:231
  91.1 6.4 %collective-permute-start.12 = (bf16[48,16,128]{2,1,0:T(8,128)(2,1)S(1)}, bf16[48,16,128]{2,1,0:T(8,128)(2,1)S(1)}, u32[]{:S(2)}, u32[]{:S(2)}) collective-permute-start(bf16[48,16,128]{2,1,0:T(8,128)(2,1)S(1)} %get-tuple-element.52.rest_0_), channel_id=1, source_target_pairs={{0,32},{16,48},{32,64},{48,80},{64,96},{80,112},{96,0},{112,16},{1... | collective-permute-start | bytes 589832 | tf_op jit(solution)/shard_map/ppermute | solution.py:231
  92.2 5.4 %collective-permute-start.11 = (bf16[48,16,128]{2,1,0:T(8,128)(2,1)S(1)}, bf16[48,16,128]{2,1,0:T(8,128)(2,1)S(1)}, u32[]{:S(2)}, u32[]{:S(2)}) collective-permute-start(bf16[48,16,128]{2,1,0:T(8,128)(2,1)S(1)} %get-tuple-element.52.rest_0_), channel_id=1, source_target_pairs={{0,96},{16,112},{32,0},{48,16},{64,32},{80,48},{96,64},{112,80},{1... | collective-permute-start | bytes 589832 | tf_op jit(solution)/shard_map/ppermute | solution.py:231
  93.8 9.1 %collective-permute-start.10 = (bf16[48,16,128]{2,1,0:T(8,128)(2,1)S(1)}, bf16[48,16,128]{2,1,0:T(8,128)(2,1)S(1)}, u32[]{:S(2)}, u32[]{:S(2)}) collective-permute-start(bf16[48,16,128]{2,1,0:T(8,128)(2,1)S(1)} %get-tuple-element.52.rest_0_), channel_id=1, source_target_pairs={{0,64},{16,80},{32,96},{48,112},{64,0},{80,16},{96,32},{112,48},{1... | collective-permute-start | bytes 589832 | tf_op jit(solution)/shard_map/ppermute | solution.py:231
  102.9 3.5 %collective-permute-start.13 = (bf16[48,16,128]{2,1,0:T(8,128)(2,1)S(1)}, bf16[48,16,128]{2,1,0:T(8,128)(2,1)S(1)}, u32[]{:S(2)}, u32[]{:S(2)}) collective-permute-start(bf16[48,16,128]{2,1,0:T(8,128)(2,1)S(1)} %get-tuple-element.52.rest_0_), channel_id=1, source_target_pairs={{0,16},{16,0},{32,48},{48,32},{64,80},{80,64},{96,112},{112,96},{1... | collective-permute-start | bytes 589832 | tf_op jit(solution)/shard_map/ppermute | solution.py:228
  105.0 3.2 %collective-permute-start.14 = (bf16[48,16,128]{2,1,0:T(8,128)(2,1)S(1)}, bf16[48,16,128]{2,1,0:T(8,128)(2,1)S(1)}, u32[]{:S(2)}, u32[]{:S(2)}) collective-permute-start(bf16[48,16,128]{2,1,0:T(8,128)(2,1)S(1)} %collective-permute-done.11.rest_1_), channel_id=1, source_target_pairs={{0,16},{16,0},{32,48},{48,32},{64,80},{80,64},{96,112},{112,96},{1... | collective-permute-start | bytes 589832 | tf_op jit(solution)/shard_map/ppermute | solution.py:228
  105.0 3.7 %collective-permute-start.15 = (bf16[48,16,128]{2,1,0:T(8,128)(2,1)S(1)}, bf16[48,16,128]{2,1,0:T(8,128)(2,1)S(1)}, u32[]{:S(2)}, u32[]{:S(2)}) collective-permute-start(bf16[48,16,128]{2,1,0:T(8,128)(2,1)S(1)} %collective-permute-done.10.rest_2_), channel_id=1, source_target_pairs={{0,16},{16,0},{32,48},{48,32},{64,80},{80,64},{96,112},{112,96},{1... | collective-permute-start | bytes 589832 | tf_op jit(solution)/shard_map/ppermute | solution.py:228
  105.5 3.2 %collective-permute-start.16 = (bf16[48,16,128]{2,1,0:T(8,128)(2,1)S(1)}, bf16[48,16,128]{2,1,0:T(8,128)(2,1)S(1)}, u32[]{:S(2)}, u32[]{:S(2)}) collective-permute-start(bf16[48,16,128]{2,1,0:T(8,128)(2,1)S(1)} %collective-permute-done.12.rest_3_), channel_id=1, source_target_pairs={{0,16},{16,0},{32,48},{48,32},{64,80},{80,64},{96,112},{112,96},{1... | collective-permute-start | bytes 589832 | tf_op jit(solution)/shard_map/ppermute | solution.py:228
  105.5 12.5 %collective-permute-start.9 = (bf16[48,16,128]{2,1,0:T(8,128)(2,1)S(1)}, bf16[48,16,128]{2,1,0:T(8,128)(2,1)S(1)}, u32[]{:S(2)}, u32[]{:S(2)}) collective-permute-start(bf16[48,16,128]{2,1,0:T(8,128)(2,1)S(1)} %get-tuple-element.57.rest_8_.rest_0_), channel_id=1, source_target_pairs={{0,32},{16,48},{32,64},{48,80},{64,96},{80,112},{96,0},{112,16},{1... | collective-permute-start | bytes 589832 | tf_op jit(solution)/shard_map/ppermute | solution.py:231
  106.4 11.7 %collective-permute-start.8 = (bf16[48,16,128]{2,1,0:T(8,128)(2,1)S(1)}, bf16[48,16,128]{2,1,0:T(8,128)(2,1)S(1)}, u32[]{:S(2)}, u32[]{:S(2)}) collective-permute-start(bf16[48,16,128]{2,1,0:T(8,128)(2,1)S(1)} %get-tuple-element.57.rest_8_.rest_0_), channel_id=1, source_target_pairs={{0,96},{16,112},{32,0},{48,16},{64,32},{80,48},{96,64},{112,80},{1... | collective-permute-start | bytes 589832 | tf_op jit(solution)/shard_map/ppermute | solution.py:231
  108.2 9.9 %collective-permute-start.7 = (bf16[48,16,128]{2,1,0:T(8,128)(2,1)S(1)}, bf16[48,16,128]{2,1,0:T(8,128)(2,1)S(1)}, u32[]{:S(2)}, u32[]{:S(2)}) collective-permute-start(bf16[48,16,128]{2,1,0:T(8,128)(2,1)S(1)} %get-tuple-element.57.rest_8_.rest_0_), channel_id=1, source_target_pairs={{0,64},{16,80},{32,96},{48,112},{64,0},{80,16},{96,32},{112,48},{1... | collective-permute-start | bytes 589832 | tf_op jit(solution)/shard_map/ppermute | solution.py:231
  118.1 2.8 %collective-permute-start.17 = (bf16[48,16,128]{2,1,0:T(8,128)(2,1)S(1)}, bf16[48,16,128]{2,1,0:T(8,128)(2,1)S(1)}, u32[]{:S(2)}, u32[]{:S(2)}) collective-permute-start(bf16[48,16,128]{2,1,0:T(8,128)(2,1)S(1)} %get-tuple-element.57.rest_8_.rest_0_), channel_id=1, source_target_pairs={{0,16},{16,0},{32,48},{48,32},{64,80},{80,64},{96,112},{112,96},{1... | collective-permute-start | bytes 589832 | tf_op jit(solution)/shard_map/ppermute | solution.py:228
  119.8 1.4 collective-permute-start.18
  119.9 1.6 collective-permute-start.19
  120.4 1.5 collective-permute-start.20
  133.0 32.4 %copy-start.1 = (s32[1,16,4]{2,1,0:T(8,128)S(1)}, s32[1,16,4]{2,1,0:T(8,128)}, u32[]{:S(2)}) copy-start(s32[1,16,4]{2,1,0:T(8,128)} %copy-done) | copy-start | bytes 772

commit v5 on v4

--- a/solution.py
+++ b/solution.py
@@ -317,7 +317,7 @@
         else:
             near, token = lax.optimization_barrier((near, token))
         near = [near[0], near[2], near[1], near[3]]
-        near = near + [swap(x) for x in near]
+        near = near + [swap(grads[g][0])] + [swap(x) for x in near[1:]]
         acc = pl.pallas_call(
             functools.partial(backward_kernel, g=g),
             out_shape=packed_shape if last else slot_sums,

time: 168 us -> 169 us (level)
  transfers between devices with their start and end apart: 21 -> 21, of which waited for: 9 -> 8; matrix products, arithmetic and copies ran while one was open for 0% -> 0% of each run, Pallas kernels for 12% -> 12%
where the time goes in v5:
time: 169 us
  blocking collectives  66.9 us (40%)
  Pallas kernels  56.5 us (33%)
  starting transfers between devices  20.6 us (12%)
  waiting for transfers between devices  17.8 us (11%)
  local copies, waits for them, and re-layouts  5.99 us (4%)
    all_to_all x1, blocking collectives, local(): lax.all_to_all(outgoing, 'tile', split_axis=0, concat_axis=0, tiled=True)  34.9 us
    all_to_all x1, blocking collectives, local(): lax.all_to_all(acc, 'tile', split_axis=0, concat_axis=0, tiled=True)  32.1 us
    pallas_call x2, Pallas kernels, local(): pl.pallas_call(functools.partial(backward_kernel, g=g), out_shape=packed_...  20.4 us
    pallas_call x1, Pallas kernels, local(): pl.pallas_call(forward_kernel, out_shape=(band_sum,) * 8, in_specs=[SMEM]...  19.7 us
    ppermute x9, waiting for transfers between devices, along(): return lax.ppermute(x, 'slab', [(i, (i + 2 * s) % 8) for i in range(8)])  15.3 us
    ppermute x9, starting transfers between devices, along(): return lax.ppermute(x, 'slab', [(i, (i + 2 * s) % 8) for i in range(8)])  13.2 us
    pallas_call x1, Pallas kernels, local(): pl.pallas_call(functools.partial(prepare_kernel, per=per), out_shape=(jax...  8.83 us
    ppermute x12, starting transfers between devices, swap(): return lax.ppermute(x, 'slab', pair)  7.37 us
  transfers between devices with their start and end apart: 21, of which 8 were waited for; matrix products, arithmetic and copies ran while one was open for 0% of the time, Pallas kernels for 12%

profile of v5, /device:TPU:1, one launch (start us, length us, event | category | flops | bytes accessed | tf_op | source)
XLA Modules:
  0.0 168.8 jit_solution(2822283905229563722)
XLA Ops:
  0.6 0.8 copy.12.send
  1.4 1.2 copy-done.6
  2.6 0.8 shard_map.104
  3.4 0.6 copy-done
  4.0 34.9 %all_to_all.10 = bf16[16,4,128,128]{3,2,1,0:T(8,128)(2,1)S(1)} all-to-all(bf16[16,4,128,128]{3,2,1,0:T(8,128)(2,1)S(1)} %shard_map.104), channel_id=1, replica_groups=mesh['slab'=8,'tile'=16] {'tile'}, dimensions={0} | all-to-all | bytes 4194304 | tf_op jit(solution)/shard_map/all_to_all | solution.py:242
  39.0 0.1 broadcast_add_fusion
  39.0 0.1 add.73.bands
  39.1 1.6 copy-done.2
  40.7 1.6 copy-done.4
  42.3 19.7 %shard_map.105 = (f32[96,16,128]{2,1,0:T(8,128)S(1)}, f32[96,16,128]{2,1,0:T(8,128)S(1)}, f32[96,16,128]{2,1,0:T(8,128)S(1)}, f32[96,16,128]{2,1,0:T(8,128)S(1)}...) custom-call(s32[8]{0:T(128)S(1)} %add.73.bands, ...), custom_call_target="tpu_custom_call" | custom-call | flops 199999995904 | bytes 600000000 | tf_op jit(solution)/shard_map/pallas_call | solution.py:250
  62.0 2.0 %collective-permute-start.1 = (f32[96,16,128]{2,1,0:T(8,128)S(1)}, f32[96,16,128]{2,1,0:T(8,128)S(1)}, u32[]{:S(2)}, u32[]{:S(2)}) collective-permute-start(f32[96,16,128]{2,1,0:T(8,128)S(1)} %get-tuple-element.39), channel_id=1, source_target_pairs={{0,16},{16,0},{32,48},{48,32},{64,80},{80,64},{96,112},{112,96},{1... | collective-permute-start | bytes 2359304 | tf_op jit(solution)/shard_map/ppermute | solution.py:228
  64.0 0.1 collective-permute-start.3
  64.1 0.4 collective-permute-start
  64.5 0.1 collective-permute-start.5
  64.6 1.3 collective-permute-done.1.got
  65.9 0.4 shard_map.106
  66.4 1.8 %collective-permute-start.2 = (s16[102,16,128]{2,1,0:T(8,128)(2,1)S(1)}, s16[102,16,128]{2,1,0:T(8,128)(2,1)S(1)}, u32[]{:S(2)}, u32[]{:S(2)}) collective-permute-start(s16[102,16,128]{2,1,0:T(8,128)(2,1)S(1)} %shard_map.106), channel_id=1, source_target_pairs={{0,32},{16,48},{32,64},{48,80},{64,96},{80,112},{96,0},{112,16},{1... | collective-permute-start | bytes 1253384 | tf_op jit(solution)/shard_map/ppermute | solution.py:231
  68.2 0.4 shard_map.107.after
  68.6 2.8 %collective-permute-start.4 = (s16[102,16,128]{2,1,0:T(8,128)(2,1)S(1)}, s16[102,16,128]{2,1,0:T(8,128)(2,1)S(1)}, u32[]{:S(2)}, u32[]{:S(2)}) collective-permute-start(s16[102,16,128]{2,1,0:T(8,128)(2,1)S(1)} %shard_map.107.after), channel_id=1, source_target_pairs={{0,96},{16,112},{32,0},{48,16},{64,32},{80,48},{96,64},{112,80},{1... | collective-permute-start | bytes 1253384 | tf_op jit(solution)/shard_map/ppermute | solution.py:231
  71.4 0.5 shard_map.108
  71.9 1.6 collective-permute-start.6
  73.5 0.1 copy-done.5
  73.6 8.8 %shard_map.109 = (s32[1,1792]{1,0:T(1,128)S(1)}, s32[2]{0:T(128)S(1)}, bf16[65,128,128]{2,1,0:T(8,128)(2,1)S(1)}, bf16[64,128,128]{2,1,0:T(8,128)(2,1)S(1)}) custom-call(s32[8]{0:T(128)S(1)} %add.73.bands, s32[1,768]{1,0:T(1,128)S(1)} %copy-done.7, s32[1,768]{1,0:T(1,128)S(1)} %copy-done.8, s32[1,768]{1,0:T(1,128)S(1)} %copy-done.9, ...), custom_call_target="tpu_custom_call" | custom-call | flops 99999997952 | bytes 300000000 | tf_op jit(solution)/shard_map/pallas_call | solution.py:273
  82.5 6.4 %collective-permute-done.4.q2 = s16[102,16,128]{2,1,0:T(8,128)(2,1)S(1)} collective-permute-done((s16[102,16,128]{2,1,0:T(8,128)(2,1)S(1)}, s16[102,16,128]{2,1,0:T(8,128)(2,1)S(1)}, u32[]{:S(2)}, u32[]{:S(2)}) %collective-permute-start.4) | collective-permute-done | bytes 417824 | tf_op jit(solution)/shard_map/ppermute | solution.py:231
  88.8 0.9 collective-permute-done.6.q3
  89.8 1.3 shard_map.110
  91.1 1.2 collective-permute-start.13
  92.3 1.4 collective-permute-start.12
  93.7 1.3 collective-permute-start.11
  95.0 1.1 collective-permute-start.10
  96.1 1.3 shard_map.111
  97.4 2.6 %collective-permute-done.12.rest_3_ = bf16[48,16,128]{2,1,0:T(8,128)(2,1)S(1)} collective-permute-done((bf16[48,16,128]{2,1,0:T(8,128)(2,1)S(1)}, bf16[48,16,128]{2,1,0:T(8,128)(2,1)S(1)}, u32[]{:S(2)}, u32[]{:S(2)}) %collective-permute-start.12) | collective-permute-done | bytes 196640 | tf_op jit(solution)/shard_map/ppermute | solution.py:231
  100.0 5.4 %collective-permute-done.10.rest_2_ = bf16[48,16,128]{2,1,0:T(8,128)(2,1)S(1)} collective-permute-done((bf16[48,16,128]{2,1,0:T(8,128)(2,1)S(1)}, bf16[48,16,128]{2,1,0:T(8,128)(2,1)S(1)}, u32[]{:S(2)}, u32[]{:S(2)}) %collective-permute-start.10) | collective-permute-done | bytes 196640 | tf_op jit(solution)/shard_map/ppermute | solution.py:231
  105.4 0.8 collective-permute-start.14
  106.2 0.5 collective-permute-start.16
  106.7 0.9 collective-permute-start.9
  107.6 1.8 %collective-permute-start.8 = (bf16[48,16,128]{2,1,0:T(8,128)(2,1)S(1)}, bf16[48,16,128]{2,1,0:T(8,128)(2,1)S(1)}, u32[]{:S(2)}, u32[]{:S(2)}) collective-permute-start(bf16[48,16,128]{2,1,0:T(8,128)(2,1)S(1)} %get-tuple-element.57.rest_8_.rest_0_), channel_id=1, source_target_pairs={{0,96},{16,112},{32,0},{48,16},{64,32},{80,48},{96,64},{112,80},{1... | collective-permute-start | bytes 589832 | tf_op jit(solution)/shard_map/ppermute | solution.py:231
  109.4 0.5 collective-permute-start.7
  109.9 9.3 %shard_map.112.rest_8_ = f32[64,128,128]{2,1,0:T(8,128)S(1)} custom-call(s32[1,1792]{1,0:T(1,128)S(1)} %get-tuple-element.47.lists, s32[2]{0:T(128)S(1)} %get-tuple-element.48.counts, bf16[65,128,128]{2,1,0:T(8,128)(2,1)S(1)} %get-tuple-element.44.rest_0_.rest_1_.rows_t, bf16[64,128,128]{2,1,0:T(8,128)(2,1)S(1)} %get-tuple-element.49.cols_t, ...), custom_call_target="tpu_custom_call" | custom-call | flops 99999997952 | bytes 300000000 | tf_op jit(solution)/shard_map/pallas_call | solution.py:321
  119.3 1.7 %collective-permute-start.18 = (bf16[48,16,128]{2,1,0:T(8,128)(2,1)S(1)}, bf16[48,16,128]{2,1,0:T(8,128)(2,1)S(1)}, u32[]{:S(2)}, u32[]{:S(2)}) collective-permute-start(bf16[48,16,128]{2,1,0:T(8,128)(2,1)S(1)} %collective-permute-done.8.rest_1_), channel_id=1, source_target_pairs={{0,16},{16,0},{32,48},{48,32},{64,80},{80,64},{96,112},{112,96},{1... | collective-permute-start | bytes 589832 | tf_op jit(solution)/shard_map/ppermute | solution.py:228
  121.0 0.3 collective-permute-start.19
  121.3 0.2 collective-permute-start.20
  121.5 0.6 collective-permute-done.18.rest_5_
  122.1 0.4 collective-permute-done.19.rest_6_
  122.5 0.3 collective-permute-done.20.rest_7_
  122.7 11.1 %shard_map.113 = s16[16,528,128]{2,1,0:T(8,128)(2,1)S(1)} custom-call(s32[1,1792]{1,0:T(1,128)S(1)} %get-tuple-element.47.lists, s32[2]{0:T(128)S(1)} %get-tuple-element.48.counts, bf16[65,128,128]{2,1,0:T(8,128)(2,1)S(1)} %get-tuple-element.44.rest_0_.rest_1_.rows_t, bf16[64,128,128]{2,1,0:T(8,128)(2,1)S(1)} %get-tuple-element.49.cols_t, ...), custom_call_target="tpu_custom_call" | custom-call | flops 99999997952 | bytes 300000000 | tf_op jit(solution)/shard_map/pallas_call | solution.py:321
  133.9 32.1 %all_to_all.11.coded = s16[16,528,128]{2,1,0:T(8,128)(2,1)S(1)} all-to-all(s16[16,528,128]{2,1,0:T(8,128)(2,1)S(1)} %shard_map.113), channel_id=1, replica_groups=mesh['slab'=8,'tile'=16] {'tile'}, dimensions={0} | all-to-all | bytes 4325376 | tf_op jit(solution)/shard_map/all_to_all | solution.py:330
  165.9 2.8 %shard_map.114 = f32[32,128,128]{2,1,0:T(8,128)} custom-call(s32[1,16,4]{2,1,0:T(8,128)S(1)} %copy-done.1, s16[16,528,128]{2,1,0:T(8,128)(2,1)S(1)} %all_to_all.11.coded), custom_call_target="tpu_custom_call" | custom-call | flops 40000000000 | bytes 120000000 | tf_op jit(solution)/shard_map/pallas_call | solution.py:331
  (39 shorter events, 0.1 us)
Async XLA Ops:
  1.4 1.2 copy-start.6
  3.4 0.6 copy-start
  4.0 35.1 %copy-start.7 = (s32[1,768]{1,0:T(1,128)S(1)}, s32[1,768]{1,0:T(1,128)}, u32[]{:S(2)}) copy-start(s32[1,768]{1,0:T(1,128)} %tile_ids.3) | copy-start | bytes 9220
  4.0 35.1 %copy-start.8 = (s32[1,768]{1,0:T(1,128)S(1)}, s32[1,768]{1,0:T(1,128)}, u32[]{:S(2)}) copy-start(s32[1,768]{1,0:T(1,128)} %block_ids.3) | copy-start | bytes 9220
  4.0 35.1 %copy-start.9 = (s32[1,768]{1,0:T(1,128)S(1)}, s32[1,768]{1,0:T(1,128)}, u32[]{:S(2)}) copy-start(s32[1,768]{1,0:T(1,128)} %row_ids.3) | copy-start | bytes 9220
  4.0 35.1 %copy-start.10 = (s32[1,768]{1,0:T(1,128)S(1)}, s32[1,768]{1,0:T(1,128)}, u32[]{:S(2)}) copy-start(s32[1,768]{1,0:T(1,128)} %col_ids.3) | copy-start | bytes 9220
  39.1 1.6 copy-start.2
  40.7 1.6 copy-start.4
  62.0 3.9 %collective-permute-start.1 = (f32[96,16,128]{2,1,0:T(8,128)S(1)}, f32[96,16,128]{2,1,0:T(8,128)S(1)}, u32[]{:S(2)}, u32[]{:S(2)}) collective-permute-start(f32[96,16,128]{2,1,0:T(8,128)S(1)} %get-tuple-element.39), channel_id=1, source_target_pairs={{0,16},{16,0},{32,48},{48,32},{64,80},{80,64},{96,112},{112,96},{1... | collective-permute-start | bytes 2359304 | tf_op jit(solution)/shard_map/ppermute | solution.py:228
  64.0 4.1 %collective-permute-start.3 = (f32[96,16,128]{2,1,0:T(8,128)S(1)}, f32[96,16,128]{2,1,0:T(8,128)S(1)}, u32[]{:S(2)}, u32[]{:S(2)}) collective-permute-start(f32[96,16,128]{2,1,0:T(8,128)S(1)} %get-tuple-element.41), channel_id=1, source_target_pairs={{0,16},{16,0},{32,48},{48,32},{64,80},{80,64},{96,112},{112,96},{1... | collective-permute-start | bytes 2359304 | tf_op jit(solution)/shard_map/ppermute | solution.py:228
  64.1 18.3 %collective-permute-start = (f32[96,16,128]{2,1,0:T(8,128)S(1)}, f32[96,16,128]{2,1,0:T(8,128)S(1)}, u32[]{:S(2)}, u32[]{:S(2)}) collective-permute-start(f32[96,16,128]{2,1,0:T(8,128)S(1)} %get-tuple-element.37), channel_id=1, source_target_pairs={{0,16},{16,0},{32,48},{48,32},{64,80},{80,64},{96,112},{112,96},{1... | collective-permute-start | bytes 2359304 | tf_op jit(solution)/shard_map/ppermute | solution.py:228
  64.5 6.8 %collective-permute-start.5 = (f32[96,16,128]{2,1,0:T(8,128)S(1)}, f32[96,16,128]{2,1,0:T(8,128)S(1)}, u32[]{:S(2)}, u32[]{:S(2)}) collective-permute-start(f32[96,16,128]{2,1,0:T(8,128)S(1)} %get-tuple-element.43), channel_id=1, source_target_pairs={{0,16},{16,0},{32,48},{48,32},{64,80},{80,64},{96,112},{112,96},{1... | collective-permute-start | bytes 2359304 | tf_op jit(solution)/shard_map/ppermute | solution.py:228
  66.4 16.1 %collective-permute-start.2 = (s16[102,16,128]{2,1,0:T(8,128)(2,1)S(1)}, s16[102,16,128]{2,1,0:T(8,128)(2,1)S(1)}, u32[]{:S(2)}, u32[]{:S(2)}) collective-permute-start(s16[102,16,128]{2,1,0:T(8,128)(2,1)S(1)} %shard_map.106), channel_id=1, source_target_pairs={{0,32},{16,48},{32,64},{48,80},{64,96},{80,112},{96,0},{112,16},{1... | collective-permute-start | bytes 1253384 | tf_op jit(solution)/shard_map/ppermute | solution.py:231
  68.6 20.3 %collective-permute-start.4 = (s16[102,16,128]{2,1,0:T(8,128)(2,1)S(1)}, s16[102,16,128]{2,1,0:T(8,128)(2,1)S(1)}, u32[]{:S(2)}, u32[]{:S(2)}) collective-permute-start(s16[102,16,128]{2,1,0:T(8,128)(2,1)S(1)} %shard_map.107.after), channel_id=1, source_target_pairs={{0,96},{16,112},{32,0},{48,16},{64,32},{80,48},{96,64},{112,80},{1... | collective-permute-start | bytes 1253384 | tf_op jit(solution)/shard_map/ppermute | solution.py:231
  71.4 2.1 %copy-start.3 = (bf16[64,128,128]{2,1,0:T(8,128)(2,1)S(1)}, bf16[64,128,128]{2,1,0:T(8,128)(2,1)}, u32[]{:S(2)}) copy-start(bf16[64,128,128]{2,1,0:T(8,128)(2,1)} %rows_table.1) | copy-start | bytes 6291460
  71.4 2.2 %copy-start.5 = (bf16[64,128,128]{2,1,0:T(8,128)(2,1)S(1)}, bf16[64,128,128]{2,1,0:T(8,128)(2,1)}, u32[]{:S(2)}) copy-start(bf16[64,128,128]{2,1,0:T(8,128)(2,1)} %cols_table.1) | copy-start | bytes 6291460
  71.4 18.4 %slice-start = ((s8[6291456]{0:T(1024)(128)(4,1)}), s8[4194304]{0:T(1024)(128)(4,1)S(1)}, s32[]{:S(2)}) async-start(s8[6291456]{0:T(1024)(128)(4,1)} %bitcast.3), calls=%async_computation.2 | async-start | bytes 8388608
  71.9 17.9 %slice-start.1 = ((s8[6291456]{0:T(1024)(128)(4,1)}), s8[2097152]{0:T(1024)(128)(4,1)S(1)}, s32[]{:S(2)}) async-start(s8[6291456]{0:T(1024)(128)(4,1)} %bitcast.3), calls=%async_computation.3 | async-start | bytes 4194304
  71.9 17.9 %collective-permute-start.6 = (s16[102,16,128]{2,1,0:T(8,128)(2,1)S(1)}, s16[102,16,128]{2,1,0:T(8,128)(2,1)S(1)}, u32[]{:S(2)}, u32[]{:S(2)}) collective-permute-start(s16[102,16,128]{2,1,0:T(8,128)(2,1)S(1)} %shard_map.108), channel_id=1, source_target_pairs={{0,64},{16,80},{32,96},{48,112},{64,0},{80,16},{96,32},{112,48},{1... | collective-permute-start | bytes 1253384 | tf_op jit(solution)/shard_map/ppermute | solution.py:231
  91.1 15.6 %collective-permute-start.13 = (bf16[48,16,128]{2,1,0:T(8,128)(2,1)S(1)}, bf16[48,16,128]{2,1,0:T(8,128)(2,1)S(1)}, u32[]{:S(2)}, u32[]{:S(2)}) collective-permute-start(bf16[48,16,128]{2,1,0:T(8,128)(2,1)S(1)} %get-tuple-element.52.rest_0_), channel_id=1, source_target_pairs={{0,16},{16,0},{32,48},{48,32},{64,80},{80,64},{96,112},{112,96},{1... | collective-permute-start | bytes 589832 | tf_op jit(solution)/shard_map/ppermute | solution.py:228
  92.3 7.7 %collective-permute-start.12 = (bf16[48,16,128]{2,1,0:T(8,128)(2,1)S(1)}, bf16[48,16,128]{2,1,0:T(8,128)(2,1)S(1)}, u32[]{:S(2)}, u32[]{:S(2)}) collective-permute-start(bf16[48,16,128]{2,1,0:T(8,128)(2,1)S(1)} %get-tuple-element.52.rest_0_), channel_id=1, source_target_pairs={{0,32},{16,48},{32,64},{48,80},{64,96},{80,112},{96,0},{112,16},{1... | collective-permute-start | bytes 589832 | tf_op jit(solution)/shard_map/ppermute | solution.py:231
  93.7 6.4 %collective-permute-start.11 = (bf16[48,16,128]{2,1,0:T(8,128)(2,1)S(1)}, bf16[48,16,128]{2,1,0:T(8,128)(2,1)S(1)}, u32[]{:S(2)}, u32[]{:S(2)}) collective-permute-start(bf16[48,16,128]{2,1,0:T(8,128)(2,1)S(1)} %get-tuple-element.52.rest_0_), channel_id=1, source_target_pairs={{0,96},{16,112},{32,0},{48,16},{64,32},{80,48},{96,64},{112,80},{1... | collective-permute-start | bytes 589832 | tf_op jit(solution)/shard_map/ppermute | solution.py:231
  95.0 10.4 %collective-permute-start.10 = (bf16[48,16,128]{2,1,0:T(8,128)(2,1)S(1)}, bf16[48,16,128]{2,1,0:T(8,128)(2,1)S(1)}, u32[]{:S(2)}, u32[]{:S(2)}) collective-permute-start(bf16[48,16,128]{2,1,0:T(8,128)(2,1)S(1)} %get-tuple-element.52.rest_0_), channel_id=1, source_target_pairs={{0,64},{16,80},{32,96},{48,112},{64,0},{80,16},{96,32},{112,48},{1... | collective-permute-start | bytes 589832 | tf_op jit(solution)/shard_map/ppermute | solution.py:231
  105.4 2.2 %collective-permute-start.14 = (bf16[48,16,128]{2,1,0:T(8,128)(2,1)S(1)}, bf16[48,16,128]{2,1,0:T(8,128)(2,1)S(1)}, u32[]{:S(2)}, u32[]{:S(2)}) collective-permute-start(bf16[48,16,128]{2,1,0:T(8,128)(2,1)S(1)} %collective-permute-done.11.rest_1_), channel_id=1, source_target_pairs={{0,16},{16,0},{32,48},{48,32},{64,80},{80,64},{96,112},{112,96},{1... | collective-permute-start | bytes 589832 | tf_op jit(solution)/shard_map/ppermute | solution.py:228
  106.2 3.2 %collective-permute-start.15 = (bf16[48,16,128]{2,1,0:T(8,128)(2,1)S(1)}, bf16[48,16,128]{2,1,0:T(8,128)(2,1)S(1)}, u32[]{:S(2)}, u32[]{:S(2)}) collective-permute-start(bf16[48,16,128]{2,1,0:T(8,128)(2,1)S(1)} %collective-permute-done.10.rest_2_), channel_id=1, source_target_pairs={{0,16},{16,0},{32,48},{48,32},{64,80},{80,64},{96,112},{112,96},{1... | collective-permute-start | bytes 589832 | tf_op jit(solution)/shard_map/ppermute | solution.py:228
  106.2 3.7 %collective-permute-start.16 = (bf16[48,16,128]{2,1,0:T(8,128)(2,1)S(1)}, bf16[48,16,128]{2,1,0:T(8,128)(2,1)S(1)}, u32[]{:S(2)}, u32[]{:S(2)}) collective-permute-start(bf16[48,16,128]{2,1,0:T(8,128)(2,1)S(1)} %collective-permute-done.12.rest_3_), channel_id=1, source_target_pairs={{0,16},{16,0},{32,48},{48,32},{64,80},{80,64},{96,112},{112,96},{1... | collective-permute-start | bytes 589832 | tf_op jit(solution)/shard_map/ppermute | solution.py:228
  106.7 14.8 %collective-permute-start.17 = (bf16[48,16,128]{2,1,0:T(8,128)(2,1)S(1)}, bf16[48,16,128]{2,1,0:T(8,128)(2,1)S(1)}, u32[]{:S(2)}, u32[]{:S(2)}) collective-permute-start(bf16[48,16,128]{2,1,0:T(8,128)(2,1)S(1)} %get-tuple-element.57.rest_8_.rest_0_), channel_id=1, source_target_pairs={{0,16},{16,0},{32,48},{48,32},{64,80},{80,64},{96,112},{112,96},{1... | collective-permute-start | bytes 589832 | tf_op jit(solution)/shard_map/ppermute | solution.py:228
  106.7 12.5 %collective-permute-start.9 = (bf16[48,16,128]{2,1,0:T(8,128)(2,1)S(1)}, bf16[48,16,128]{2,1,0:T(8,128)(2,1)S(1)}, u32[]{:S(2)}, u32[]{:S(2)}) collective-permute-start(bf16[48,16,128]{2,1,0:T(8,128)(2,1)S(1)} %get-tuple-element.57.rest_8_.rest_0_), channel_id=1, source_target_pairs={{0,32},{16,48},{32,64},{48,80},{64,96},{80,112},{96,0},{112,16},{1... | collective-permute-start | bytes 589832 | tf_op jit(solution)/shard_map/ppermute | solution.py:231
  107.6 11.7 %collective-permute-start.8 = (bf16[48,16,128]{2,1,0:T(8,128)(2,1)S(1)}, bf16[48,16,128]{2,1,0:T(8,128)(2,1)S(1)}, u32[]{:S(2)}, u32[]{:S(2)}) collective-permute-start(bf16[48,16,128]{2,1,0:T(8,128)(2,1)S(1)} %get-tuple-element.57.rest_8_.rest_0_), channel_id=1, source_target_pairs={{0,96},{16,112},{32,0},{48,16},{64,32},{80,48},{96,64},{112,80},{1... | collective-permute-start | bytes 589832 | tf_op jit(solution)/shard_map/ppermute | solution.py:231
  109.4 9.9 %collective-permute-start.7 = (bf16[48,16,128]{2,1,0:T(8,128)(2,1)S(1)}, bf16[48,16,128]{2,1,0:T(8,128)(2,1)S(1)}, u32[]{:S(2)}, u32[]{:S(2)}) collective-permute-start(bf16[48,16,128]{2,1,0:T(8,128)(2,1)S(1)} %get-tuple-element.57.rest_8_.rest_0_), channel_id=1, source_target_pairs={{0,64},{16,80},{32,96},{48,112},{64,0},{80,16},{96,32},{112,48},{1... | collective-permute-start | bytes 589832 | tf_op jit(solution)/shard_map/ppermute | solution.py:231
  119.3 2.8 %collective-permute-start.18 = (bf16[48,16,128]{2,1,0:T(8,128)(2,1)S(1)}, bf16[48,16,128]{2,1,0:T(8,128)(2,1)S(1)}, u32[]{:S(2)}, u32[]{:S(2)}) collective-permute-start(bf16[48,16,128]{2,1,0:T(8,128)(2,1)S(1)} %collective-permute-done.8.rest_1_), channel_id=1, source_target_pairs={{0,16},{16,0},{32,48},{48,32},{64,80},{80,64},{96,112},{112,96},{1... | collective-permute-start | bytes 589832 | tf_op jit(solution)/shard_map/ppermute | solution.py:228
  121.0 1.4 collective-permute-start.19
  121.3 1.4 collective-permute-start.20
  133.9 32.1 %copy-start.1 = (s32[1,16,4]{2,1,0:T(8,128)S(1)}, s32[1,16,4]{2,1,0:T(8,128)}, u32[]{:S(2)}) copy-start(s32[1,16,4]{2,1,0:T(8,128)} %copy-done) | copy-start | bytes 772
